TPU v7x, 32 devices: a whole 2x2x4 slice. The times are simulated.
32 devices in a mesh: ctx: 4 (over y, x), chan: 8 (over z, core).
Axes of the slice: x: 2, y: 2, z: 4, core: 2. Of those that a mesh axis runs over, the one named last changes fastest.
Arguments:
- tokens: bfloat16 [2048, 4096], P('ctx', 'chan'), may hold values from -7 to 7
- in_proj: bfloat16 [3, 4096, 4096], P(None, 'chan'), may hold values from -0.125 to 0.125
- short_taps: float32 [3, 4096, 3], P(None, 'chan'), may hold values from -3.5 to 3.5
- long_filter: bfloat16 [4096, 2048], P('chan', 'ctx'), may hold values from -1.3 to 1.3
- skip_gain: float32 [4096], P('chan'), may hold values from -4 to 4
Outputs:
- gated: bfloat16 [4096, 2048], P('chan', 'ctx')
All inputs are finite; a program needn't handle non-finite values.
Results may differ from a plain program's by a relative error of at most 0.0075.
Values may be sent and summed in bfloat16 or wider, within the bound.
No kernel may reach another device: no remote copies, remote signals or barrier semaphores. Data moves between devices by JAX's collectives and lax.ppermute only.
A program may use at most 192 MiB of HBM per device.

v0:
```python
import math

import jax
import jax.numpy as jnp
from jax import lax
from jax.sharding import PartitionSpec as P


def from_behind(x, axis, by):
    size = lax.axis_size(axis)
    pairs = [(i, i + by) for i in range(size) if 0 <= i + by < size]
    return lax.ppermute(x, axis, pairs)


def wave_tables(length):
    size = 2 * length
    index = jnp.arange(size, dtype=jnp.int32)
    phase = index[:, None] * index[None, :] % size
    angle = phase.astype(jnp.float32) * (2.0 * math.pi / size)
    return (jnp.cos(angle), jnp.sin(angle))


def forward(values, cosine, sine):
    count = values.shape[-1]
    real_part = jnp.dot(
        values, cosine[:count], precision=lax.Precision.HIGHEST, preferred_element_type=jnp.float32
    )
    imag_part = -jnp.dot(
        values, sine[:count], precision=lax.Precision.HIGHEST, preferred_element_type=jnp.float32
    )
    return (real_part, imag_part)


def inverse(spectra, cosine, sine, length):
    upper = cosine[:, length:]
    upper_sine = sine[:, length:]
    values = jnp.dot(
        spectra[0], upper, precision=lax.Precision.HIGHEST, preferred_element_type=jnp.float32
    )
    values = values - jnp.dot(
        spectra[1], upper_sine, precision=lax.Precision.HIGHEST, preferred_element_type=jnp.float32
    )
    return values * (1.0 / (2 * length))


def body(tokens, in_proj, short_taps, long_filter, skip_gain):
    length = tokens.shape[0]
    summed = lax.psum_scatter(
        jnp.einsum("td,kdc->ckt", tokens, in_proj, preferred_element_type=jnp.float32),
        "chan",
        scatter_dimension=0,
        tiled=True,
    )
    mixed = summed.astype(jnp.bfloat16)
    earlier = from_behind(mixed[:, :, length - 2 :], "ctx", 1)
    extended = jnp.concatenate([earlier, mixed], axis=2).astype(jnp.float32)
    weights = jnp.transpose(short_taps, (1, 0, 2))
    featured = (
        weights[:, :, 0:1] * extended[:, :, 2:]
        + weights[:, :, 1:2] * extended[:, :, 1 : length + 1]
        + weights[:, :, 2:3] * extended[:, :, 0:length]
    )
    product = (featured[:, 1] * featured[:, 2]).astype(jnp.bfloat16)
    cycle_size = lax.axis_size("ctx")
    cosine, sine = wave_tables(length)
    moved_product, moved_filter = (
        lax.all_to_all(product, "ctx", split_axis=0, concat_axis=1, tiled=True),
        lax.all_to_all(long_filter, "ctx", split_axis=0, concat_axis=1, tiled=True),
    )
    few_rows = moved_product.shape[0]
    input_blocks = moved_product.reshape(few_rows * cycle_size, length).astype(jnp.float32)
    input_re, input_im = forward(input_blocks, cosine, sine)
    input_re = input_re.reshape(few_rows, cycle_size, 2 * length)
    input_im = input_im.reshape(few_rows, cycle_size, 2 * length)
    filter_blocks = moved_filter.reshape(few_rows, cycle_size, length)
    previous = jnp.concatenate(
        [jnp.zeros_like(filter_blocks[:, :1]), filter_blocks[:, :-1]], axis=1
    )
    windows = (
        jnp.concatenate([previous, filter_blocks], axis=2)
        .reshape(few_rows * cycle_size, 2 * length)
        .astype(jnp.float32)
    )
    taps_re, taps_im = forward(windows, cosine, sine)
    taps_re = taps_re.reshape(few_rows, cycle_size, 2 * length)
    taps_im = taps_im.reshape(few_rows, cycle_size, 2 * length)
    sum_re = jnp.zeros_like(input_re)
    sum_im = jnp.zeros_like(input_im)
    for offset in range(cycle_size):
        later_re = (
            input_re[:, : cycle_size - offset] * taps_re[:, offset : offset + 1]
            - input_im[:, : cycle_size - offset] * taps_im[:, offset : offset + 1]
        )
        later_im = (
            input_re[:, : cycle_size - offset] * taps_im[:, offset : offset + 1]
            + input_im[:, : cycle_size - offset] * taps_re[:, offset : offset + 1]
        )
        sum_re = sum_re.at[:, offset:].add(later_re)
        sum_im = sum_im.at[:, offset:].add(later_im)
    spectra = jnp.stack(
        [
            sum_re.reshape(few_rows * cycle_size, 2 * length),
            sum_im.reshape(few_rows * cycle_size, 2 * length),
        ]
    )
    full_rows = inverse(spectra, cosine, sine, length).reshape(few_rows, cycle_size * length)
    total = lax.all_to_all(full_rows, "ctx", split_axis=1, concat_axis=0, tiled=True)
    answer = total + skip_gain[:, None] * product.astype(jnp.float32)
    return (featured[:, 0] * answer).astype(jnp.bfloat16)


def solution(mesh):
    in_specs = (
        P("ctx", "chan"),
        P(None, "chan", None),
        P(None, "chan", None),
        P("chan", "ctx"),
        P("chan"),
    )
    out_specs = P("chan", "ctx")
    return jax.shard_map(body, mesh=mesh, in_specs=in_specs, out_specs=out_specs, check_vma=False)
```

profile of v0, /device:TPU:8, one launch (start us, length us, event | category | flops | bytes accessed | tf_op | source)
XLA Modules:
  0.0 370.5 jit_solution(17269976370804359584)
XLA Ops:
  7.6 16.5 %convolution_bitcast_fusion = f32[4096,3,512]{2,0,1:T(8,128)} fusion(bf16[3,512,4096]{2,1,0:T(8,128)(2,1)} %param.26, bf16[512,512]{1,0:T(8,128)(2,1)S(1)} %copy-done), kind=kOutput, calls=%fused_computation | convolution fusion | flops 6442450944 | bytes 38273024 | tf_op jit(solution)/shard_map/td,kdc->ckt/dot_general | solution.py:49
  24.1 3.7 %all-to-all-start.1 = ((bf16[4,128,512]{2,1,0:T(8,128)(2,1)}), bf16[4,128,512]{2,1,0:T(8,128)(2,1)S(1)}, u32[]{:S(2)}, u32[]{:S(2)}) async-start(bf16[4,128,512]{2,1,0:T(8,128)(2,1)} %bitcast.7), calls=%async_computation.2 | async-start | bytes 1048576 | tf_op jit(solution)/shard_map/all_to_all | solution.py:68
  27.9 16.2 %fusion.18 = f32[1024,1024]{1,0:T(8,128)} fusion(), kind=kLoop, calls=%fused_computation.28 | loop fusion | flops 14680064 | bytes 4194304 | tf_op jit(solution)/shard_map/cos | solution.py:20
  44.1 16.5 %fusion.17 = f32[1024,1024]{1,0:T(8,128)} fusion(), kind=kLoop, calls=%fused_computation.27 | loop fusion | flops 14680064 | bytes 4194304 | tf_op jit(solution)/shard_map/sin | solution.py:20
  61.7 20.4 %fusion.25 = f32[512,1024]{1,0:T(8,128)} fusion(bf16[512,512]{1,0:T(8,128)(2,1)S(1)} %concatenate.37, bf16[512,512]{1,0:T(8,128)(2,1)S(1)} %concatenate.36), kind=kOutput, calls=%fused_computation.34 | convolution fusion | flops 6459752448 | bytes 3145728 | tf_op jit(solution)/shard_map/dot_general | solution.py:28
  82.1 2.3 reshape.281
  84.4 20.2 %fusion.3 = f32[128,4,1024]{2,0,1:T(8,128)} fusion(bf16[128,4,512]{2,0,1:T(8,128)(2,1)S(1)} %bitcast.57, bf16[128,4,512]{2,0,1:T(8,128)(2,1)S(1)} %concatenate.34), kind=kOutput, calls=%fused_computation.7 | convolution fusion | flops 6459228160 | bytes 3145728 | tf_op jit(solution)/shard_map/dot_general | solution.py:25
  104.6 165.1 %reduce-scatter.2.cloned.1.call-done = f32[512,3,512]{2,0,1:T(8,128)} async-done(((f32[4096,3,512]{2,0,1:T(8,128)}), f32[512,3,512]{2,0,1:T(8,128)}) %reduce-scatter.2.cloned.1.call-update) | async-done | bytes 3145744 | tf_op jit(solution)/shard_map/reduce_scatter | solution.py:48
  272.0 3.5 collective-permute-start
  275.5 2.6 fusion.58
  278.1 6.7 %collective-permute-done = bf16[512,3,2]{2,0,1:T(8,128)(2,1)S(1)} collective-permute-done((bf16[512,3,2]{2,0,1:T(8,128)(2,1)S(1)}, bf16[512,3,2]{2,0,1:T(8,128)(2,1)S(1)}, u32[]{:S(2)}, u32[]{:S(2)}) %collective-permute-start) | collective-permute-done | bytes 6176 | tf_op jit(solution)/shard_map/ppermute | solution.py:12
  285.6 2.8 fusion.8
  291.0 4.7 %all-to-all-start = ((bf16[4,128,512]{2,1,0:T(8,128)(2,1)}), bf16[4,128,512]{2,1,0:T(8,128)(2,1)S(1)}, u32[]{:S(2)}, u32[]{:S(2)}) async-start(bf16[4,128,512]{2,1,0:T(8,128)(2,1)} %bitcast.4), calls=%async_computation.1 | async-start | bytes 1048576 | tf_op jit(solution)/shard_map/all_to_all | solution.py:67
  295.7 2.2 copy_bitcast_fusion
  297.9 2.4 slice_bitcast_fusion.3
  300.4 4.5 %all-to-all-done = bf16[4,128,512]{2,1,0:T(8,128)(2,1)S(1)} async-done(((bf16[4,128,512]{2,1,0:T(8,128)(2,1)}), bf16[4,128,512]{2,1,0:T(8,128)(2,1)S(1)}, u32[]{:S(2)}, u32[]{:S(2)}) %all-to-all-start) | async-done | bytes 524320 | tf_op jit(solution)/shard_map/all_to_all | solution.py:67
  305.4 3.5 fusion.22
  310.5 3.6 fusion.16
  319.5 2.7 copy.19
  322.2 3.2 squeeze_stack_reshape.7
  325.4 6.7 %fusion.10 = f32[512,512]{1,0:T(8,128)} fusion(f32[512,1024]{1,0:T(8,128)} %squeeze_stack_reshape.7, f32[1024,1024]{1,0:T(8,128)} %fusion.17), kind=kOutput, calls=%fused_computation.17 | convolution fusion | flops 3221225472 | bytes 5242880 | tf_op jit(solution)/shard_map/dot_general | solution.py:40
  332.1 2.7 copy.17
  336.8 6.3 %fusion.31 = f32[512,512]{1,0:T(8,128)} fusion(f32[512,512]{1,0:T(8,128)} %fusion.10, f32[512,1024]{1,0:T(8,128)S(1)} %squeeze_stack_reshape.6, f32[1024,1024]{1,0:T(8,128)} %fusion.18), kind=kOutput, calls=%fused_computation.36 | convolution fusion | flops 3221749760 | bytes 6291456 | tf_op jit(solution)/shard_map/dot_general | solution.py:37
  345.1 17.1 %all_to_all.48 = f32[128,4,512]{2,0,1:T(8,128)S(1)} all-to-all(f32[128,4,512]{2,0,1:T(8,128)S(1)} %copy.20), channel_id=1, replica_groups=mesh['ctx'=4,'chan'=8] {'ctx'}, dimensions={1} | all-to-all | bytes 2097152 | tf_op jit(solution)/shard_map/all_to_all | solution.py:107
  (57 shorter events, 20.2 us)
Async XLA Ops:
  6.5 1.0 copy-start
  6.5 263.2 %reduce-scatter.2.cloned.1.call-start = ((), (), s32[]{:S(2)}) async-start(), calls=%async_computation.4 | async-start | bytes 28311552 | tf_op jit(solution)/shard_map/reduce_scatter | solution.py:48
  24.1 3.8 %copy-start.13 = (f32[3,512,3]{1,2,0:T(4,128)S(1)}, f32[3,512,3]{1,2,0:T(4,128)}, u32[]{:S(2)}) copy-start(f32[3,512,3]{1,2,0:T(4,128)} %param.27) | copy-start | bytes 55300
  24.1 36.5 %all-to-all-start.1 = ((bf16[4,128,512]{2,1,0:T(8,128)(2,1)}), bf16[4,128,512]{2,1,0:T(8,128)(2,1)S(1)}, u32[]{:S(2)}, u32[]{:S(2)}) async-start(bf16[4,128,512]{2,1,0:T(8,128)(2,1)} %bitcast.7), calls=%async_computation.2 | async-start | bytes 1048576 | tf_op jit(solution)/shard_map/all_to_all | solution.py:68
  272.0 12.8 %collective-permute-start = (bf16[512,3,2]{2,0,1:T(8,128)(2,1)S(1)}, bf16[512,3,2]{2,0,1:T(8,128)(2,1)S(1)}, u32[]{:S(2)}, u32[]{:S(2)}) collective-permute-start(bf16[512,3,2]{2,0,1:T(8,128)(2,1)S(1)} %slice.323), channel_id=1, source_target_pairs={{0,8},{8,16},{16,24},{1,9},{9,17},{17,25},{2,10},{10,18},{18,26},{... | collective-permute-start | bytes 18440 | tf_op jit(solution)/shard_map/ppermute | solution.py:12
  288.4 1.6 copy-start.2
  290.0 7.9 %copy-start.6 = (f32[128,4,1024]{2,0,1:T(8,128)S(1)}, f32[128,4,1024]{2,0,1:T(8,128)}, u32[]{:S(2)}) copy-start(f32[128,4,1024]{2,0,1:T(8,128)} %fusion.3) | copy-start | bytes 6291460
  291.0 13.8 %all-to-all-start = ((bf16[4,128,512]{2,1,0:T(8,128)(2,1)}), bf16[4,128,512]{2,1,0:T(8,128)(2,1)S(1)}, u32[]{:S(2)}, u32[]{:S(2)}) async-start(bf16[4,128,512]{2,1,0:T(8,128)(2,1)} %bitcast.4), calls=%async_computation.1 | async-start | bytes 1048576 | tf_op jit(solution)/shard_map/all_to_all | solution.py:67
  310.5 3.7 copy-start.4
  310.5 3.7 copy-start.8
  310.5 3.7 copy-start.9
  314.2 1.5 copy-start.11
  314.2 1.5 copy-start.12
  315.7 1.3 copy-start.5
  315.7 1.3 copy-start.7
  317.0 1.0 copy-start.10
  343.1 19.0 %copy-start.14 = (f32[512]{0:T(512)S(1)}, f32[512]{0:T(512)}, u32[]{:S(2)}) copy-start(f32[512]{0:T(512)} %param.29) | copy-start | bytes 6148
  344.7 17.5 %copy-start.3 = (f32[512,3,512]{2,0,1:T(8,128)S(1)}, f32[512,3,512]{2,0,1:T(8,128)}, u32[]{:S(2)}) copy-start(f32[512,3,512]{2,0,1:T(8,128)} %copy-done.2) | copy-start | bytes 9437188
  344.7 18.5 %copy-start.1 = (bf16[512,512]{1,0:T(8,128)(2,1)S(1)}, bf16[512,512]{1,0:T(8,128)(2,1)}, u32[]{:S(2)}) copy-start(bf16[512,512]{1,0:T(8,128)(2,1)} %param.25) | copy-start | bytes 1572868
Sparse Core Ops, SparseCore 0:
  24.2 245.4 reduce-scatter.1
where the time goes:
time: 376 us; the launch traced here: 370 us
  waiting for transfers between devices  176 us (47%)
  matrix products  77.3 us (21%)
  other arithmetic  45.2 us (12%)
  local copies, waits for them, and re-layouts  28.6 us (8%)
  blocking collectives  17.1 us (5%)
  between operations  14.1 us (4%)
  starting transfers between devices  11.9 us (3%)
    reduce_scatter x1, waiting for transfers between devices, body(): lax.psum_scatter(jnp.einsum('td,kdc->ckt', tokens, in_proj, preferred_ele...  165 us
    dot_general x2, matrix products, forward(): jnp.dot(values, sine[:count], precision=lax.Precision.HIGHEST, preferred_...  23.9 us
    dot_general x2, matrix products, forward(): jnp.dot(values, cosine[:count], precision=lax.Precision.HIGHEST, preferre...  23.8 us
    all_to_all x1, blocking collectives, body(): lax.all_to_all(full_rows, 'ctx', split_axis=1, concat_axis=0, tiled=True)  17.1 us
    dot_general x1, matrix products, body(): jnp.einsum('td,kdc->ckt', tokens, in_proj, preferred_element_type=jnp.flo...  16.5 us
    sin x1, other arithmetic, wave_tables(): return (jnp.cos(angle), jnp.sin(angle))  16.5 us
    cos x1, other arithmetic, wave_tables(): return (jnp.cos(angle), jnp.sin(angle))  16.2 us
  transfers between devices with their start and end apart: 4, of which 3 were waited for; matrix products, arithmetic and copies ran while one was open for 23% of the time, Pallas kernels for 0%

commit v1 on v0

v1 whole, which is shorter than its diff:
```python
import functools

import jax
import jax.numpy as jnp
import ml_dtypes
import numpy as np
from jax import lax
from jax.experimental import pallas as pl
from jax.experimental.pallas import tpu as pltpu
from jax.sharding import PartitionSpec as P

VMEM_LIMIT = 48 * 1024 * 1024
F32 = jnp.float32
BF16 = jnp.bfloat16


def wave_tables(length):
    position = np.arange(length, dtype=np.int64)
    phase = (position[:, None] * (2 * position[None, :] + 1)) % (4 * length)
    angle = phase.astype(np.float64) * (2.0 * np.pi / (4 * length))
    table = np.concatenate([np.cos(angle), -np.sin(angle)], axis=1)
    high = table.astype(ml_dtypes.bfloat16)
    low = (table - high.astype(np.float64)).astype(ml_dtypes.bfloat16)
    return high, low


def spectrum(values, high, low):
    return jnp.dot(values, high, preferred_element_type=F32) + jnp.dot(
        values, low, preferred_element_type=F32
    )


def filter_kernel(taps_ref, high_ref, low_ref, out_ref):
    blocks, rows, length = taps_ref.shape
    values = taps_ref[...].reshape(blocks * rows, length)
    waves = spectrum(values, high_ref[...], low_ref[...]) * (1.0 / length)
    lane = lax.broadcasted_iota(jnp.int32, (rows, length), 1)
    sign = jnp.where(lane % 2 == 0, 1.0, -1.0)
    for m in range(blocks):
        real = waves[m * rows : (m + 1) * rows, :length]
        imag = waves[m * rows : (m + 1) * rows, length:]
        if m:
            real = real - sign * waves[(m - 1) * rows : m * rows, length:]
            imag = imag + sign * waves[(m - 1) * rows : m * rows, :length]
        out_ref[m, :, :length] = real
        out_ref[m, :, length:] = imag


def filter_waves(moved_filter, high, low):
    blocks, rows, length = moved_filter.shape
    step = min(rows, 64)
    return pl.pallas_call(
        filter_kernel,
        grid=(rows // step,),
        in_specs=[
            pl.BlockSpec((blocks, step, length), lambda g: (0, g, 0)),
            pl.BlockSpec((length, 2 * length), lambda g: (0, 0)),
            pl.BlockSpec((length, 2 * length), lambda g: (0, 0)),
        ],
        out_specs=pl.BlockSpec((blocks, step, 2 * length), lambda g: (0, g, 0)),
        out_shape=jax.ShapeDtypeStruct((blocks, rows, 2 * length), F32),
        compiler_params=pltpu.CompilerParams(vmem_limit_bytes=VMEM_LIMIT),
        name="filter_waves",
    )(moved_filter, high, low)


def feature(own, other, taps):
    mixed = (own + other).astype(BF16).astype(F32)
    lane = lax.broadcasted_iota(jnp.int32, mixed.shape, 1)
    one = jnp.where(lane >= 1, pltpu.roll(mixed, 1, 1), 0.0)
    two = jnp.where(lane >= 2, pltpu.roll(mixed, 2, 1), 0.0)
    return taps[:, 0:1] * mixed + taps[:, 1:2] * one + taps[:, 2:3] * two


def conv_kernel(own_ref, other_ref, taps_ref, skip_ref, waves_ref, high_ref, low_ref, out_ref):
    blocks, rows, double = waves_ref.shape
    length = double // 2
    product = (
        feature(own_ref[0], other_ref[0], taps_ref[1]) * feature(own_ref[1], other_ref[1], taps_ref[2])
    ).astype(BF16)
    values = jnp.concatenate(
        [product[:, p * length : (p + 1) * length] for p in range(blocks)], axis=0
    )
    high = high_ref[...]
    low = low_ref[...]
    waves = spectrum(values, high, low)
    pieces = []
    for p in range(blocks):
        real = jnp.zeros((rows, length), F32)
        imag = jnp.zeros((rows, length), F32)
        for q in range(p + 1):
            in_real = waves[q * rows : (q + 1) * rows, :length]
            in_imag = waves[q * rows : (q + 1) * rows, length:]
            tap_real = waves_ref[p - q, :, :length]
            tap_imag = waves_ref[p - q, :, length:]
            real = real + (in_real * tap_real - in_imag * tap_imag)
            imag = imag + (in_real * tap_imag + in_imag * tap_real)
        pieces.append(jnp.concatenate([real, imag], axis=1))
    total = jnp.concatenate(pieces, axis=0)
    total_high = total.astype(BF16)
    total_low = (total - total_high.astype(F32)).astype(BF16)
    dims = (((1,), (1,)), ((), ()))
    back = (
        lax.dot_general(total_high, high, dims, preferred_element_type=F32)
        + lax.dot_general(total_low, high, dims, preferred_element_type=F32)
        + lax.dot_general(total_high, low, dims, preferred_element_type=F32)
    )
    skip = skip_ref[...]
    for p in range(blocks):
        span = slice(p * length, (p + 1) * length)
        out_ref[:, span] = back[p * rows : (p + 1) * rows] + skip * product[:, span].astype(F32)


def convolve(own, other, taps, skip, waves, high, low):
    streams, rows, span = own.shape
    blocks, _, double = waves.shape
    step = min(rows, 64)
    return pl.pallas_call(
        conv_kernel,
        grid=(rows // step,),
        in_specs=[
            pl.BlockSpec((streams, step, span), lambda g: (0, g, 0)),
            pl.BlockSpec((streams, step, span), lambda g: (0, g, 0)),
            pl.BlockSpec((3, step, 3), lambda g: (0, g, 0)),
            pl.BlockSpec((step, 1), lambda g: (g, 0)),
            pl.BlockSpec((blocks, step, double), lambda g: (0, g, 0)),
            pl.BlockSpec((double // 2, double), lambda g: (0, 0)),
            pl.BlockSpec((double // 2, double), lambda g: (0, 0)),
        ],
        out_specs=pl.BlockSpec((step, span), lambda g: (g, 0)),
        out_shape=jax.ShapeDtypeStruct((rows, span), F32),
        compiler_params=pltpu.CompilerParams(vmem_limit_bytes=VMEM_LIMIT),
        name="convolve",
    )(own, other, taps, skip, waves, high, low)


def gate_kernel(own_ref, other_ref, taps_ref, answer_ref, out_ref):
    blocks, _, length = out_ref.shape
    gated = (feature(own_ref[...], other_ref[...], taps_ref[0]) * answer_ref[...]).astype(BF16)
    for p in range(blocks):
        out_ref[p] = gated[:, p * length : (p + 1) * length]


def gate(own, other, taps, answer, blocks):
    rows, span = own.shape
    step = min(rows, 64)
    return pl.pallas_call(
        gate_kernel,
        grid=(rows // step,),
        in_specs=[
            pl.BlockSpec((step, span), lambda g: (g, 0)),
            pl.BlockSpec((step, span), lambda g: (g, 0)),
            pl.BlockSpec((3, step, 3), lambda g: (0, g, 0)),
            pl.BlockSpec((step, span), lambda g: (g, 0)),
        ],
        out_specs=pl.BlockSpec((blocks, step, span // blocks), lambda g: (0, g, 0)),
        out_shape=jax.ShapeDtypeStruct((blocks, rows, span // blocks), BF16),
        compiler_params=pltpu.CompilerParams(vmem_limit_bytes=VMEM_LIMIT),
        name="gate",
    )(own, other, taps, answer)


def swap(x, axis, bit):
    return lax.ppermute(x, axis, [(i, i ^ bit) for i in range(lax.axis_size(axis))])


def gather_context(block):
    size = lax.axis_size("ctx")
    if size != 4:
        return lax.all_gather(block, "ctx", axis=1, tiled=True)
    me = lax.axis_index("ctx")
    groups, length, depth = block.shape
    half = length // 2
    near = swap(block, "ctx", 1)
    far = swap(block, "ctx", 2)
    first = swap(far[:, :half], "ctx", 1)
    second = swap(near[:, half:], "ctx", 2)
    whole = jnp.zeros((groups, size * length, depth), block.dtype)
    for piece, row in (
        (block, me * length),
        (near, (me ^ 1) * length),
        (far, (me ^ 2) * length),
        (first, (me ^ 3) * length),
        (second, (me ^ 3) * length + half),
    ):
        whole = lax.dynamic_update_slice(whole, piece, (0, row, 0))
    return whole


def gather_features(block):
    size = lax.axis_size("chan")
    chips = size // 2
    place = lax.axis_index("chan") // 2
    left, right = [], []
    up, down = block, block
    for _ in range(1, chips):
        up = lax.ppermute(up, "chan", [(i, i + 2) for i in range(size - 2)])
        down = lax.ppermute(down, "chan", [(i + 2, i) for i in range(size - 2)])
        left.append(up)
        right.append(down)
    return jnp.stack(
        [jnp.where(place >= s, left[s - 1], right[chips - s - 1]) for s in range(1, chips)]
    )


def body(tokens, in_proj, short_taps, long_filter, skip_gain):
    length, _ = tokens.shape
    cycle = lax.axis_size("ctx")
    size = lax.axis_size("chan")
    chips = size // 2
    me = lax.axis_index("ctx")
    place = lax.axis_index("chan") // 2
    core = lax.axis_index("chan") % 2
    few = in_proj.shape[2] // (size * cycle)
    high, low = (jnp.asarray(t) for t in wave_tables(length))

    def columns(s, streams):
        owner = (place + s) % chips
        parts = []
        for side in range(2):
            start = ((2 * owner + (core ^ side)) * cycle + me) * few
            for k in streams:
                parts.append(lax.dynamic_slice_in_dim(in_proj[k], start, few, axis=1))
        return jnp.concatenate(parts, axis=1)

    def travel(piece, s):
        pairs = [(i, (i + 2 * s) % size) for i in range(size)]
        return lax.ppermute(piece, "chan", pairs)

    moved_filter = lax.all_to_all(
        long_filter.reshape(cycle, few, length), "ctx", split_axis=0, concat_axis=0, tiled=True
    )
    waves = filter_waves(moved_filter, high, low)

    others = gather_features(tokens)
    own_tokens = gather_context(tokens[None])[0]
    other_tokens = gather_context(others)

    def project(streams):
        total = None
        for s in range(chips):
            piece = columns(s, streams)
            if s:
                piece = travel(piece, s)
            these = own_tokens if s == 0 else other_tokens[s - 1]
            part = jnp.einsum("td,dc->ct", these, piece, preferred_element_type=F32)
            total = part if total is None else total + part
        rows = len(streams) * few
        return total[:rows], swap(total[rows:], "chan", 1)

    own_taps = lax.dynamic_slice_in_dim(short_taps, me * few, few, axis=1)
    own_skip = lax.dynamic_slice_in_dim(skip_gain, me * few, few)[:, None]
    span = own_tokens.shape[0]
    mine, theirs = project((1, 2))
    answer = convolve(
        mine.reshape(2, few, span), theirs.reshape(2, few, span), own_taps, own_skip, waves, high, low
    )
    mine, theirs = project((0,))
    gated = gate(mine, theirs, own_taps, answer, cycle)
    moved = lax.all_to_all(gated, "ctx", split_axis=0, concat_axis=0, tiled=True)
    return moved.reshape(cycle * few, length)


def solution(mesh):
    in_specs = (
        P("ctx", "chan"),
        P(None, "chan", None),
        P(None, "chan", None),
        P("chan", "ctx"),
        P("chan"),
    )
    out_specs = P("chan", "ctx")
    return jax.shard_map(body, mesh=mesh, in_specs=in_specs, out_specs=out_specs, check_vma=False)
```

time: 376 us -> 219 us (0.58)
  the two profiles are of different devices: /device:TPU:8 before, /device:TPU:0 now
where the time goes in v1:
time: 219 us; the launch traced here: 217 us
  waiting for transfers between devices  96.1 us (44%)
  starting transfers between devices  41.5 us (19%)
  local copies, waits for them, and re-layouts  34.1 us (16%)
  matrix products  18.1 us (8%)
  Pallas kernels  11 us (5%)
  blocking collectives  10.5 us (5%)
  other arithmetic  5.53 us (3%)
    ppermute x10, waiting for transfers between devices, swap(): lax.ppermute(x, axis, [(i, i ^ bit) for i in range(lax.axis_size(axis))])  39.2 us
    ppermute x6, waiting for transfers between devices, travel(): return lax.ppermute(piece, 'chan', pairs)  31.7 us
    dot_general x8, matrix products, project(): part = jnp.einsum('td,dc->ct', these, piece, preferred_element_type=F32)  18.1 us
    ppermute x3, starting transfers between devices, gather_features(): up = lax.ppermute(up, 'chan', [(i, i + 2) for i in range(size - 2)])  13.5 us
    ppermute x3, waiting for transfers between devices, gather_features(): down = lax.ppermute(down, 'chan', [(i + 2, i) for i in range(size - 2)])  11.6 us
    all_to_all x1, blocking collectives, body(): lax.all_to_all(gated, 'ctx', split_axis=0, concat_axis=0, tiled=True)  10.5 us
    ppermute x10, starting transfers between devices, swap(): lax.ppermute(x, axis, [(i, i ^ bit) for i in range(lax.axis_size(axis))])  10.4 us
    ppermute x6, starting transfers between devices, travel(): return lax.ppermute(piece, 'chan', pairs)  9.49 us
  transfers between devices with their start and end apart: 23, of which 9 were waited for; matrix products, arithmetic and copies ran while one was open for 25% of the time, Pallas kernels for 4%

profile of v1, /device:TPU:0, one launch (start us, length us, event | category | flops | bytes accessed | tf_op | source)
XLA Modules:
  0.0 217.5 jit_solution(12874871623936106311)
XLA Ops:
  1.4 5.6 %collective-permute-start.5 = (bf16[512,512]{1,0:T(8,128)(2,1)}, bf16[512,512]{1,0:T(8,128)(2,1)S(1)}, u32[]{:S(2)}, u32[]{:S(2)}) collective-permute-start(bf16[512,512]{1,0:T(8,128)(2,1)} %param.7), channel_id=1, source_target_pairs={{0,2},{1,3},{2,4},{3,5},{4,6},{5,7},{8,10},{9,11},{10,12},{11,13},... | collective-permute-start | bytes 1572872 | tf_op jit(solution)/shard_map/ppermute | solution.py:197
  10.5 6.6 %collective-permute-done.6 = bf16[512,512]{1,0:T(8,128)(2,1)S(1)} collective-permute-done((bf16[512,512]{1,0:T(8,128)(2,1)}, bf16[512,512]{1,0:T(8,128)(2,1)S(1)}, u32[]{:S(2)}, u32[]{:S(2)}) %collective-permute-start.6) | collective-permute-done | bytes 524320 | tf_op jit(solution)/shard_map/ppermute | solution.py:198
  18.5 4.6 %collective-permute-start.9 = (bf16[512,512]{1,0:T(8,128)(2,1)S(1)}, bf16[512,512]{1,0:T(8,128)(2,1)S(1)}, u32[]{:S(2)}, u32[]{:S(2)}) collective-permute-start(bf16[512,512]{1,0:T(8,128)(2,1)S(1)} %collective-permute-done.5), channel_id=1, source_target_pairs={{0,2},{1,3},{2,4},{3,5},{4,6},{5,7},{8,10},{9,11},{10,12},{11,13},... | collective-permute-start | bytes 1572872 | tf_op jit(solution)/shard_map/ppermute | solution.py:197
  23.1 8.8 %fusion.21 = (bf16[1,512,4096]{2,1,0:T(8,128)(2,1)}, bf16[1,512,4096]{2,1,0:T(8,128)(2,1)}, bf16[1,512,4096]{2,1,0:T(8,128)(2,1)}) fusion(bf16[3,512,4096]{2,1,0:T(8,128)(2,1)} %param.8), kind=kLoop, calls=%fused_computation.72 | loop fusion | bytes 25165824 | tf_op jit(solution)/shard_map/slice | solution.py:223
  36.4 2.6 %collective-permute-start.4 = (bf16[512,256]{1,0:T(8,128)(2,1)}, bf16[512,256]{1,0:T(8,128)(2,1)}, u32[]{:S(2)}, u32[]{:S(2)}) collective-permute-start(bf16[512,256]{1,0:T(8,128)(2,1)} %pad_maximum_fusion.4), channel_id=1, source_target_pairs={{0,2},{1,3},{2,4},{3,5},{4,6},{5,7},{6,0},{7,1},{8,10},{9,11},{10,... | collective-permute-start | bytes 786440 | tf_op jit(solution)/shard_map/ppermute | solution.py:228
  39.1 3.4 %collective-permute-start.10 = (bf16[512,512]{1,0:T(8,128)(2,1)S(1)}, bf16[512,512]{1,0:T(8,128)(2,1)S(1)}, u32[]{:S(2)}, u32[]{:S(2)}) collective-permute-start(bf16[512,512]{1,0:T(8,128)(2,1)S(1)} %collective-permute-done.9), channel_id=1, source_target_pairs={{0,2},{1,3},{2,4},{3,5},{4,6},{5,7},{8,10},{9,11},{10,12},{11,13},... | collective-permute-start | bytes 1572872 | tf_op jit(solution)/shard_map/ppermute | solution.py:197
  42.5 4.7 %collective-permute-done.8 = bf16[512,512]{1,0:T(8,128)(2,1)} collective-permute-done((bf16[512,512]{1,0:T(8,128)(2,1)S(1)}, bf16[512,512]{1,0:T(8,128)(2,1)}, u32[]{:S(2)}, u32[]{:S(2)}) %collective-permute-start.8) | collective-permute-done | bytes 524320 | tf_op jit(solution)/shard_map/ppermute | solution.py:198
  48.3 6.1 %collective-permute-done.10 = bf16[512,512]{1,0:T(8,128)(2,1)S(1)} collective-permute-done((bf16[512,512]{1,0:T(8,128)(2,1)S(1)}, bf16[512,512]{1,0:T(8,128)(2,1)S(1)}, u32[]{:S(2)}, u32[]{:S(2)}) %collective-permute-start.10) | collective-permute-done | bytes 524320 | tf_op jit(solution)/shard_map/ppermute | solution.py:197
  54.5 3.2 %broadcast_in_dim.11 = bf16[3,2048,512]{2,1,0:T(8,128)(2,1)} broadcast(bf16[]{:T(256)} %constant.110.clone.1), dimensions={} | broadcast | bytes 6291458 | tf_op jit(solution)/shard_map/broadcast_in_dim | solution.py:178
  67.7 33.6 %collective-permute-done.2 = bf16[1,256,512]{2,1,0:T(8,128)(2,1)S(1)} collective-permute-done((bf16[1,256,512]{2,1,0:T(8,128)(2,1)S(1)}, bf16[1,256,512]{2,1,0:T(8,128)(2,1)S(1)}, u32[]{:S(2)}, u32[]{:S(2)}) %collective-permute-start.2) | collective-permute-done | bytes 262176 | tf_op jit(solution)/shard_map/ppermute | solution.py:164
  101.2 4.2 %collective-permute-start.15 = (bf16[512,256]{1,0:T(8,128)(2,1)S(1)}, bf16[512,256]{1,0:T(8,128)(2,1)S(1)}, u32[]{:S(2)}, u32[]{:S(2)}) collective-permute-start(bf16[512,256]{1,0:T(8,128)(2,1)S(1)} %copy-done.13), channel_id=1, source_target_pairs={{0,4},{1,5},{2,6},{3,7},{4,0},{5,1},{6,2},{7,3},{8,12},{9,13},{10,... | collective-permute-start | bytes 786440 | tf_op jit(solution)/shard_map/ppermute | solution.py:228
  112.0 2.7 %constant_dynamic-update-slice_fusion.3 = bf16[3,2048,512]{2,1,0:T(8,128)(2,1)} fusion(bf16[3,2048,512]{2,1,0:T(8,128)(2,1)} %get-tuple-element.37, bf16[3,512,512]{2,1,0:T(8,128)(2,1)} %collective-permute-done.11, s32[]{:T(128)S(6)} %select_n.126), kind=kLoop, calls=%fused_computation.66 | loop fusion | bytes 3145732 | tf_op jit(solution)/shard_map/dynamic_update_slice | solution.py:186
  114.7 2.7 %constant_dynamic-update-slice_fusion.2 = bf16[3,2048,512]{2,1,0:T(8,128)(2,1)} fusion(bf16[3,2048,512]{2,1,0:T(8,128)(2,1)} %constant_dynamic-update-slice_fusion.3, bf16[3,512,512]{2,1,0:T(8,128)(2,1)} %collective-permute-done.12, s32[]{:T(128)S(6)} %select_n.127), kind=kLoop, calls=%fused_computation.65 | loop fusion | bytes 3145732 | tf_op jit(solution)/shard_map/dynamic_update_slice | solution.py:186
  117.4 5.6 %collective-permute-done.13 = bf16[3,256,512]{2,1,0:T(8,128)(2,1)S(1)} collective-permute-done((bf16[3,256,512]{2,1,0:T(8,128)(2,1)S(1)}, bf16[3,256,512]{2,1,0:T(8,128)(2,1)S(1)}, u32[]{:S(2)}, u32[]{:S(2)}) %collective-permute-start.13) | collective-permute-done | bytes 786464 | tf_op jit(solution)/shard_map/ppermute | solution.py:164
  127.4 20.8 %collective-permute-done.19 = bf16[512,512]{1,0:T(8,128)(2,1)S(1)} collective-permute-done((bf16[512,512]{1,0:T(8,128)(2,1)S(1)}, bf16[512,512]{1,0:T(8,128)(2,1)S(1)}, u32[]{:S(2)}, u32[]{:S(2)}) %collective-permute-start.19) | collective-permute-done | bytes 524320 | tf_op jit(solution)/shard_map/ppermute | solution.py:228
  148.2 2.9 %fusion.4 = f32[512,2048]{1,0:T(8,128)S(1)} fusion(bf16[512,512]{1,0:T(8,128)(2,1)S(1)} %collective-permute-done.19, bf16[3,2048,512]{2,1,0:T(8,128)(2,1)} %constant_dynamic-update-slice_fusion), kind=kOutput, calls=%fused_computation.9 | convolution fusion | flops 1073741824 | bytes 6815744 | tf_op jit(solution)/shard_map/td,dc->ct/dot_general | solution.py:246
  151.2 2.9 %fusion.2 = f32[512,2048]{1,0:T(8,128)S(1)} fusion(bf16[512,512]{1,0:T(8,128)(2,1)S(1)} %collective-permute-done.18, bf16[3,2048,512]{2,1,0:T(8,128)(2,1)} %constant_dynamic-update-slice_fusion), kind=kOutput, calls=%fused_computation.7 | convolution fusion | flops 1073741824 | bytes 6815744 | tf_op jit(solution)/shard_map/td,dc->ct/dot_general | solution.py:246
  154.1 10.9 %collective-permute-done.20 = bf16[512,512]{1,0:T(8,128)(2,1)S(1)} collective-permute-done((bf16[512,512]{1,0:T(8,128)(2,1)S(1)}, bf16[512,512]{1,0:T(8,128)(2,1)S(1)}, u32[]{:S(2)}, u32[]{:S(2)}) %collective-permute-start.20) | collective-permute-done | bytes 524320 | tf_op jit(solution)/shard_map/ppermute | solution.py:228
  165.0 3.0 %add_add_fusion = f32[512,2048]{1,0:T(8,128)S(1)} fusion(f32[512,2048]{1,0:T(8,128)S(1)} %fusion.4, f32[512,2048]{1,0:T(8,128)S(1)} %fusion.8, f32[512,2048]{1,0:T(8,128)S(1)} %fusion.2, bf16[512,512]{1,0:T(8,128)(2,1)S(1)} %collective-permute-done.20, bf16[3,2048,512]{2,1,0:T(8,128)(2,1)} %constant_dynamic-update-slice_fusion), kind=kOutput, calls=%fused_computation | convolution fusion | flops 1076887552 | bytes 19398656 | tf_op jit(solution)/shard_map/td,dc->ct/dot_general | solution.py:246
  174.3 2.6 %fusion.3 = f32[256,2048]{1,0:T(8,128)S(1)} fusion(bf16[512,256]{1,0:T(8,128)(2,1)} %collective-permute-done.4, bf16[3,2048,512]{2,1,0:T(8,128)(2,1)} %constant_dynamic-update-slice_fusion), kind=kOutput, calls=%fused_computation.8 | convolution fusion | flops 536870912 | bytes 4456448 | tf_op jit(solution)/shard_map/td,dc->ct/dot_general | solution.py:246
  179.8 4.1 %all-to-all-start = ((bf16[4,128,512]{2,1,0:T(8,128)(2,1)}), bf16[4,128,512]{2,1,0:T(8,128)(2,1)}, u32[]{:S(2)}, u32[]{:S(2)}) async-start(bf16[4,128,512]{2,1,0:T(8,128)(2,1)} %bitcast.93), calls=%async_computation | async-start | bytes 1048576 | tf_op jit(solution)/shard_map/all_to_all | solution.py:230
  185.0 7.5 %all-to-all-done.taps_ref = bf16[4,128,512]{2,1,0:T(8,128)(2,1)} async-done(((bf16[4,128,512]{2,1,0:T(8,128)(2,1)}), bf16[4,128,512]{2,1,0:T(8,128)(2,1)}, u32[]{:S(2)}, u32[]{:S(2)}) %all-to-all-start) | async-done | bytes 524320 | tf_op jit(solution)/shard_map/all_to_all | solution.py:230
  197.6 6.5 %convolve.1.answer_ref = f32[128,2048]{1,0:T(8,128)S(1)} custom-call(f32[2,128,2048]{2,1,0:T(8,128)S(1)} %bitcast.91, f32[2,128,2048]{2,1,0:T(8,128)} %bitcast.36.other_ref, f32[3,128,3]{2,1,0:T(8,128)S(1)} %copy.10.taps_ref, f32[128,1]{1,0:T(8,128)S(1)} %copy.9.skip_ref, f32[4,128,1024]{2,1,0:T(8,128)} %copy-done.1, bf16[512,1024]{1,0:T(8,128)(2,1)S(1)} %copy-done.3, ...), custom_call_target="tpu_custom_call" | custom-call | tf_op jit(solution)/shard_map/convolve/pallas_call | solution.py:118
  206.1 10.5 %all_to_all.10 = bf16[4,128,512]{2,1,0:T(8,128)(2,1)S(1)} all-to-all(bf16[4,128,512]{2,1,0:T(8,128)(2,1)S(1)} %gate.1), channel_id=1, replica_groups=mesh['ctx'=4,'chan'=8] {'ctx'}, dimensions={0} | all-to-all | bytes 1048576 | tf_op jit(solution)/shard_map/all_to_all | solution.py:260
  (97 shorter events, 50.9 us)
Async XLA Ops:
  0.0 184.8 %copy-start = (f32[3,512,3]{1,2,0:T(4,128)S(1)}, f32[3,512,3]{1,2,0:T(4,128)}, u32[]{:S(2)}) copy-start(f32[3,512,3]{1,2,0:T(4,128)} %param.9) | copy-start | bytes 55300
  0.0 17.2 %collective-permute-start.6 = (bf16[512,512]{1,0:T(8,128)(2,1)}, bf16[512,512]{1,0:T(8,128)(2,1)S(1)}, u32[]{:S(2)}, u32[]{:S(2)}) collective-permute-start(bf16[512,512]{1,0:T(8,128)(2,1)} %param.7), channel_id=1, source_target_pairs={{2,0},{3,1},{4,2},{5,3},{6,4},{7,5},{10,8},{11,9},{12,10},{13,11},... | collective-permute-start | bytes 1572872 | tf_op jit(solution)/shard_map/ppermute | solution.py:198
  1.4 17.1 %collective-permute-start.5 = (bf16[512,512]{1,0:T(8,128)(2,1)}, bf16[512,512]{1,0:T(8,128)(2,1)S(1)}, u32[]{:S(2)}, u32[]{:S(2)}) collective-permute-start(bf16[512,512]{1,0:T(8,128)(2,1)} %param.7), channel_id=1, source_target_pairs={{0,2},{1,3},{2,4},{3,5},{4,6},{5,7},{8,10},{9,11},{10,12},{11,13},... | collective-permute-start | bytes 1572872 | tf_op jit(solution)/shard_map/ppermute | solution.py:197
  7.0 59.2 %collective-permute-start.1 = (bf16[1,512,512]{2,1,0:T(8,128)(2,1)}, bf16[1,512,512]{2,1,0:T(8,128)(2,1)S(1)}, u32[]{:S(2)}, u32[]{:S(2)}) collective-permute-start(bf16[1,512,512]{2,1,0:T(8,128)(2,1)} %bitcast.94), channel_id=1, source_target_pairs={{0,16},{8,24},{16,0},{24,8},{1,17},{9,25},{17,1},{25,9},{2,18},{10... | collective-permute-start | bytes 1572872 | tf_op jit(solution)/shard_map/ppermute | solution.py:164
  9.0 57.8 %collective-permute-start = (bf16[1,512,512]{2,1,0:T(8,128)(2,1)}, bf16[1,512,512]{2,1,0:T(8,128)(2,1)S(1)}, u32[]{:S(2)}, u32[]{:S(2)}) collective-permute-start(bf16[1,512,512]{2,1,0:T(8,128)(2,1)} %bitcast.95), channel_id=1, source_target_pairs={{0,8},{8,0},{16,24},{24,16},{1,9},{9,1},{17,25},{25,17},{2,10},{10... | collective-permute-start | bytes 1572872 | tf_op jit(solution)/shard_map/ppermute | solution.py:164
  17.2 15.0 %collective-permute-start.7 = (bf16[512,512]{1,0:T(8,128)(2,1)S(1)}, bf16[512,512]{1,0:T(8,128)(2,1)S(1)}, u32[]{:S(2)}, u32[]{:S(2)}) collective-permute-start(bf16[512,512]{1,0:T(8,128)(2,1)S(1)} %collective-permute-done.6), channel_id=1, source_target_pairs={{2,0},{3,1},{4,2},{5,3},{6,4},{7,5},{10,8},{11,9},{12,10},{13,11},... | collective-permute-start | bytes 1572872 | tf_op jit(solution)/shard_map/ppermute | solution.py:198
  18.5 20.6 %collective-permute-start.9 = (bf16[512,512]{1,0:T(8,128)(2,1)S(1)}, bf16[512,512]{1,0:T(8,128)(2,1)S(1)}, u32[]{:S(2)}, u32[]{:S(2)}) collective-permute-start(bf16[512,512]{1,0:T(8,128)(2,1)S(1)} %collective-permute-done.5), channel_id=1, source_target_pairs={{0,2},{1,3},{2,4},{3,5},{4,6},{5,7},{8,10},{9,11},{10,12},{11,13},... | collective-permute-start | bytes 1572872 | tf_op jit(solution)/shard_map/ppermute | solution.py:197
  32.2 15.0 %collective-permute-start.8 = (bf16[512,512]{1,0:T(8,128)(2,1)S(1)}, bf16[512,512]{1,0:T(8,128)(2,1)}, u32[]{:S(2)}, u32[]{:S(2)}) collective-permute-start(bf16[512,512]{1,0:T(8,128)(2,1)S(1)} %collective-permute-done.7), channel_id=1, source_target_pairs={{2,0},{3,1},{4,2},{5,3},{6,4},{7,5},{10,8},{11,9},{12,10},{13,11},... | collective-permute-start | bytes 1572872 | tf_op jit(solution)/shard_map/ppermute | solution.py:198
  36.4 137.9 %collective-permute-start.4 = (bf16[512,256]{1,0:T(8,128)(2,1)}, bf16[512,256]{1,0:T(8,128)(2,1)}, u32[]{:S(2)}, u32[]{:S(2)}) collective-permute-start(bf16[512,256]{1,0:T(8,128)(2,1)} %pad_maximum_fusion.4), channel_id=1, source_target_pairs={{0,2},{1,3},{2,4},{3,5},{4,6},{5,7},{6,0},{7,1},{8,10},{9,11},{10,... | collective-permute-start | bytes 786440 | tf_op jit(solution)/shard_map/ppermute | solution.py:228
  39.1 15.4 %collective-permute-start.10 = (bf16[512,512]{1,0:T(8,128)(2,1)S(1)}, bf16[512,512]{1,0:T(8,128)(2,1)S(1)}, u32[]{:S(2)}, u32[]{:S(2)}) collective-permute-start(bf16[512,512]{1,0:T(8,128)(2,1)S(1)} %collective-permute-done.9), channel_id=1, source_target_pairs={{0,2},{1,3},{2,4},{3,5},{4,6},{5,7},{8,10},{9,11},{10,12},{11,13},... | collective-permute-start | bytes 1572872 | tf_op jit(solution)/shard_map/ppermute | solution.py:197
  59.6 45.9 %collective-permute-start.12 = (bf16[3,512,512]{2,1,0:T(8,128)(2,1)}, bf16[3,512,512]{2,1,0:T(8,128)(2,1)}, u32[]{:S(2)}, u32[]{:S(2)}) collective-permute-start(bf16[3,512,512]{2,1,0:T(8,128)(2,1)} %get-tuple-element.36), channel_id=1, source_target_pairs={{0,16},{8,24},{16,0},{24,8},{1,17},{9,25},{17,1},{25,9},{2,18},{10... | collective-permute-start | bytes 4718600 | tf_op jit(solution)/shard_map/ppermute | solution.py:164
  61.9 46.4 %collective-permute-start.11 = (bf16[3,512,512]{2,1,0:T(8,128)(2,1)}, bf16[3,512,512]{2,1,0:T(8,128)(2,1)}, u32[]{:S(2)}, u32[]{:S(2)}) collective-permute-start(bf16[3,512,512]{2,1,0:T(8,128)(2,1)} %get-tuple-element.36), channel_id=1, source_target_pairs={{0,8},{8,0},{16,24},{24,16},{1,9},{9,1},{17,25},{25,17},{2,10},{10... | collective-permute-start | bytes 4718600 | tf_op jit(solution)/shard_map/ppermute | solution.py:164
  66.3 34.9 %collective-permute-start.2 = (bf16[1,256,512]{2,1,0:T(8,128)(2,1)S(1)}, bf16[1,256,512]{2,1,0:T(8,128)(2,1)S(1)}, u32[]{:S(2)}, u32[]{:S(2)}) collective-permute-start(bf16[1,256,512]{2,1,0:T(8,128)(2,1)S(1)} %slice.80), channel_id=1, source_target_pairs={{0,8},{8,0},{16,24},{24,16},{1,9},{9,1},{17,25},{25,17},{2,10},{10... | collective-permute-start | bytes 786440 | tf_op jit(solution)/shard_map/ppermute | solution.py:164
  66.9 39.8 %collective-permute-start.3 = (bf16[1,256,512]{2,1,0:T(8,128)(2,1)S(1)}, bf16[1,256,512]{2,1,0:T(8,128)(2,1)S(1)}, u32[]{:S(2)}, u32[]{:S(2)}) collective-permute-start(bf16[1,256,512]{2,1,0:T(8,128)(2,1)S(1)} %slice.81), channel_id=1, source_target_pairs={{0,16},{8,24},{16,0},{24,8},{1,17},{9,25},{17,1},{25,9},{2,18},{10... | collective-permute-start | bytes 786440 | tf_op jit(solution)/shard_map/ppermute | solution.py:164
  101.2 70.7 %collective-permute-start.15 = (bf16[512,256]{1,0:T(8,128)(2,1)S(1)}, bf16[512,256]{1,0:T(8,128)(2,1)S(1)}, u32[]{:S(2)}, u32[]{:S(2)}) collective-permute-start(bf16[512,256]{1,0:T(8,128)(2,1)S(1)} %copy-done.13), channel_id=1, source_target_pairs={{0,4},{1,5},{2,6},{3,7},{4,0},{5,1},{6,2},{7,3},{8,12},{9,13},{10,... | collective-permute-start | bytes 786440 | tf_op jit(solution)/shard_map/ppermute | solution.py:228
  105.5 42.8 %collective-permute-start.19 = (bf16[512,512]{1,0:T(8,128)(2,1)S(1)}, bf16[512,512]{1,0:T(8,128)(2,1)S(1)}, u32[]{:S(2)}, u32[]{:S(2)}) collective-permute-start(bf16[512,512]{1,0:T(8,128)(2,1)S(1)} %pad_maximum_fusion.2), channel_id=1, source_target_pairs={{0,4},{1,5},{2,6},{3,7},{4,0},{5,1},{6,2},{7,3},{8,12},{9,13},{10,... | collective-permute-start | bytes 1572872 | tf_op jit(solution)/shard_map/ppermute | solution.py:228
  106.8 16.3 %collective-permute-start.13 = (bf16[3,256,512]{2,1,0:T(8,128)(2,1)S(1)}, bf16[3,256,512]{2,1,0:T(8,128)(2,1)S(1)}, u32[]{:S(2)}, u32[]{:S(2)}) collective-permute-start(bf16[3,256,512]{2,1,0:T(8,128)(2,1)S(1)} %slice.82), channel_id=1, source_target_pairs={{0,8},{8,0},{16,24},{24,16},{1,9},{9,1},{17,25},{25,17},{2,10},{10... | collective-permute-start | bytes 2359304 | tf_op jit(solution)/shard_map/ppermute | solution.py:164
  110.1 16.3 %collective-permute-start.14 = (bf16[3,256,512]{2,1,0:T(8,128)(2,1)S(1)}, bf16[3,256,512]{2,1,0:T(8,128)(2,1)S(1)}, u32[]{:S(2)}, u32[]{:S(2)}) collective-permute-start(bf16[3,256,512]{2,1,0:T(8,128)(2,1)S(1)} %slice.83), channel_id=1, source_target_pairs={{0,16},{8,24},{16,0},{24,8},{1,17},{9,25},{17,1},{25,9},{2,18},{10... | collective-permute-start | bytes 2359304 | tf_op jit(solution)/shard_map/ppermute | solution.py:164
  123.0 46.5 %collective-permute-start.16 = (bf16[512,256]{1,0:T(8,128)(2,1)S(1)}, bf16[512,256]{1,0:T(8,128)(2,1)S(1)}, u32[]{:S(2)}, u32[]{:S(2)}) collective-permute-start(bf16[512,256]{1,0:T(8,128)(2,1)S(1)} %copy-done.12), channel_id=1, source_target_pairs={{0,6},{1,7},{2,0},{3,1},{4,2},{5,3},{6,4},{7,5},{8,14},{9,15},{10,... | collective-permute-start | bytes 786440 | tf_op jit(solution)/shard_map/ppermute | solution.py:228
  126.4 24.7 %collective-permute-start.18 = (bf16[512,512]{1,0:T(8,128)(2,1)S(1)}, bf16[512,512]{1,0:T(8,128)(2,1)S(1)}, u32[]{:S(2)}, u32[]{:S(2)}) collective-permute-start(bf16[512,512]{1,0:T(8,128)(2,1)S(1)} %pad_maximum_fusion.1), channel_id=1, source_target_pairs={{0,2},{1,3},{2,4},{3,5},{4,6},{5,7},{6,0},{7,1},{8,10},{9,11},{10,... | collective-permute-start | bytes 1572872 | tf_op jit(solution)/shard_map/ppermute | solution.py:228
  148.2 16.7 %collective-permute-start.20 = (bf16[512,512]{1,0:T(8,128)(2,1)S(1)}, bf16[512,512]{1,0:T(8,128)(2,1)S(1)}, u32[]{:S(2)}, u32[]{:S(2)}) collective-permute-start(bf16[512,512]{1,0:T(8,128)(2,1)S(1)} %pad_maximum_fusion.3), channel_id=1, source_target_pairs={{0,6},{1,7},{2,0},{3,1},{4,2},{5,3},{6,4},{7,5},{8,14},{9,15},{10,... | collective-permute-start | bytes 1572872 | tf_op jit(solution)/shard_map/ppermute | solution.py:228
  169.5 28.1 %collective-permute-start.21 = (f32[256,2048]{1,0:T(8,128)}, f32[256,2048]{1,0:T(8,128)}, u32[]{:S(2)}, u32[]{:S(2)}) collective-permute-start(f32[256,2048]{1,0:T(8,128)} %get-tuple-element.8), channel_id=1, source_target_pairs={{0,1},{1,0},{2,3},{3,2},{4,5},{5,4},{6,7},{7,6},{8,9},{9,8},{10,11... | collective-permute-start | bytes 6291464 | tf_op jit(solution)/shard_map/ppermute | solution.py:164
  179.3 24.9 %collective-permute-start.17 = (f32[128,2048]{1,0:T(8,128)}, f32[128,2048]{1,0:T(8,128)}, u32[]{:S(2)}, u32[]{:S(2)}) collective-permute-start(f32[128,2048]{1,0:T(8,128)} %get-tuple-element.34), channel_id=1, source_target_pairs={{0,1},{1,0},{2,3},{3,2},{4,5},{5,4},{6,7},{7,6},{8,9},{9,8},{10,11... | collective-permute-start | bytes 3145736 | tf_op jit(solution)/shard_map/ppermute | solution.py:164
  179.8 12.7 %all-to-all-start = ((bf16[4,128,512]{2,1,0:T(8,128)(2,1)}), bf16[4,128,512]{2,1,0:T(8,128)(2,1)}, u32[]{:S(2)}, u32[]{:S(2)}) async-start(bf16[4,128,512]{2,1,0:T(8,128)(2,1)} %bitcast.93), calls=%async_computation | async-start | bytes 1048576 | tf_op jit(solution)/shard_map/all_to_all | solution.py:230
  (13 other events, 90.4 us)

commit v2 on v1

--- a/solution.py
+++ b/solution.py
@@ -9,7 +9,8 @@
 from jax.experimental.pallas import tpu as pltpu
 from jax.sharding import PartitionSpec as P
 
-VMEM_LIMIT = 48 * 1024 * 1024
+VMEM_LIMIT = 32 * 1024 * 1024
+PROJECT_LIMIT = 60 * 1024 * 1024
 F32 = jnp.float32
 BF16 = jnp.bfloat16
 
@@ -164,47 +165,252 @@
     return lax.ppermute(x, axis, [(i, i ^ bit) for i in range(lax.axis_size(axis))])
 
 
-def gather_context(block):
-    size = lax.axis_size("ctx")
-    if size != 4:
-        return lax.all_gather(block, "ctx", axis=1, tiled=True)
+def pick_kernel(at_ref, in_proj_ref, *refs):
+    chips = len(refs) // 2
+    few = in_proj_ref.shape[2]
+    for s in range(chips):
+
+        @pl.when(pl.program_id(0) // 2 == s)
+        def _():
+            refs[s][:, :few] = in_proj_ref[1]
+            refs[s][:, few:] = in_proj_ref[2]
+            refs[chips + s][...] = in_proj_ref[0]
+
+
+def pick_columns(in_proj, chips, few, place, core, me, cycle):
+    depth = in_proj.shape[1]
+    order = [2 * (place ^ s) + (core ^ side) for s in range(chips) for side in range(2)]
+    at = jnp.stack([o * cycle + me for o in order]).astype(jnp.int32)
+    if few % 128:
+        parts = [
+            [lax.dynamic_slice_in_dim(in_proj[k], at[n] * few, few, axis=1) for n in range(2 * chips)]
+            for k in range(3)
+        ]
+        pairs = [
+            jnp.concatenate([parts[k][2 * s + side] for side in range(2) for k in (1, 2)], axis=1)
+            for s in range(chips)
+        ]
+        singles = [jnp.concatenate(parts[0][2 * s : 2 * s + 2], axis=1) for s in range(chips)]
+        return pairs, singles
+
+    def target(s):
+        return lambda g, at: (0, jnp.clip(g - 2 * s, 0, 1))
+
+    outs = pl.pallas_call(
+        pick_kernel,
+        grid_spec=pltpu.PrefetchScalarGridSpec(
+            num_scalar_prefetch=1,
+            grid=(2 * chips,),
+            in_specs=[pl.BlockSpec((3, depth, few), lambda g, at: (0, 0, at[g]))],
+            out_specs=[pl.BlockSpec((depth, 2 * few), target(s)) for s in range(chips)]
+            + [pl.BlockSpec((depth, few), target(s)) for s in range(chips)],
+        ),
+        out_shape=[jax.ShapeDtypeStruct((depth, 4 * few), BF16)] * chips
+        + [jax.ShapeDtypeStruct((depth, 2 * few), BF16)] * chips,
+        compiler_params=pltpu.CompilerParams(vmem_limit_bytes=VMEM_LIMIT),
+        name="pick_columns",
+    )(at, in_proj)
+    return outs[:chips], outs[chips:]
+
+
+def swap_far(block):
+    return swap(block, "ctx", 1), swap(block, "ctx", 2)
+
+
+def move_chips(x, pairs):
+    return lax.ppermute(x, "chan", [(2 * a + k, 2 * b + k) for a, b in pairs for k in range(2)])
+
+
+def turn_chips(x, s):
+    return move_chips(x, [(z, z ^ s) for z in range(lax.axis_size("chan") // 2)])
+
+
+def gather(block, pairs, singles, long_filter, move_filter, make_waves):
+    place = lax.axis_index("chan") // 2
+    middle = [(1, 2), (2, 1)]
+    ends = [(1, 0), (2, 3)]
+    inner = (place == 1) | (place == 2)
+    order = lax.optimization_barrier
+    pairs, singles = list(pairs), list(singles)
+    length = block.shape[0]
+    half = length // 2
+
+    def spread(near, far, own):
+        if near is None:
+            return swap_far(own)
+        skip = near.shape[0] - length
+        to_near, to_far = far[skip : skip + half], near[skip + half :]
+        if own is not None:
+            to_near, to_far = jnp.concatenate([to_near, own]), jnp.concatenate([to_far, own])
+        return swap(to_near, "ctx", 1), swap(to_far, "ctx", 2)
+
+    pair = move_chips(block, [(0, 1), (1, 0), (2, 3), (3, 2)])
+    across = move_chips(block, middle)
+    near0, far0 = spread(None, None, block)
+    pair, across, near0, far0, pairs, singles, long_filter = order(
+        (pair, across, near0, far0, pairs, singles, long_filter)
+    )
+
+    farther = move_chips(pair, middle)
+    second = move_chips(across, ends)
+    near1, far1 = spread(near0, far0, pair)
+    pairs[3] = turn_chips(pairs[3], 3)
+    pair_3 = pairs.pop()
+    farther, second, near1, far1, pairs, singles, long_filter = order(
+        (farther, second, near1, far1, pairs, singles, long_filter)
+    )
+
+    second = jnp.where(inner, across, second)
+    third = move_chips(farther, ends)
+    near2, far2 = spread(near1, far1, second)
+    pair_2 = turn_chips(pairs[2], 2)
+    moved_filter = move_filter(long_filter)
+    third, near2, far2, pair_3, pairs, singles, moved_filter = order(
+        (third, near2, far2, pair_3, pairs, singles, moved_filter)
+    )
+
+    third = jnp.where(inner, farther, third)
+    near3, far3 = spread(near2, far2, third)
+    pair_1 = turn_chips(pairs[1], 1)
+    single_3 = turn_chips(singles[3], 3)
+    waves = make_waves(moved_filter)
+    near3, far3, pair_2, pair_1, singles, waves = order(
+        (near3, far3, pair_2, pair_1, singles, waves)
+    )
+
+    near4, far4 = spread(near3, far3, None)
+    single_1, single_2 = turn_chips(singles[1], 1), turn_chips(singles[2], 2)
+    pairs = [pairs[0], pair_1, pair_2, pair_3]
+    singles = [singles[0], single_1, single_2, single_3]
+    slots = (
+        [block, pair, second, third],
+        [near0, near1, near2, near3, near4],
+        [far0, far1, far2, far3, far4],
+    )
+    return slots, pairs, singles, waves
+
+
+def gather_plain(block, pairs, singles, long_filter, move_filter, make_waves):
+    chips = lax.axis_size("chan") // 2
+    slots = [turn_chips(block, s) if s else block for s in range(chips)]
+    pairs, singles = (
+        [turn_chips(x, s) if s else x for s, x in enumerate(w)] for w in (pairs, singles)
+    )
+    return slots, pairs, singles, make_waves(move_filter(long_filter))
+
+
+def project_kernel(plan, which, arrays, adds, at_ref, *refs):
+    weights_refs, refs = refs[:4], refs[4:]
+    pieces, refs = refs[:arrays], refs[arrays:]
+    sums, (own_ref, other_ref, weights, values, weight_sems, sems) = refs[: 2 * adds], refs[2 * adds :]
+    rows = own_ref.shape[0]
+    length = values.shape[1] // 4
+    weight_copies = [
+        pltpu.make_async_copy(weights_refs[s], weights.at[s], weight_sems.at[s]) for s in range(4)
+    ]
+    copies = [
+        [
+            pltpu.make_async_copy(
+                pieces[array].at[pl.ds(start, count)],
+                values.at[s, pl.ds(target, count)],
+                sems.at[5 * s + n],
+            )
+            for n, (array, start, count, target) in enumerate(plan[s])
+        ]
+        for s in range(len(plan))
+    ]
+    for copy in weight_copies:
+        copy.start()
+    for slot in copies:
+        for copy in slot:
+            copy.start()
+    for copy in weight_copies:
+        copy.wait()
+    for s in range(len(plan)):
+        turned = weights[at_ref[4 + which[s]]].T
+        for copy in copies[s]:
+            copy.wait()
+        for q in range(4):
+            part = lax.dot_general(
+                turned,
+                values[s, q * length : (q + 1) * length],
+                (((1,), (1,)), ((), ())),
+                preferred_element_type=F32,
+            )
+            span = pl.ds(pl.multiple_of(at_ref[q], length), length)
+            if s:
+                own_ref[:, span] += part[:rows]
+                other_ref[:, span] += part[rows:]
+            elif adds:
+                own_ref[:, span] = sums[0][:, span] + part[:rows]
+                other_ref[:, span] = sums[1][:, span] + part[rows:]
+            else:
+                own_ref[:, span] = part[:rows]
+                other_ref[:, span] = part[rows:]
+
+
+def project_plain(slots, weights):
+    total = 0.0
+    for block, piece in zip(slots, weights):
+        full = lax.all_gather(block, "ctx", axis=0, tiled=True)
+        total = total + jnp.einsum("td,dc->ct", full, piece, preferred_element_type=F32)
+    rows = total.shape[0] // 2
+    return total[:rows], total[rows:]
+
+
+def project(slots, weights, first, last, sums=()):
+    blocks, near, far = slots
+    length, depth = blocks[0].shape
+    half = length // 2
+    rows = weights[0].shape[1] // 2
     me = lax.axis_index("ctx")
-    groups, length, depth = block.shape
-    half = length // 2
-    near = swap(block, "ctx", 1)
-    far = swap(block, "ctx", 2)
-    first = swap(far[:, :half], "ctx", 1)
-    second = swap(near[:, half:], "ctx", 2)
-    whole = jnp.zeros((groups, size * length, depth), block.dtype)
-    for piece, row in (
-        (block, me * length),
-        (near, (me ^ 1) * length),
-        (far, (me ^ 2) * length),
-        (first, (me ^ 3) * length),
-        (second, (me ^ 3) * length + half),
-    ):
-        whole = lax.dynamic_update_slice(whole, piece, (0, row, 0))
-    return whole
-
-
-def gather_features(block):
-    size = lax.axis_size("chan")
-    chips = size // 2
     place = lax.axis_index("chan") // 2
-    left, right = [], []
-    up, down = block, block
-    for _ in range(1, chips):
-        up = lax.ppermute(up, "chan", [(i, i + 2) for i in range(size - 2)])
-        down = lax.ppermute(down, "chan", [(i + 2, i) for i in range(size - 2)])
-        left.append(up)
-        right.append(down)
-    return jnp.stack(
-        [jnp.where(place >= s, left[s - 1], right[chips - s - 1]) for s in range(1, chips)]
-    )
+    swapped = jnp.where((place == 1) | (place == 2), 1, 0)
+    at = jnp.stack([(me ^ q) * length for q in range(4)] + [0 * me, 0 * me + 1, 2 + swapped, 3 - swapped])
+    arrays, plan = [], []
+
+    def place_of(x):
+        for n, y in enumerate(arrays):
+            if y is x:
+                return n
+        arrays.append(x)
+        return len(arrays) - 1
+
+    for s in range(first, last):
+        skip = half if s else 0
+        plan.append(
+            (
+                (place_of(blocks[s]), 0, length, 0),
+                (place_of(near[s]), skip, length, length),
+                (place_of(far[s]), skip, length, 2 * length),
+                (place_of(near[s + 1]), 0, half, 3 * length),
+                (place_of(far[s + 1]), 0, half, 3 * length + half),
+            )
+        )
+    out = jax.ShapeDtypeStruct((rows, 4 * length), F32)
+    spec = pl.BlockSpec((rows, 4 * length), lambda g, at: (0, 0))
+    return pl.pallas_call(
+        functools.partial(project_kernel, plan, range(first, last), len(arrays), len(sums) // 2),
+        grid_spec=pltpu.PrefetchScalarGridSpec(
+            num_scalar_prefetch=1,
+            grid=(1,),
+            in_specs=[pl.BlockSpec(memory_space=pl.ANY)] * (4 + len(arrays)) + [spec] * len(sums),
+            out_specs=[spec] * 2,
+            scratch_shapes=[
+                pltpu.VMEM((4, *weights[0].shape), BF16),
+                pltpu.VMEM((last - first, 4 * length, depth), BF16),
+                pltpu.SemaphoreType.DMA((4,)),
+                pltpu.SemaphoreType.DMA((5 * (last - first),)),
+            ],
+        ),
+        out_shape=[out, out],
+        compiler_params=pltpu.CompilerParams(vmem_limit_bytes=PROJECT_LIMIT),
+        name="project",
+    )(at.astype(jnp.int32), *weights, *arrays, *sums)
 
 
 def body(tokens, in_proj, short_taps, long_filter, skip_gain):
-    length, _ = tokens.shape
+    length, depth = tokens.shape
     cycle = lax.axis_size("ctx")
     size = lax.axis_size("chan")
     chips = size // 2
@@ -212,51 +418,35 @@
     place = lax.axis_index("chan") // 2
     core = lax.axis_index("chan") % 2
     few = in_proj.shape[2] // (size * cycle)
+    span = length * cycle
     high, low = (jnp.asarray(t) for t in wave_tables(length))
-
-    def columns(s, streams):
-        owner = (place + s) % chips
-        parts = []
-        for side in range(2):
-            start = ((2 * owner + (core ^ side)) * cycle + me) * few
-            for k in streams:
-                parts.append(lax.dynamic_slice_in_dim(in_proj[k], start, few, axis=1))
-        return jnp.concatenate(parts, axis=1)
-
-    def travel(piece, s):
-        pairs = [(i, (i + 2 * s) % size) for i in range(size)]
-        return lax.ppermute(piece, "chan", pairs)
-
-    moved_filter = lax.all_to_all(
-        long_filter.reshape(cycle, few, length), "ctx", split_axis=0, concat_axis=0, tiled=True
-    )
-    waves = filter_waves(moved_filter, high, low)
-
-    others = gather_features(tokens)
-    own_tokens = gather_context(tokens[None])[0]
-    other_tokens = gather_context(others)
-
-    def project(streams):
-        total = None
-        for s in range(chips):
-            piece = columns(s, streams)
-            if s:
-                piece = travel(piece, s)
-            these = own_tokens if s == 0 else other_tokens[s - 1]
-            part = jnp.einsum("td,dc->ct", these, piece, preferred_element_type=F32)
-            total = part if total is None else total + part
-        rows = len(streams) * few
-        return total[:rows], swap(total[rows:], "chan", 1)
-
+    pairs, singles = pick_columns(in_proj, chips, few, place, core, me, cycle)
+    fits = cycle == 4 and chips == 4 and length % 512 == 0 and depth % 128 == 0
+
+    def move_filter(values):
+        return lax.all_to_all(
+            values.reshape(cycle, few, length), "ctx", split_axis=0, concat_axis=0, tiled=True
+        )
+
+    def make_waves(moved):
+        return filter_waves(moved, high, low)
+
+    slots, pairs, singles, waves = (gather if fits else gather_plain)(
+        tokens, pairs, singles, long_filter, move_filter, make_waves
+    )
     own_taps = lax.dynamic_slice_in_dim(short_taps, me * few, few, axis=1)
     own_skip = lax.dynamic_slice_in_dim(skip_gain, me * few, few)[:, None]
-    span = own_tokens.shape[0]
-    mine, theirs = project((1, 2))
+    if fits:
+        sums, singles = lax.optimization_barrier((project(slots, pairs, 0, 3), singles))
+        mine, send = project(slots, pairs, 3, 4, sums)
+    else:
+        mine, send = project_plain(slots, pairs)
+    theirs = swap(send, "chan", 1)
     answer = convolve(
         mine.reshape(2, few, span), theirs.reshape(2, few, span), own_taps, own_skip, waves, high, low
     )
-    mine, theirs = project((0,))
-    gated = gate(mine, theirs, own_taps, answer, cycle)
+    mine, send = project(slots, singles, 0, 4) if fits else project_plain(slots, singles)
+    gated = gate(mine, swap(send, "chan", 1), own_taps, answer, cycle)
     moved = lax.all_to_all(gated, "ctx", split_axis=0, concat_axis=0, tiled=True)
     return moved.reshape(cycle * few, length)
 

time: 219 us -> 163 us (0.74)
  waiting for transfers between devices: 96.1 us -> 56.8 us
  Pallas kernels: 11 us -> 41.8 us
  local copies, waits for them, and re-layouts: 34.1 us -> 14.7 us
  matrix products: 18.1 us -> 0 us
  starting transfers between devices: 41.5 us -> 33.6 us
    ppermute x10 -> x12, waiting for transfers between devices: 39.2 us -> 2.62 us  [swap(): lax.ppermute(x, axis, [(i, i ^ bit) for i in range(lax.axis_size(axis))])]
    pallas_call x0 -> x4, Pallas kernels: none -> 32.1 us  [the longest x3 27.6 us: project(): pl.pallas_call(functools.partial(project_kernel, plan, range(first, last)...]
    dot_general x8 -> x0, matrix products: 18.1 us -> none  [project(): part = jnp.einsum('td,dc->ct', these, piece, preferred_element_type=F32)]
    slice x7 -> x8, local copies, waits for them, and re-layouts: 15 us -> 2.84 us  [spread(): to_near, to_far = (far[skip:skip + half], near[skip + half:])]
    ppermute x12 -> x11, starting transfers between devices: 27 us -> 16.9 us  [move_chips(): lax.ppermute(x, 'chan', [(2 * a + k, 2 * b + k) for a, b in pairs for k i...]
    dynamic_update_slice x9 -> x0, local copies, waits for them, and re-layouts: 7.38 us -> none  [gather_context(): whole = lax.dynamic_update_slice(whole, piece, (0, row, 0))]
    unnamed x30 -> x54, local copies, waits for them, and re-layouts: 3.56 us -> 10.3 us
    ppermute x12 -> x11, waiting for transfers between devices: 49.4 us -> 45 us  [move_chips(): lax.ppermute(x, 'chan', [(2 * a + k, 2 * b + k) for a, b in pairs for k i...]
  transfers between devices with their start and end apart: 23 -> 24, of which waited for: 9 -> 8; matrix products, arithmetic and copies ran while one was open for 25% -> 2% of each run, Pallas kernels for 4% -> 19%
where the time goes in v2:
time: 163 us
  waiting for transfers between devices  56.8 us (35%)
  Pallas kernels  41.8 us (26%)
  starting transfers between devices  33.6 us (21%)
  local copies, waits for them, and re-layouts  14.7 us (9%)
  blocking collectives  11.4 us (7%)
  other arithmetic  3.93 us (2%)
    ppermute x11, waiting for transfers between devices, move_chips(): lax.ppermute(x, 'chan', [(2 * a + k, 2 * b + k) for a, b in pairs for k i...  45 us
    pallas_call x3, Pallas kernels, project(): pl.pallas_call(functools.partial(project_kernel, plan, range(first, last)...  27.6 us
    ppermute x11, starting transfers between devices, move_chips(): lax.ppermute(x, 'chan', [(2 * a + k, 2 * b + k) for a, b in pairs for k i...  16.9 us
    ppermute x12, starting transfers between devices, swap(): lax.ppermute(x, axis, [(i, i ^ bit) for i in range(lax.axis_size(axis))])  13.1 us
    all_to_all x1, blocking collectives, body(): lax.all_to_all(gated, 'ctx', split_axis=0, concat_axis=0, tiled=True)  11.4 us
    unnamed x54, local copies, waits for them, and re-layouts  10.3 us
    all_to_all x1, waiting for transfers between devices, move_filter(): lax.all_to_all(values.reshape(cycle, few, length), 'ctx', split_axis=0, c...  9.22 us
    pallas_call x1, Pallas kernels, convolve(): pl.pallas_call(conv_kernel, grid=(rows // step,), in_specs=[pl.BlockSpec(...  6.14 us
  transfers between devices with their start and end apart: 24, of which 8 were waited for; matrix products, arithmetic and copies ran while one was open for 2% of the time, Pallas kernels for 19%

profile of v2, /device:TPU:0, one launch (start us, length us, event | category | flops | bytes accessed | tf_op | source)
XLA Modules:
  0.0 162.6 jit_solution(12116908692880969427)
XLA Ops:
  0.0 3.0 %collective-permute-start = (bf16[512,512]{1,0:T(8,128)(2,1)}, bf16[512,512]{1,0:T(8,128)(2,1)S(1)}, u32[]{:S(2)}, u32[]{:S(2)}) collective-permute-start(bf16[512,512]{1,0:T(8,128)(2,1)} %refs_4_.3), channel_id=1, source_target_pairs={{0,2},{1,3},{2,0},{3,1},{4,6},{5,7},{6,4},{7,5},{8,10},{9,11},{10,... | collective-permute-start | bytes 1572872 | tf_op jit(solution)/shard_map/ppermute | solution.py:221
  3.7 1.6 collective-permute-start.2
  6.9 4.6 %copy-done.1 = bf16[3,512,4096]{2,1,0:T(8,128)(2,1)S(1)} copy-done((bf16[3,512,4096]{2,1,0:T(8,128)(2,1)S(1)}, bf16[3,512,4096]{2,1,0:T(8,128)(2,1)}, u32[]{:S(2)}) %copy-start.1) | copy-done | bytes 12582936
  11.5 4.5 %pick_columns.1 = (bf16[512,512]{1,0:T(8,128)(2,1)S(1)}, bf16[512,512]{1,0:T(8,128)(2,1)}, bf16[512,512]{1,0:T(8,128)(2,1)}, bf16[512,512]{1,0:T(8,128)(2,1)S(1)...) custom-call(s32[8]{0:T(128)S(1)} %stack.77.at_ref, ...), custom_call_target="tpu_custom_call" | custom-call | tf_op jit(solution)/shard_map/pick_columns/pallas_call | solution.py:199
  24.8 14.8 %collective-permute-done.5 = bf16[512,512]{1,0:T(8,128)(2,1)S(1)} collective-permute-done((bf16[512,512]{1,0:T(8,128)(2,1)}, bf16[512,512]{1,0:T(8,128)(2,1)S(1)}, u32[]{:S(2)}, u32[]{:S(2)}) %collective-permute-start.5) | collective-permute-done | bytes 524320 | tf_op jit(solution)/shard_map/ppermute | solution.py:221
  44.8 2.4 %collective-permute-start.11 = (bf16[512,512]{1,0:T(8,128)(2,1)S(1)}, bf16[512,512]{1,0:T(8,128)(2,1)S(1)}, u32[]{:S(2)}, u32[]{:S(2)}) collective-permute-start(bf16[512,512]{1,0:T(8,128)(2,1)S(1)} %get-tuple-element.93), channel_id=1, source_target_pairs={{0,6},{1,7},{2,4},{3,5},{4,2},{5,3},{6,0},{7,1},{8,14},{9,15},{10,... | collective-permute-start | bytes 1572872 | tf_op jit(solution)/shard_map/ppermute | solution.py:221
  48.4 3.5 %all-to-all-start = ((bf16[4,128,512]{2,1,0:T(8,128)(2,1)}), bf16[4,128,512]{2,1,0:T(8,128)(2,1)S(1)}, u32[]{:S(2)}, u32[]{:S(2)}) async-start(bf16[4,128,512]{2,1,0:T(8,128)(2,1)} %bitcast.22), calls=%async_computation | async-start | bytes 1048576 | tf_op jit(solution)/shard_map/all_to_all | solution.py:427
  51.9 5.0 %collective-permute-done.11.refs_3_ = bf16[512,512]{1,0:T(8,128)(2,1)S(1)} collective-permute-done((bf16[512,512]{1,0:T(8,128)(2,1)S(1)}, bf16[512,512]{1,0:T(8,128)(2,1)S(1)}, u32[]{:S(2)}, u32[]{:S(2)}) %collective-permute-start.11) | collective-permute-done | bytes 524320 | tf_op jit(solution)/shard_map/ppermute | solution.py:221
  56.9 9.2 %all-to-all-done.taps_ref = bf16[4,128,512]{2,1,0:T(8,128)(2,1)S(1)} async-done(((bf16[4,128,512]{2,1,0:T(8,128)(2,1)}), bf16[4,128,512]{2,1,0:T(8,128)(2,1)S(1)}, u32[]{:S(2)}, u32[]{:S(2)}) %all-to-all-start) | async-done | bytes 524320 | tf_op jit(solution)/shard_map/all_to_all | solution.py:427
  66.1 1.9 %collective-permute-done.8 = bf16[512,512]{1,0:T(8,128)(2,1)S(1)} collective-permute-done((bf16[512,512]{1,0:T(8,128)(2,1)}, bf16[512,512]{1,0:T(8,128)(2,1)S(1)}, u32[]{:S(2)}, u32[]{:S(2)}) %collective-permute-start.8) | collective-permute-done | bytes 524320 | tf_op jit(solution)/shard_map/ppermute | solution.py:221
  70.7 1.5 collective-permute-start.13
  72.2 1.9 %collective-permute-start.14 = (bf16[512,512]{1,0:T(8,128)(2,1)}, bf16[512,512]{1,0:T(8,128)(2,1)S(1)}, u32[]{:S(2)}, u32[]{:S(2)}) collective-permute-start(bf16[512,512]{1,0:T(8,128)(2,1)} %get-tuple-element.96), channel_id=1, source_target_pairs={{0,4},{1,5},{2,6},{3,7},{4,0},{5,1},{6,2},{7,3},{8,12},{9,13},{10,... | collective-permute-start | bytes 1572872 | tf_op jit(solution)/shard_map/ppermute | solution.py:221
  74.7 1.9 %collective-permute-start.18 = (bf16[512,256]{1,0:T(8,128)(2,1)}, bf16[512,256]{1,0:T(8,128)(2,1)}, u32[]{:S(2)}, u32[]{:S(2)}) collective-permute-start(bf16[512,256]{1,0:T(8,128)(2,1)} %get-tuple-element.110), channel_id=1, source_target_pairs={{0,6},{1,7},{2,4},{3,5},{4,2},{5,3},{6,0},{7,1},{8,14},{9,15},{10,... | collective-permute-start | bytes 786440 | tf_op jit(solution)/shard_map/ppermute | solution.py:221
  77.7 1.7 %filter_waves.1.waves_ref = f32[4,128,1024]{2,1,0:T(8,128)S(1)} custom-call(bf16[4,128,512]{2,1,0:T(8,128)(2,1)S(1)} %copy-done.8, bf16[512,1024]{1,0:T(8,128)(2,1)S(1)} %copy-done.2, bf16[512,1024]{1,0:T(8,128)(2,1)S(1)} %copy-done.3), custom_call_target="tpu_custom_call" | custom-call | tf_op jit(solution)/shard_map/filter_waves/pallas_call | solution.py:53
  79.4 22.8 %collective-permute-done.14.refs_2_ = bf16[512,512]{1,0:T(8,128)(2,1)S(1)} collective-permute-done((bf16[512,512]{1,0:T(8,128)(2,1)}, bf16[512,512]{1,0:T(8,128)(2,1)S(1)}, u32[]{:S(2)}, u32[]{:S(2)}) %collective-permute-start.14) | collective-permute-done | bytes 524320 | tf_op jit(solution)/shard_map/ppermute | solution.py:221
  102.3 2.4 %collective-permute-start.17 = (bf16[512,256]{1,0:T(8,128)(2,1)S(1)}, bf16[512,256]{1,0:T(8,128)(2,1)}, u32[]{:S(2)}, u32[]{:S(2)}) collective-permute-start(bf16[512,256]{1,0:T(8,128)(2,1)S(1)} %get-tuple-element.121), channel_id=1, source_target_pairs={{0,4},{1,5},{2,6},{3,7},{4,0},{5,1},{6,2},{7,3},{8,12},{9,13},{10,... | collective-permute-start | bytes 786440 | tf_op jit(solution)/shard_map/ppermute | solution.py:221
  107.3 1.9 %collective-permute-start.20 = (bf16[256,512]{1,0:T(8,128)(2,1)}, bf16[256,512]{1,0:T(8,128)(2,1)}, u32[]{:S(2)}, u32[]{:S(2)}) collective-permute-start(bf16[256,512]{1,0:T(8,128)(2,1)} %slice.31), channel_id=1, source_target_pairs={{0,16},{8,24},{16,0},{24,8},{1,17},{9,25},{17,1},{25,9},{2,18},{10... | collective-permute-start | bytes 786440 | tf_op jit(solution)/shard_map/ppermute | solution.py:165
  109.9 10.2 %project.3 = (f32[256,2048]{1,0:T(8,128)}, f32[256,2048]{1,0:T(8,128)}) custom-call(s32[8]{0:T(128)} %stack.68.at_ref, bf16[512,512]{1,0:T(8,128)(2,1)} %copy-done.6, bf16[512,512]{1,0:T(8,128)(2,1)} %copy-done.23, bf16[512,512]{1,0:T(8,128)(2,1)} %copy-done.22, bf16[512,512]{1,0:T(8,128)(2,1)} %copy-done.21, bf16[512,512]{1,0:T(8,128)(2,1)} %refs_4_.3, ...), custom_call_target="tpu_custom_call" | custom-call | tf_op jit(solution)/shard_map/project/pallas_call | solution.py:392
  120.5 8.4 %project.5 = (f32[256,2048]{1,0:T(8,128)}, f32[256,2048]{1,0:T(8,128)}) custom-call(s32[8]{0:T(128)} %stack.68.at_ref, bf16[512,512]{1,0:T(8,128)(2,1)} %copy-done.6, bf16[512,512]{1,0:T(8,128)(2,1)} %copy-done.23, bf16[512,512]{1,0:T(8,128)(2,1)} %copy-done.22, bf16[512,512]{1,0:T(8,128)(2,1)} %copy-done.21, bf16[512,512]{1,0:T(8,128)(2,1)} %copy-done.14, ...), custom_call_target="tpu_custom_call" | custom-call | tf_op jit(solution)/shard_map/project/pallas_call | solution.py:392
  129.0 9.0 %project.4 = (f32[128,2048]{1,0:T(8,128)}, f32[128,2048]{1,0:T(8,128)}) custom-call(s32[8]{0:T(128)} %stack.68.at_ref, bf16[512,256]{1,0:T(8,128)(2,1)} %copy-done.10, bf16[512,256]{1,0:T(8,128)(2,1)} %collective-permute-done.16.refs_1_, bf16[512,256]{1,0:T(8,128)(2,1)} %collective-permute-done.17.refs_2_, bf16[512,256]{1,0:T(8,128)(2,1)} %collective-permute-done.18.refs_3_, ...), custom_call_target="tpu_custom_call" | custom-call | tf_op jit(solution)/shard_map/project/pallas_call | solution.py:392
  140.8 1.6 copy-done.5
  142.4 6.1 %convolve.1.answer_ref = f32[128,2048]{1,0:T(8,128)S(1)} custom-call(f32[2,128,2048]{2,1,0:T(8,128)S(1)} %bitcast.20, f32[2,128,2048]{2,1,0:T(8,128)} %bitcast.16.other_ref, f32[3,128,3]{2,1,0:T(8,128)S(1)} %copy.10.taps_ref, f32[128,1]{1,0:T(8,128)S(1)} %copy.9.skip_ref, f32[4,128,1024]{2,1,0:T(8,128)S(1)} %filter_waves.1.waves_ref, ...), custom_call_target="tpu_custom_call" | custom-call | tf_op jit(solution)/shard_map/convolve/pallas_call | solution.py:119
  148.6 1.9 %gate.1 = bf16[4,128,512]{2,1,0:T(8,128)(2,1)S(1)} custom-call(f32[128,2048]{1,0:T(8,128)S(1)} %copy-done.9, f32[128,2048]{1,0:T(8,128)} %collective-permute-done.21.other_ref, f32[3,128,3]{2,1,0:T(8,128)S(1)} %copy.10.taps_ref, f32[128,2048]{1,0:T(8,128)S(1)} %convolve.1.answer_ref), custom_call_target="tpu_custom_call" | custom-call | tf_op jit(solution)/shard_map/gate/pallas_call | solution.py:148
  150.4 11.4 %all_to_all.10 = bf16[4,128,512]{2,1,0:T(8,128)(2,1)S(1)} all-to-all(bf16[4,128,512]{2,1,0:T(8,128)(2,1)S(1)} %gate.1), channel_id=1, replica_groups=mesh['ctx'=4,'chan'=8] {'ctx'}, dimensions={0} | all-to-all | bytes 1048576 | tf_op jit(solution)/shard_map/all_to_all | solution.py:450
  (104 shorter events, 29.1 us)
Async XLA Ops:
  0.0 16.0 %collective-permute-start = (bf16[512,512]{1,0:T(8,128)(2,1)}, bf16[512,512]{1,0:T(8,128)(2,1)S(1)}, u32[]{:S(2)}, u32[]{:S(2)}) collective-permute-start(bf16[512,512]{1,0:T(8,128)(2,1)} %refs_4_.3), channel_id=1, source_target_pairs={{0,2},{1,3},{2,0},{3,1},{4,6},{5,7},{6,4},{7,5},{8,10},{9,11},{10,... | collective-permute-start | bytes 1572872 | tf_op jit(solution)/shard_map/ppermute | solution.py:221
  3.0 12.9 %collective-permute-start.1 = (bf16[512,512]{1,0:T(8,128)(2,1)}, bf16[512,512]{1,0:T(8,128)(2,1)S(1)}, u32[]{:S(2)}, u32[]{:S(2)}) collective-permute-start(bf16[512,512]{1,0:T(8,128)(2,1)} %refs_4_.3), channel_id=1, source_target_pairs={{2,4},{3,5},{4,2},{5,3},{10,12},{11,13},{12,10},{13,11},{18,20},{1... | collective-permute-start | bytes 1572872 | tf_op jit(solution)/shard_map/ppermute | solution.py:221
  3.7 13.7 %collective-permute-start.2 = (bf16[512,512]{1,0:T(8,128)(2,1)}, bf16[512,512]{1,0:T(8,128)(2,1)S(1)}, u32[]{:S(2)}, u32[]{:S(2)}) collective-permute-start(bf16[512,512]{1,0:T(8,128)(2,1)} %refs_4_.3), channel_id=1, source_target_pairs={{0,8},{8,0},{16,24},{24,16},{1,9},{9,1},{17,25},{25,17},{2,10},{10... | collective-permute-start | bytes 1572872 | tf_op jit(solution)/shard_map/ppermute | solution.py:165
  5.3 13.3 %collective-permute-start.3 = (bf16[512,512]{1,0:T(8,128)(2,1)}, bf16[512,512]{1,0:T(8,128)(2,1)S(1)}, u32[]{:S(2)}, u32[]{:S(2)}) collective-permute-start(bf16[512,512]{1,0:T(8,128)(2,1)} %refs_4_.3), channel_id=1, source_target_pairs={{0,16},{8,24},{16,0},{24,8},{1,17},{9,25},{17,1},{25,9},{2,18},{10... | collective-permute-start | bytes 1572872 | tf_op jit(solution)/shard_map/ppermute | solution.py:165
  19.9 19.7 %collective-permute-start.6 = (bf16[768,512]{1,0:T(8,128)(2,1)}, bf16[768,512]{1,0:T(8,128)(2,1)S(1)}, u32[]{:S(2)}, u32[]{:S(2)}) collective-permute-start(bf16[768,512]{1,0:T(8,128)(2,1)} %get-tuple-element.138), channel_id=1, source_target_pairs={{0,8},{8,0},{16,24},{24,16},{1,9},{9,1},{17,25},{25,17},{2,10},{10... | collective-permute-start | bytes 2359304 | tf_op jit(solution)/shard_map/ppermute | solution.py:165
  20.6 19.1 %collective-permute-start.7 = (bf16[768,512]{1,0:T(8,128)(2,1)}, bf16[768,512]{1,0:T(8,128)(2,1)S(1)}, u32[]{:S(2)}, u32[]{:S(2)}) collective-permute-start(bf16[768,512]{1,0:T(8,128)(2,1)} %get-tuple-element.137), channel_id=1, source_target_pairs={{0,16},{8,24},{16,0},{24,8},{1,17},{9,25},{17,1},{25,9},{2,18},{10... | collective-permute-start | bytes 2359304 | tf_op jit(solution)/shard_map/ppermute | solution.py:165
  22.1 2.7 %collective-permute-start.4 = (bf16[512,512]{1,0:T(8,128)(2,1)S(1)}, bf16[512,512]{1,0:T(8,128)(2,1)}, u32[]{:S(2)}, u32[]{:S(2)}) collective-permute-start(bf16[512,512]{1,0:T(8,128)(2,1)S(1)} %collective-permute-done.refs_9_), channel_id=1, source_target_pairs={{2,4},{3,5},{4,2},{5,3},{10,12},{11,13},{12,10},{13,11},{18,20},{1... | collective-permute-start | bytes 1572872 | tf_op jit(solution)/shard_map/ppermute | solution.py:221
  23.5 16.1 %collective-permute-start.5 = (bf16[512,512]{1,0:T(8,128)(2,1)}, bf16[512,512]{1,0:T(8,128)(2,1)S(1)}, u32[]{:S(2)}, u32[]{:S(2)}) collective-permute-start(bf16[512,512]{1,0:T(8,128)(2,1)} %copy-done.24), channel_id=1, source_target_pairs={{2,0},{3,1},{4,6},{5,7},{10,8},{11,9},{12,14},{13,15},{18,16},{19,... | collective-permute-start | bytes 1572872 | tf_op jit(solution)/shard_map/ppermute | solution.py:221
  43.0 25.0 %collective-permute-start.9 = (bf16[768,512]{1,0:T(8,128)(2,1)}, bf16[768,512]{1,0:T(8,128)(2,1)S(1)}, u32[]{:S(2)}, u32[]{:S(2)}) collective-permute-start(bf16[768,512]{1,0:T(8,128)(2,1)} %get-tuple-element.136), channel_id=1, source_target_pairs={{0,8},{8,0},{16,24},{24,16},{1,9},{9,1},{17,25},{25,17},{2,10},{10... | collective-permute-start | bytes 2359304 | tf_op jit(solution)/shard_map/ppermute | solution.py:165
  44.3 23.8 %collective-permute-start.10 = (bf16[768,512]{1,0:T(8,128)(2,1)}, bf16[768,512]{1,0:T(8,128)(2,1)}, u32[]{:S(2)}, u32[]{:S(2)}) collective-permute-start(bf16[768,512]{1,0:T(8,128)(2,1)} %get-tuple-element.135), channel_id=1, source_target_pairs={{0,16},{8,24},{16,0},{24,8},{1,17},{9,25},{17,1},{25,9},{2,18},{10... | collective-permute-start | bytes 2359304 | tf_op jit(solution)/shard_map/ppermute | solution.py:165
  44.8 12.1 %collective-permute-start.11 = (bf16[512,512]{1,0:T(8,128)(2,1)S(1)}, bf16[512,512]{1,0:T(8,128)(2,1)S(1)}, u32[]{:S(2)}, u32[]{:S(2)}) collective-permute-start(bf16[512,512]{1,0:T(8,128)(2,1)S(1)} %get-tuple-element.93), channel_id=1, source_target_pairs={{0,6},{1,7},{2,4},{3,5},{4,2},{5,3},{6,0},{7,1},{8,14},{9,15},{10,... | collective-permute-start | bytes 1572872 | tf_op jit(solution)/shard_map/ppermute | solution.py:221
  47.1 20.9 %collective-permute-start.8 = (bf16[512,512]{1,0:T(8,128)(2,1)}, bf16[512,512]{1,0:T(8,128)(2,1)S(1)}, u32[]{:S(2)}, u32[]{:S(2)}) collective-permute-start(bf16[512,512]{1,0:T(8,128)(2,1)} %collective-permute-done.4), channel_id=1, source_target_pairs={{2,0},{3,1},{4,6},{5,7},{10,8},{11,9},{12,14},{13,15},{18,16},{19,... | collective-permute-start | bytes 1572872 | tf_op jit(solution)/shard_map/ppermute | solution.py:221
  48.4 17.7 %all-to-all-start = ((bf16[4,128,512]{2,1,0:T(8,128)(2,1)}), bf16[4,128,512]{2,1,0:T(8,128)(2,1)S(1)}, u32[]{:S(2)}, u32[]{:S(2)}) async-start(bf16[4,128,512]{2,1,0:T(8,128)(2,1)} %bitcast.22), calls=%async_computation | async-start | bytes 1048576 | tf_op jit(solution)/shard_map/all_to_all | solution.py:427
  69.7 32.5 %collective-permute-start.12 = (bf16[768,512]{1,0:T(8,128)(2,1)S(1)}, bf16[768,512]{1,0:T(8,128)(2,1)S(1)}, u32[]{:S(2)}, u32[]{:S(2)}) collective-permute-start(bf16[768,512]{1,0:T(8,128)(2,1)S(1)} %get-tuple-element.134), channel_id=1, source_target_pairs={{0,8},{8,0},{16,24},{24,16},{1,9},{9,1},{17,25},{25,17},{2,10},{10... | collective-permute-start | bytes 2359304 | tf_op jit(solution)/shard_map/ppermute | solution.py:165
  70.7 31.5 %collective-permute-start.13 = (bf16[768,512]{1,0:T(8,128)(2,1)S(1)}, bf16[768,512]{1,0:T(8,128)(2,1)S(1)}, u32[]{:S(2)}, u32[]{:S(2)}) collective-permute-start(bf16[768,512]{1,0:T(8,128)(2,1)S(1)} %get-tuple-element.133), channel_id=1, source_target_pairs={{0,16},{8,24},{16,0},{24,8},{1,17},{9,25},{17,1},{25,9},{2,18},{10... | collective-permute-start | bytes 2359304 | tf_op jit(solution)/shard_map/ppermute | solution.py:165
  72.2 29.9 %collective-permute-start.14 = (bf16[512,512]{1,0:T(8,128)(2,1)}, bf16[512,512]{1,0:T(8,128)(2,1)S(1)}, u32[]{:S(2)}, u32[]{:S(2)}) collective-permute-start(bf16[512,512]{1,0:T(8,128)(2,1)} %get-tuple-element.96), channel_id=1, source_target_pairs={{0,4},{1,5},{2,6},{3,7},{4,0},{5,1},{6,2},{7,3},{8,12},{9,13},{10,... | collective-permute-start | bytes 1572872 | tf_op jit(solution)/shard_map/ppermute | solution.py:221
  74.1 28.1 %collective-permute-start.15 = (bf16[512,512]{1,0:T(8,128)(2,1)}, bf16[512,512]{1,0:T(8,128)(2,1)S(1)}, u32[]{:S(2)}, u32[]{:S(2)}) collective-permute-start(bf16[512,512]{1,0:T(8,128)(2,1)} %get-tuple-element.106), channel_id=1, source_target_pairs={{0,2},{1,3},{2,0},{3,1},{4,6},{5,7},{6,4},{7,5},{8,10},{9,11},{10,... | collective-permute-start | bytes 1572872 | tf_op jit(solution)/shard_map/ppermute | solution.py:221
  74.7 45.3 %collective-permute-start.18 = (bf16[512,256]{1,0:T(8,128)(2,1)}, bf16[512,256]{1,0:T(8,128)(2,1)}, u32[]{:S(2)}, u32[]{:S(2)}) collective-permute-start(bf16[512,256]{1,0:T(8,128)(2,1)} %get-tuple-element.110), channel_id=1, source_target_pairs={{0,6},{1,7},{2,4},{3,5},{4,2},{5,3},{6,0},{7,1},{8,14},{9,15},{10,... | collective-permute-start | bytes 786440 | tf_op jit(solution)/shard_map/ppermute | solution.py:221
  102.2 17.8 %collective-permute-start.16 = (bf16[512,256]{1,0:T(8,128)(2,1)}, bf16[512,256]{1,0:T(8,128)(2,1)}, u32[]{:S(2)}, u32[]{:S(2)}) collective-permute-start(bf16[512,256]{1,0:T(8,128)(2,1)} %get-tuple-element.120), channel_id=1, source_target_pairs={{0,2},{1,3},{2,0},{3,1},{4,6},{5,7},{6,4},{7,5},{8,10},{9,11},{10,... | collective-permute-start | bytes 786440 | tf_op jit(solution)/shard_map/ppermute | solution.py:221
  102.3 18.1 %collective-permute-start.17 = (bf16[512,256]{1,0:T(8,128)(2,1)S(1)}, bf16[512,256]{1,0:T(8,128)(2,1)}, u32[]{:S(2)}, u32[]{:S(2)}) collective-permute-start(bf16[512,256]{1,0:T(8,128)(2,1)S(1)} %get-tuple-element.121), channel_id=1, source_target_pairs={{0,4},{1,5},{2,6},{3,7},{4,0},{5,1},{6,2},{7,3},{8,12},{9,13},{10,... | collective-permute-start | bytes 786440 | tf_op jit(solution)/shard_map/ppermute | solution.py:221
  105.5 15.0 %collective-permute-start.19 = (bf16[256,512]{1,0:T(8,128)(2,1)}, bf16[256,512]{1,0:T(8,128)(2,1)}, u32[]{:S(2)}, u32[]{:S(2)}) collective-permute-start(bf16[256,512]{1,0:T(8,128)(2,1)} %slice.30), channel_id=1, source_target_pairs={{0,8},{8,0},{16,24},{24,16},{1,9},{9,1},{17,25},{25,17},{2,10},{10... | collective-permute-start | bytes 786440 | tf_op jit(solution)/shard_map/ppermute | solution.py:165
  107.3 13.2 %collective-permute-start.20 = (bf16[256,512]{1,0:T(8,128)(2,1)}, bf16[256,512]{1,0:T(8,128)(2,1)}, u32[]{:S(2)}, u32[]{:S(2)}) collective-permute-start(bf16[256,512]{1,0:T(8,128)(2,1)} %slice.31), channel_id=1, source_target_pairs={{0,16},{8,24},{16,0},{24,8},{1,17},{9,25},{17,1},{25,9},{2,18},{10... | collective-permute-start | bytes 786440 | tf_op jit(solution)/shard_map/ppermute | solution.py:165
  128.9 10.7 %collective-permute-start.22 = (f32[256,2048]{1,0:T(8,128)}, f32[256,2048]{1,0:T(8,128)}, u32[]{:S(2)}, u32[]{:S(2)}) collective-permute-start(f32[256,2048]{1,0:T(8,128)} %get-tuple-element.131), channel_id=1, source_target_pairs={{0,1},{1,0},{2,3},{3,2},{4,5},{5,4},{6,7},{7,6},{8,9},{9,8},{10,11... | collective-permute-start | bytes 6291464 | tf_op jit(solution)/shard_map/ppermute | solution.py:165
  138.0 10.6 %collective-permute-start.21 = (f32[128,2048]{1,0:T(8,128)}, f32[128,2048]{1,0:T(8,128)}, u32[]{:S(2)}, u32[]{:S(2)}) collective-permute-start(f32[128,2048]{1,0:T(8,128)} %get-tuple-element.127), channel_id=1, source_target_pairs={{0,1},{1,0},{2,3},{3,2},{4,5},{5,4},{6,7},{7,6},{8,9},{9,8},{10,11... | collective-permute-start | bytes 3145736 | tf_op jit(solution)/shard_map/ppermute | solution.py:165
  (26 other events, 244.3 us)

commit v3 on v2

--- a/solution.py
+++ b/solution.py
@@ -66,7 +66,7 @@
 
 
 def feature(own, other, taps):
-    mixed = (own + other).astype(BF16).astype(F32)
+    mixed = (own + other.astype(F32)).astype(BF16).astype(F32)
     lane = lax.broadcasted_iota(jnp.int32, mixed.shape, 1)
     one = jnp.where(lane >= 1, pltpu.roll(mixed, 1, 1), 0.0)
     two = jnp.where(lane >= 2, pltpu.roll(mixed, 2, 1), 0.0)
@@ -130,7 +130,7 @@
         ],
         out_specs=pl.BlockSpec((step, span), lambda g: (g, 0)),
         out_shape=jax.ShapeDtypeStruct((rows, span), F32),
-        compiler_params=pltpu.CompilerParams(vmem_limit_bytes=VMEM_LIMIT),
+        compiler_params=pltpu.CompilerParams(vmem_limit_bytes=PROJECT_LIMIT),
         name="convolve",
     )(own, other, taps, skip, waves, high, low)
 
@@ -207,7 +207,7 @@
         ),
         out_shape=[jax.ShapeDtypeStruct((depth, 4 * few), BF16)] * chips
         + [jax.ShapeDtypeStruct((depth, 2 * few), BF16)] * chips,
-        compiler_params=pltpu.CompilerParams(vmem_limit_bytes=VMEM_LIMIT),
+        compiler_params=pltpu.CompilerParams(vmem_limit_bytes=PROJECT_LIMIT),
         name="pick_columns",
     )(at, in_proj)
     return outs[:chips], outs[chips:]
@@ -225,7 +225,7 @@
     return move_chips(x, [(z, z ^ s) for z in range(lax.axis_size("chan") // 2)])
 
 
-def gather(block, pairs, singles, long_filter, move_filter, make_waves):
+def gather(block, pairs, singles, long_filter, early):
     place = lax.axis_index("chan") // 2
     middle = [(1, 2), (2, 1)]
     ends = [(1, 0), (2, 3)]
@@ -235,25 +235,19 @@
     length = block.shape[0]
     half = length // 2
 
-    def spread(near, far, own):
-        if near is None:
-            return swap_far(own)
-        skip = near.shape[0] - length
-        to_near, to_far = far[skip : skip + half], near[skip + half :]
-        if own is not None:
-            to_near, to_far = jnp.concatenate([to_near, own]), jnp.concatenate([to_far, own])
-        return swap(to_near, "ctx", 1), swap(to_far, "ctx", 2)
+    def spread(to_near, to_far):
+        return swap(jnp.concatenate(to_near), "ctx", 1), swap(jnp.concatenate(to_far), "ctx", 2)
 
     pair = move_chips(block, [(0, 1), (1, 0), (2, 3), (3, 2)])
     across = move_chips(block, middle)
-    near0, far0 = spread(None, None, block)
+    near0, far0 = swap_far(block)
     pair, across, near0, far0, pairs, singles, long_filter = order(
         (pair, across, near0, far0, pairs, singles, long_filter)
     )
 
     farther = move_chips(pair, middle)
     second = move_chips(across, ends)
-    near1, far1 = spread(near0, far0, pair)
+    near1, far1 = swap_far(pair)
     pairs[3] = turn_chips(pairs[3], 3)
     pair_3 = pairs.pop()
     farther, second, near1, far1, pairs, singles, long_filter = order(
@@ -262,23 +256,23 @@
 
     second = jnp.where(inner, across, second)
     third = move_chips(farther, ends)
-    near2, far2 = spread(near1, far1, second)
+    near2, far2 = spread(
+        [far0[:half], far1[:half], second], [near0[half:], near1[half:], second]
+    )
     pair_2 = turn_chips(pairs[2], 2)
-    moved_filter = move_filter(long_filter)
-    third, near2, far2, pair_3, pairs, singles, moved_filter = order(
-        (third, near2, far2, pair_3, pairs, singles, moved_filter)
+    third, near2, far2, pair_3, pairs, singles, long_filter = order(
+        (third, near2, far2, pair_3, pairs, singles, long_filter)
     )
 
     third = jnp.where(inner, farther, third)
-    near3, far3 = spread(near2, far2, third)
+    near3, far3 = spread(
+        [far2[length : length + half], third], [near2[length + half :], third]
+    )
     pair_1 = turn_chips(pairs[1], 1)
     single_3 = turn_chips(singles[3], 3)
-    waves = make_waves(moved_filter)
-    near3, far3, pair_2, pair_1, singles, waves = order(
-        (near3, far3, pair_2, pair_1, singles, waves)
-    )
-
-    near4, far4 = spread(near3, far3, None)
+    near3, far3, singles, long_filter, early = order((near3, far3, singles, long_filter, early))
+
+    near4, far4 = spread([far3[half:length]], [near3[length:]])
     single_1, single_2 = turn_chips(singles[1], 1), turn_chips(singles[2], 2)
     pairs = [pairs[0], pair_1, pair_2, pair_3]
     singles = [singles[0], single_1, single_2, single_3]
@@ -287,26 +281,30 @@
         [near0, near1, near2, near3, near4],
         [far0, far1, far2, far3, far4],
     )
-    return slots, pairs, singles, waves
-
-
-def gather_plain(block, pairs, singles, long_filter, move_filter, make_waves):
+    return slots, pairs, singles, long_filter, early
+
+
+def gather_plain(block, pairs, singles, long_filter, early):
     chips = lax.axis_size("chan") // 2
     slots = [turn_chips(block, s) if s else block for s in range(chips)]
     pairs, singles = (
         [turn_chips(x, s) if s else x for s, x in enumerate(w)] for w in (pairs, singles)
     )
-    return slots, pairs, singles, make_waves(move_filter(long_filter))
-
-
-def project_kernel(plan, which, arrays, adds, at_ref, *refs):
-    weights_refs, refs = refs[:4], refs[4:]
+    return slots, pairs, singles, long_filter, early
+
+
+def project_kernel(plan, which, first, arrays, adds, at_ref, *refs):
+    weights_refs, refs = refs[: len(which)], refs[len(which) :]
     pieces, refs = refs[:arrays], refs[arrays:]
-    sums, (own_ref, other_ref, weights, values, weight_sems, sems) = refs[: 2 * adds], refs[2 * adds :]
+    sums, refs = refs[: 2 * adds], refs[2 * adds :]
+    own_ref, other_ref, weights, turned, values, weight_sems, sems = refs
+    slots = len(plan)
     rows = own_ref.shape[0]
-    length = values.shape[1] // 4
+    length = own_ref.shape[1]
+    step = pl.program_id(0)
     weight_copies = [
-        pltpu.make_async_copy(weights_refs[s], weights.at[s], weight_sems.at[s]) for s in range(4)
+        pltpu.make_async_copy(weights_refs[s], weights.at[s], weight_sems.at[s])
+        for s in range(len(which))
     ]
     copies = [
         [
@@ -315,38 +313,45 @@
                 values.at[s, pl.ds(target, count)],
                 sems.at[5 * s + n],
             )
+            for s in range(slots)
             for n, (array, start, count, target) in enumerate(plan[s])
+            if target // length == q
         ]
-        for s in range(len(plan))
+        for q in range(4)
     ]
-    for copy in weight_copies:
-        copy.start()
-    for slot in copies:
-        for copy in slot:
+
+    @pl.when(step == 0)
+    def _():
+        for copy in weight_copies + copies[0] + copies[1]:
             copy.start()
-    for copy in weight_copies:
-        copy.wait()
-    for s in range(len(plan)):
-        turned = weights[at_ref[4 + which[s]]].T
-        for copy in copies[s]:
+        for copy in weight_copies:
             copy.wait()
-        for q in range(4):
-            part = lax.dot_general(
-                turned,
-                values[s, q * length : (q + 1) * length],
-                (((1,), (1,)), ((), ())),
-                preferred_element_type=F32,
-            )
-            span = pl.ds(pl.multiple_of(at_ref[q], length), length)
-            if s:
-                own_ref[:, span] += part[:rows]
-                other_ref[:, span] += part[rows:]
-            elif adds:
-                own_ref[:, span] = sums[0][:, span] + part[:rows]
-                other_ref[:, span] = sums[1][:, span] + part[rows:]
-            else:
-                own_ref[:, span] = part[:rows]
-                other_ref[:, span] = part[rows:]
+        for s in range(slots):
+            turned[s] = weights[at_ref[4 + s] - first].T
+
+    for q in range(4):
+
+        @pl.when(step == q)
+        def _():
+            for copy in copies[q]:
+                copy.wait()
+            if 0 < q < 3:
+                for copy in copies[q + 1]:
+                    copy.start()
+            total = None
+            for s in range(slots):
+                part = lax.dot_general(
+                    turned[s],
+                    values[s, q * length : (q + 1) * length],
+                    (((1,), (1,)), ((), ())),
+                    preferred_element_type=F32,
+                )
+                total = part if total is None else total + part
+            own, other = total[:rows], total[rows:]
+            if adds:
+                own, other = own + sums[0][...], other + sums[1][...]
+            own_ref[...] = own
+            other_ref[...] = other.astype(other_ref.dtype)
 
 
 def project_plain(slots, weights):
@@ -358,7 +363,7 @@
     return total[:rows], total[rows:]
 
 
-def project(slots, weights, first, last, sums=()):
+def project(slots, weights, first, last, sums=(), send=BF16):
     blocks, near, far = slots
     length, depth = blocks[0].shape
     half = length // 2
@@ -366,7 +371,9 @@
     me = lax.axis_index("ctx")
     place = lax.axis_index("chan") // 2
     swapped = jnp.where((place == 1) | (place == 2), 1, 0)
-    at = jnp.stack([(me ^ q) * length for q in range(4)] + [0 * me, 0 * me + 1, 2 + swapped, 3 - swapped])
+    at = jnp.stack(
+        [me ^ q for q in range(4)] + [0 * me, 0 * me + 1, 2 + swapped, 3 - swapped][first:last]
+    )
     arrays, plan = [], []
 
     def place_of(x):
@@ -377,33 +384,37 @@
         return len(arrays) - 1
 
     for s in range(first, last):
-        skip = half if s else 0
+        skip = (0, 0, length, half)[s]
+        corner, row = ((2, 0), (2, half), (3, 0), (4, 0))[s]
         plan.append(
             (
                 (place_of(blocks[s]), 0, length, 0),
                 (place_of(near[s]), skip, length, length),
                 (place_of(far[s]), skip, length, 2 * length),
-                (place_of(near[s + 1]), 0, half, 3 * length),
-                (place_of(far[s + 1]), 0, half, 3 * length + half),
+                (place_of(near[corner]), row, half, 3 * length),
+                (place_of(far[corner]), row, half, 3 * length + half),
             )
         )
-    out = jax.ShapeDtypeStruct((rows, 4 * length), F32)
-    spec = pl.BlockSpec((rows, 4 * length), lambda g, at: (0, 0))
+    spec = pl.BlockSpec((rows, length), lambda g, at: (0, at[g]))
     return pl.pallas_call(
-        functools.partial(project_kernel, plan, range(first, last), len(arrays), len(sums) // 2),
+        functools.partial(project_kernel, plan, range(len(weights)), first, len(arrays), len(sums) // 2),
         grid_spec=pltpu.PrefetchScalarGridSpec(
             num_scalar_prefetch=1,
-            grid=(1,),
-            in_specs=[pl.BlockSpec(memory_space=pl.ANY)] * (4 + len(arrays)) + [spec] * len(sums),
+            grid=(4,),
+            in_specs=[pl.BlockSpec(memory_space=pl.ANY)] * (len(weights) + len(arrays)) + [spec] * len(sums),
             out_specs=[spec] * 2,
             scratch_shapes=[
-                pltpu.VMEM((4, *weights[0].shape), BF16),
+                pltpu.VMEM((len(weights), *weights[0].shape), BF16),
+                pltpu.VMEM((last - first, 2 * rows, depth), BF16),
                 pltpu.VMEM((last - first, 4 * length, depth), BF16),
-                pltpu.SemaphoreType.DMA((4,)),
+                pltpu.SemaphoreType.DMA((len(weights),)),
                 pltpu.SemaphoreType.DMA((5 * (last - first),)),
             ],
         ),
-        out_shape=[out, out],
+        out_shape=[
+            jax.ShapeDtypeStruct((rows, 4 * length), F32),
+            jax.ShapeDtypeStruct((rows, 4 * length), send),
+        ],
         compiler_params=pltpu.CompilerParams(vmem_limit_bytes=PROJECT_LIMIT),
         name="project",
     )(at.astype(jnp.int32), *weights, *arrays, *sums)
@@ -422,25 +433,20 @@
     high, low = (jnp.asarray(t) for t in wave_tables(length))
     pairs, singles = pick_columns(in_proj, chips, few, place, core, me, cycle)
     fits = cycle == 4 and chips == 4 and length % 512 == 0 and depth % 128 == 0
-
-    def move_filter(values):
-        return lax.all_to_all(
-            values.reshape(cycle, few, length), "ctx", split_axis=0, concat_axis=0, tiled=True
-        )
-
-    def make_waves(moved):
-        return filter_waves(moved, high, low)
-
-    slots, pairs, singles, waves = (gather if fits else gather_plain)(
-        tokens, pairs, singles, long_filter, move_filter, make_waves
-    )
     own_taps = lax.dynamic_slice_in_dim(short_taps, me * few, few, axis=1)
     own_skip = lax.dynamic_slice_in_dim(skip_gain, me * few, few)[:, None]
+    slots, pairs, singles, long_filter, (own_taps, own_skip) = (gather if fits else gather_plain)(
+        tokens, pairs, singles, long_filter, (own_taps, own_skip)
+    )
+    moved_filter = lax.all_to_all(
+        long_filter.reshape(cycle, few, length), "ctx", split_axis=0, concat_axis=0, tiled=True
+    )
     if fits:
-        sums, singles = lax.optimization_barrier((project(slots, pairs, 0, 3), singles))
-        mine, send = project(slots, pairs, 3, 4, sums)
+        mine, send = project(slots, pairs, 0, 4)
+        send, singles, moved_filter = lax.optimization_barrier((send, singles, moved_filter))
     else:
         mine, send = project_plain(slots, pairs)
+    waves = filter_waves(moved_filter, high, low)
     theirs = swap(send, "chan", 1)
     answer = convolve(
         mine.reshape(2, few, span), theirs.reshape(2, few, span), own_taps, own_skip, waves, high, low

time: 163 us -> 153 us (0.939)
  local copies, waits for them, and re-layouts: 14.7 us -> 10.2 us
  Pallas kernels: 41.8 us -> 37.9 us
    ppermute x12, waiting for transfers between devices: 2.62 us -> 21.1 us  [swap(): lax.ppermute(x, axis, [(i, i ^ bit) for i in range(lax.axis_size(axis))])]
    ppermute x11, waiting for transfers between devices: 45 us -> 34.2 us  [move_chips(): lax.ppermute(x, 'chan', [(2 * a + k, 2 * b + k) for a, b in pairs for k i...]
    all_to_all x1, waiting for transfers between devices: 9.22 us -> 0.01 us  [body(): lax.all_to_all(long_filter.reshape(cycle, few, length), 'ctx', split_axis...]
    pallas_call x3 -> x2, Pallas kernels: 27.6 us -> 20 us  [project(): pl.pallas_call(functools.partial(project_kernel, plan, range(len(weights)...]
    unnamed x54 -> x49, local copies, waits for them, and re-layouts: 10.3 us -> 5.14 us
    pallas_call x1, Pallas kernels: 4.49 us -> 7.22 us  [pick_columns(): pl.pallas_call(pick_kernel, grid_spec=pltpu.PrefetchScalarGridSpec(num_sc...]
    pallas_call x1, Pallas kernels: 6.14 us -> 8.14 us  [convolve(): pl.pallas_call(conv_kernel, grid=(rows // step,), in_specs=[pl.BlockSpec(...]
  transfers between devices with their start and end apart: 24 -> 24, of which waited for: 8 -> 10; matrix products, arithmetic and copies ran while one was open for 2% -> 3% of each run, Pallas kernels for 19% -> 24%
where the time goes in v3:
time: 153 us; the launch traced here: 152 us
  waiting for transfers between devices  55.3 us (36%)
  Pallas kernels  37.9 us (25%)
  starting transfers between devices  33.7 us (22%)
  blocking collectives  11.6 us (8%)
  local copies, waits for them, and re-layouts  10.2 us (7%)
  other arithmetic  3.13 us (2%)
    ppermute x11, waiting for transfers between devices, move_chips(): lax.ppermute(x, 'chan', [(2 * a + k, 2 * b + k) for a, b in pairs for k i...  34.2 us
    ppermute x12, waiting for transfers between devices, swap(): lax.ppermute(x, axis, [(i, i ^ bit) for i in range(lax.axis_size(axis))])  21.1 us
    pallas_call x2, Pallas kernels, project(): pl.pallas_call(functools.partial(project_kernel, plan, range(len(weights)...  20 us
    ppermute x11, starting transfers between devices, move_chips(): lax.ppermute(x, 'chan', [(2 * a + k, 2 * b + k) for a, b in pairs for k i...  17.2 us
    ppermute x12, starting transfers between devices, swap(): lax.ppermute(x, axis, [(i, i ^ bit) for i in range(lax.axis_size(axis))])  12.9 us
    all_to_all x1, blocking collectives, body(): lax.all_to_all(gated, 'ctx', split_axis=0, concat_axis=0, tiled=True)  11.6 us
    pallas_call x1, Pallas kernels, convolve(): pl.pallas_call(conv_kernel, grid=(rows // step,), in_specs=[pl.BlockSpec(...  8.14 us
    pallas_call x1, Pallas kernels, pick_columns(): pl.pallas_call(pick_kernel, grid_spec=pltpu.PrefetchScalarGridSpec(num_sc...  7.22 us
  transfers between devices with their start and end apart: 24, of which 10 were waited for; matrix products, arithmetic and copies ran while one was open for 3% of the time, Pallas kernels for 24%

profile of v3, /device:TPU:0, one launch (start us, length us, event | category | flops | bytes accessed | tf_op | source)
XLA Modules:
  0.0 152.2 jit_solution(15034269812322459304)
XLA Ops:
  0.0 3.0 %collective-permute-start = (bf16[512,512]{1,0:T(8,128)(2,1)}, bf16[512,512]{1,0:T(8,128)(2,1)S(1)}, u32[]{:S(2)}, u32[]{:S(2)}) collective-permute-start(bf16[512,512]{1,0:T(8,128)(2,1)} %refs_4_.3), channel_id=1, source_target_pairs={{0,2},{1,3},{2,0},{3,1},{4,6},{5,7},{6,4},{7,5},{8,10},{9,11},{10,... | collective-permute-start | bytes 1572872 | tf_op jit(solution)/shard_map/ppermute | solution.py:221
  3.7 1.6 %collective-permute-start.2 = (bf16[512,512]{1,0:T(8,128)(2,1)}, bf16[512,512]{1,0:T(8,128)(2,1)S(1)}, u32[]{:S(2)}, u32[]{:S(2)}) collective-permute-start(bf16[512,512]{1,0:T(8,128)(2,1)} %refs_4_.3), channel_id=1, source_target_pairs={{0,8},{8,0},{16,24},{24,16},{1,9},{9,1},{17,25},{25,17},{2,10},{10... | collective-permute-start | bytes 1572872 | tf_op jit(solution)/shard_map/ppermute | solution.py:165
  5.3 1.5 collective-permute-start.3
  7.4 7.2 %pick_columns.1 = (bf16[512,512]{1,0:T(8,128)(2,1)}, bf16[512,512]{1,0:T(8,128)(2,1)}, bf16[512,512]{1,0:T(8,128)(2,1)}, bf16[512,512]{1,0:T(8,128)(2,1)}, bf16[...) custom-call(s32[8]{0:T(128)} %stack.70.at_ref, ...), custom_call_target="tpu_custom_call" | custom-call | tf_op jit(solution)/shard_map/pick_columns/pallas_call | solution.py:199
  15.2 2.2 %collective-permute-done.2.refs_5_ = bf16[512,512]{1,0:T(8,128)(2,1)S(1)} collective-permute-done((bf16[512,512]{1,0:T(8,128)(2,1)}, bf16[512,512]{1,0:T(8,128)(2,1)S(1)}, u32[]{:S(2)}, u32[]{:S(2)}) %collective-permute-start.2) | collective-permute-done | bytes 524320 | tf_op jit(solution)/shard_map/ppermute | solution.py:165
  18.6 1.5 collective-permute-start.4
  21.9 1.5 collective-permute-start.7
  23.5 12.9 %collective-permute-done.5 = bf16[512,512]{1,0:T(8,128)(2,1)} collective-permute-done((bf16[512,512]{1,0:T(8,128)(2,1)S(1)}, bf16[512,512]{1,0:T(8,128)(2,1)}, u32[]{:S(2)}, u32[]{:S(2)}) %collective-permute-start.5) | collective-permute-done | bytes 524320 | tf_op jit(solution)/shard_map/ppermute | solution.py:221
  38.8 1.5 collective-permute-start.10
  40.3 2.3 %collective-permute-start.11 = (bf16[512,512]{1,0:T(8,128)(2,1)S(1)}, bf16[512,512]{1,0:T(8,128)(2,1)S(1)}, u32[]{:S(2)}, u32[]{:S(2)}) collective-permute-start(bf16[512,512]{1,0:T(8,128)(2,1)S(1)} %copy-done.23), channel_id=1, source_target_pairs={{0,6},{1,7},{2,4},{3,5},{4,2},{5,3},{6,0},{7,1},{8,14},{9,15},{10,... | collective-permute-start | bytes 1572872 | tf_op jit(solution)/shard_map/ppermute | solution.py:221
  44.0 9.1 %collective-permute-done.11.refs_3_ = bf16[512,512]{1,0:T(8,128)(2,1)S(1)} collective-permute-done((bf16[512,512]{1,0:T(8,128)(2,1)S(1)}, bf16[512,512]{1,0:T(8,128)(2,1)S(1)}, u32[]{:S(2)}, u32[]{:S(2)}) %collective-permute-start.11) | collective-permute-done | bytes 524320 | tf_op jit(solution)/shard_map/ppermute | solution.py:221
  53.1 11.1 %collective-permute-done.8 = bf16[512,512]{1,0:T(8,128)(2,1)S(1)} collective-permute-done((bf16[512,512]{1,0:T(8,128)(2,1)}, bf16[512,512]{1,0:T(8,128)(2,1)S(1)}, u32[]{:S(2)}, u32[]{:S(2)}) %collective-permute-start.8) | collective-permute-done | bytes 524320 | tf_op jit(solution)/shard_map/ppermute | solution.py:221
  64.4 1.5 pad_maximum_fusion.2
  72.2 13.5 %collective-permute-done.14.refs_13_ = bf16[768,512]{1,0:T(8,128)(2,1)S(1)} collective-permute-done((bf16[768,512]{1,0:T(8,128)(2,1)}, bf16[768,512]{1,0:T(8,128)(2,1)S(1)}, u32[]{:S(2)}, u32[]{:S(2)}) %collective-permute-start.14) | collective-permute-done | bytes 786464 | tf_op jit(solution)/shard_map/ppermute | solution.py:165
  86.9 3.7 %all-to-all-start = ((bf16[4,128,512]{2,1,0:T(8,128)(2,1)}), bf16[4,128,512]{2,1,0:T(8,128)(2,1)S(1)}, u32[]{:S(2)}, u32[]{:S(2)}) async-start(bf16[4,128,512]{2,1,0:T(8,128)(2,1)} %bitcast.15), calls=%async_computation | async-start | bytes 1048576 | tf_op jit(solution)/shard_map/all_to_all | solution.py:441
  90.5 2.1 %collective-permute-start.20 = (bf16[512,256]{1,0:T(8,128)(2,1)}, bf16[512,256]{1,0:T(8,128)(2,1)S(1)}, u32[]{:S(2)}, u32[]{:S(2)}) collective-permute-start(bf16[512,256]{1,0:T(8,128)(2,1)} %get-tuple-element.109), channel_id=1, source_target_pairs={{0,6},{1,7},{2,4},{3,5},{4,2},{5,3},{6,0},{7,1},{8,14},{9,15},{10,... | collective-permute-start | bytes 786440 | tf_op jit(solution)/shard_map/ppermute | solution.py:221
  93.4 1.7 %collective-permute-start.16 = (bf16[256,512]{1,0:T(8,128)(2,1)}, bf16[256,512]{1,0:T(8,128)(2,1)S(1)}, u32[]{:S(2)}, u32[]{:S(2)}) collective-permute-start(bf16[256,512]{1,0:T(8,128)(2,1)} %slice.30), channel_id=1, source_target_pairs={{0,8},{8,0},{16,24},{24,16},{1,9},{9,1},{17,25},{25,17},{2,10},{10... | collective-permute-start | bytes 786440 | tf_op jit(solution)/shard_map/ppermute | solution.py:165
  97.4 2.3 %collective-permute-start.19 = (bf16[512,256]{1,0:T(8,128)(2,1)}, bf16[512,256]{1,0:T(8,128)(2,1)}, u32[]{:S(2)}, u32[]{:S(2)}) collective-permute-start(bf16[512,256]{1,0:T(8,128)(2,1)} %get-tuple-element.116), channel_id=1, source_target_pairs={{0,4},{1,5},{2,6},{3,7},{4,0},{5,1},{6,2},{7,3},{8,12},{9,13},{10,... | collective-permute-start | bytes 786440 | tf_op jit(solution)/shard_map/ppermute | solution.py:221
  100.3 3.0 %collective-permute-done.16.refs_16_ = bf16[256,512]{1,0:T(8,128)(2,1)S(1)} collective-permute-done((bf16[256,512]{1,0:T(8,128)(2,1)}, bf16[256,512]{1,0:T(8,128)(2,1)S(1)}, u32[]{:S(2)}, u32[]{:S(2)}) %collective-permute-start.16) | collective-permute-done | bytes 262176 | tf_op jit(solution)/shard_map/ppermute | solution.py:165
  104.7 11.0 %project.2 = (f32[256,2048]{1,0:T(8,128)}, bf16[256,2048]{1,0:T(8,128)(2,1)}) custom-call(s32[8]{0:T(128)} %stack.61.at_ref, bf16[512,512]{1,0:T(8,128)(2,1)} %get-tuple-element.100.refs_0_, bf16[512,512]{1,0:T(8,128)(2,1)} %collective-permute-done.12.refs_1_, bf16[512,512]{1,0:T(8,128)(2,1)} %copy-done.21, bf16[512,512]{1,0:T(8,128)(2,1)} %copy-done.20, ...), custom_call_target="tpu_custom_call" | custom-call | tf_op jit(solution)/shard_map/project/pallas_call | solution.py:399
  116.4 9.1 %project.3 = (f32[128,2048]{1,0:T(8,128)}, bf16[128,2048]{1,0:T(8,128)(2,1)}) custom-call(s32[8]{0:T(128)} %stack.61.at_ref, bf16[512,256]{1,0:T(8,128)(2,1)} %get-tuple-element.118.refs_0_, bf16[512,256]{1,0:T(8,128)(2,1)} %collective-permute-done.18.refs_1_, bf16[512,256]{1,0:T(8,128)(2,1)} %collective-permute-done.19.refs_2_, ...), custom_call_target="tpu_custom_call" | custom-call | tf_op jit(solution)/shard_map/project/pallas_call | solution.py:399
  126.5 1.7 %filter_waves.1.waves_ref = f32[4,128,1024]{2,1,0:T(8,128)S(1)} custom-call(bf16[4,128,512]{2,1,0:T(8,128)(2,1)S(1)} %all-to-all-done.taps_ref, bf16[512,1024]{1,0:T(8,128)(2,1)S(1)} %copy-done.3, bf16[512,1024]{1,0:T(8,128)(2,1)S(1)} %copy-done.4), custom_call_target="tpu_custom_call" | custom-call | tf_op jit(solution)/shard_map/filter_waves/pallas_call | solution.py:53
  129.5 8.1 %convolve.1.answer_ref = f32[128,2048]{1,0:T(8,128)} custom-call(f32[2,128,2048]{2,1,0:T(8,128)} %bitcast.21, bf16[2,128,2048]{2,1,0:T(8,128)(2,1)} %bitcast.17.other_ref, f32[3,128,3]{2,1,0:T(8,128)} %copy.10.taps_ref, f32[128,1]{1,0:T(8,128)} %copy.9.skip_ref, f32[4,128,1024]{2,1,0:T(8,128)} %copy-done.1, bf16[512,1024]{1,0:T(8,128)(2,1)} %constant.56.clone.high_ref, ...), custom_call_target="tpu_custom_call" | custom-call | tf_op jit(solution)/shard_map/convolve/pallas_call | solution.py:119
  139.8 11.6 %all_to_all.10 = bf16[4,128,512]{2,1,0:T(8,128)(2,1)S(1)} all-to-all(bf16[4,128,512]{2,1,0:T(8,128)(2,1)S(1)} %gate.1), channel_id=1, replica_groups=mesh['ctx'=4,'chan'=8] {'ctx'}, dimensions={0} | all-to-all | bytes 1048576 | tf_op jit(solution)/shard_map/all_to_all | solution.py:456
  (98 shorter events, 27.1 us)
Async XLA Ops:
  0.0 15.2 %collective-permute-start = (bf16[512,512]{1,0:T(8,128)(2,1)}, bf16[512,512]{1,0:T(8,128)(2,1)S(1)}, u32[]{:S(2)}, u32[]{:S(2)}) collective-permute-start(bf16[512,512]{1,0:T(8,128)(2,1)} %refs_4_.3), channel_id=1, source_target_pairs={{0,2},{1,3},{2,0},{3,1},{4,6},{5,7},{6,4},{7,5},{8,10},{9,11},{10,... | collective-permute-start | bytes 1572872 | tf_op jit(solution)/shard_map/ppermute | solution.py:221
  3.0 12.1 %collective-permute-start.1 = (bf16[512,512]{1,0:T(8,128)(2,1)}, bf16[512,512]{1,0:T(8,128)(2,1)S(1)}, u32[]{:S(2)}, u32[]{:S(2)}) collective-permute-start(bf16[512,512]{1,0:T(8,128)(2,1)} %refs_4_.3), channel_id=1, source_target_pairs={{2,4},{3,5},{4,2},{5,3},{10,12},{11,13},{12,10},{13,11},{18,20},{1... | collective-permute-start | bytes 1572872 | tf_op jit(solution)/shard_map/ppermute | solution.py:221
  3.7 13.7 %collective-permute-start.2 = (bf16[512,512]{1,0:T(8,128)(2,1)}, bf16[512,512]{1,0:T(8,128)(2,1)S(1)}, u32[]{:S(2)}, u32[]{:S(2)}) collective-permute-start(bf16[512,512]{1,0:T(8,128)(2,1)} %refs_4_.3), channel_id=1, source_target_pairs={{0,8},{8,0},{16,24},{24,16},{1,9},{9,1},{17,25},{25,17},{2,10},{10... | collective-permute-start | bytes 1572872 | tf_op jit(solution)/shard_map/ppermute | solution.py:165
  5.3 13.3 %collective-permute-start.3 = (bf16[512,512]{1,0:T(8,128)(2,1)}, bf16[512,512]{1,0:T(8,128)(2,1)S(1)}, u32[]{:S(2)}, u32[]{:S(2)}) collective-permute-start(bf16[512,512]{1,0:T(8,128)(2,1)} %refs_4_.3), channel_id=1, source_target_pairs={{0,16},{8,24},{16,0},{24,8},{1,17},{9,25},{17,1},{25,9},{2,18},{10... | collective-permute-start | bytes 1572872 | tf_op jit(solution)/shard_map/ppermute | solution.py:165
  18.6 4.9 %collective-permute-start.4 = (bf16[512,512]{1,0:T(8,128)(2,1)S(1)}, bf16[512,512]{1,0:T(8,128)(2,1)}, u32[]{:S(2)}, u32[]{:S(2)}) collective-permute-start(bf16[512,512]{1,0:T(8,128)(2,1)S(1)} %collective-permute-done.refs_9_), channel_id=1, source_target_pairs={{2,4},{3,5},{4,2},{5,3},{10,12},{11,13},{12,10},{13,11},{18,20},{1... | collective-permute-start | bytes 1572872 | tf_op jit(solution)/shard_map/ppermute | solution.py:221
  20.1 16.4 %collective-permute-start.5 = (bf16[512,512]{1,0:T(8,128)(2,1)S(1)}, bf16[512,512]{1,0:T(8,128)(2,1)}, u32[]{:S(2)}, u32[]{:S(2)}) collective-permute-start(bf16[512,512]{1,0:T(8,128)(2,1)S(1)} %collective-permute-done.1), channel_id=1, source_target_pairs={{2,0},{3,1},{4,6},{5,7},{10,8},{11,9},{12,14},{13,15},{18,16},{19,... | collective-permute-start | bytes 1572872 | tf_op jit(solution)/shard_map/ppermute | solution.py:221
  21.3 15.1 %collective-permute-start.6 = (bf16[512,512]{1,0:T(8,128)(2,1)S(1)}, bf16[512,512]{1,0:T(8,128)(2,1)S(1)}, u32[]{:S(2)}, u32[]{:S(2)}) collective-permute-start(bf16[512,512]{1,0:T(8,128)(2,1)S(1)} %collective-permute-done.refs_9_), channel_id=1, source_target_pairs={{0,8},{8,0},{16,24},{24,16},{1,9},{9,1},{17,25},{25,17},{2,10},{10... | collective-permute-start | bytes 1572872 | tf_op jit(solution)/shard_map/ppermute | solution.py:165
  21.9 14.5 %collective-permute-start.7 = (bf16[512,512]{1,0:T(8,128)(2,1)S(1)}, bf16[512,512]{1,0:T(8,128)(2,1)S(1)}, u32[]{:S(2)}, u32[]{:S(2)}) collective-permute-start(bf16[512,512]{1,0:T(8,128)(2,1)S(1)} %collective-permute-done.refs_9_), channel_id=1, source_target_pairs={{0,16},{8,24},{16,0},{24,8},{1,17},{9,25},{17,1},{25,9},{2,18},{10... | collective-permute-start | bytes 1572872 | tf_op jit(solution)/shard_map/ppermute | solution.py:165
  38.2 26.1 %collective-permute-start.9 = (bf16[1024,512]{1,0:T(8,128)(2,1)S(1)}, bf16[1024,512]{1,0:T(8,128)(2,1)S(1)}, u32[]{:S(2)}, u32[]{:S(2)}) collective-permute-start(bf16[1024,512]{1,0:T(8,128)(2,1)S(1)} %get-tuple-element.132), channel_id=1, source_target_pairs={{0,8},{8,0},{16,24},{24,16},{1,9},{9,1},{17,25},{25,17},{2,10},{10... | collective-permute-start | bytes 3145736 | tf_op jit(solution)/shard_map/ppermute | solution.py:165
  38.8 25.4 %collective-permute-start.10 = (bf16[1024,512]{1,0:T(8,128)(2,1)S(1)}, bf16[1024,512]{1,0:T(8,128)(2,1)S(1)}, u32[]{:S(2)}, u32[]{:S(2)}) collective-permute-start(bf16[1024,512]{1,0:T(8,128)(2,1)S(1)} %get-tuple-element.131), channel_id=1, source_target_pairs={{0,16},{8,24},{16,0},{24,8},{1,17},{9,25},{17,1},{25,9},{2,18},{10... | collective-permute-start | bytes 3145736 | tf_op jit(solution)/shard_map/ppermute | solution.py:165
  40.3 12.7 %collective-permute-start.11 = (bf16[512,512]{1,0:T(8,128)(2,1)S(1)}, bf16[512,512]{1,0:T(8,128)(2,1)S(1)}, u32[]{:S(2)}, u32[]{:S(2)}) collective-permute-start(bf16[512,512]{1,0:T(8,128)(2,1)S(1)} %copy-done.23), channel_id=1, source_target_pairs={{0,6},{1,7},{2,4},{3,5},{4,2},{5,3},{6,0},{7,1},{8,14},{9,15},{10,... | collective-permute-start | bytes 1572872 | tf_op jit(solution)/shard_map/ppermute | solution.py:221
  42.7 21.5 %collective-permute-start.8 = (bf16[512,512]{1,0:T(8,128)(2,1)}, bf16[512,512]{1,0:T(8,128)(2,1)S(1)}, u32[]{:S(2)}, u32[]{:S(2)}) collective-permute-start(bf16[512,512]{1,0:T(8,128)(2,1)} %collective-permute-done.4), channel_id=1, source_target_pairs={{2,0},{3,1},{4,6},{5,7},{10,8},{11,9},{12,14},{13,15},{18,16},{19,... | collective-permute-start | bytes 1572872 | tf_op jit(solution)/shard_map/ppermute | solution.py:221
  66.1 19.7 %collective-permute-start.14 = (bf16[768,512]{1,0:T(8,128)(2,1)}, bf16[768,512]{1,0:T(8,128)(2,1)S(1)}, u32[]{:S(2)}, u32[]{:S(2)}) collective-permute-start(bf16[768,512]{1,0:T(8,128)(2,1)} %get-tuple-element.130), channel_id=1, source_target_pairs={{0,8},{8,0},{16,24},{24,16},{1,9},{9,1},{17,25},{25,17},{2,10},{10... | collective-permute-start | bytes 2359304 | tf_op jit(solution)/shard_map/ppermute | solution.py:165
  67.5 19.4 %collective-permute-start.15 = (bf16[768,512]{1,0:T(8,128)(2,1)}, bf16[768,512]{1,0:T(8,128)(2,1)S(1)}, u32[]{:S(2)}, u32[]{:S(2)}) collective-permute-start(bf16[768,512]{1,0:T(8,128)(2,1)} %get-tuple-element.129), channel_id=1, source_target_pairs={{0,16},{8,24},{16,0},{24,8},{1,17},{9,25},{17,1},{25,9},{2,18},{10... | collective-permute-start | bytes 2359304 | tf_op jit(solution)/shard_map/ppermute | solution.py:165
  68.0 29.3 %collective-permute-start.13 = (bf16[512,512]{1,0:T(8,128)(2,1)}, bf16[512,512]{1,0:T(8,128)(2,1)S(1)}, u32[]{:S(2)}, u32[]{:S(2)}) collective-permute-start(bf16[512,512]{1,0:T(8,128)(2,1)} %get-tuple-element.94), channel_id=1, source_target_pairs={{0,4},{1,5},{2,6},{3,7},{4,0},{5,1},{6,2},{7,3},{8,12},{9,13},{10,... | collective-permute-start | bytes 1572872 | tf_op jit(solution)/shard_map/ppermute | solution.py:221
  69.3 28.0 %collective-permute-start.12 = (bf16[512,512]{1,0:T(8,128)(2,1)}, bf16[512,512]{1,0:T(8,128)(2,1)}, u32[]{:S(2)}, u32[]{:S(2)}) collective-permute-start(bf16[512,512]{1,0:T(8,128)(2,1)} %get-tuple-element.101), channel_id=1, source_target_pairs={{0,2},{1,3},{2,0},{3,1},{4,6},{5,7},{6,4},{7,5},{8,10},{9,11},{10,... | collective-permute-start | bytes 1572872 | tf_op jit(solution)/shard_map/ppermute | solution.py:221
  86.9 29.3 %all-to-all-start = ((bf16[4,128,512]{2,1,0:T(8,128)(2,1)}), bf16[4,128,512]{2,1,0:T(8,128)(2,1)S(1)}, u32[]{:S(2)}, u32[]{:S(2)}) async-start(bf16[4,128,512]{2,1,0:T(8,128)(2,1)} %bitcast.15), calls=%async_computation | async-start | bytes 1048576 | tf_op jit(solution)/shard_map/all_to_all | solution.py:441
  90.5 25.1 %collective-permute-start.20 = (bf16[512,256]{1,0:T(8,128)(2,1)}, bf16[512,256]{1,0:T(8,128)(2,1)S(1)}, u32[]{:S(2)}, u32[]{:S(2)}) collective-permute-start(bf16[512,256]{1,0:T(8,128)(2,1)} %get-tuple-element.109), channel_id=1, source_target_pairs={{0,6},{1,7},{2,4},{3,5},{4,2},{5,3},{6,0},{7,1},{8,14},{9,15},{10,... | collective-permute-start | bytes 786440 | tf_op jit(solution)/shard_map/ppermute | solution.py:221
  93.4 9.9 %collective-permute-start.16 = (bf16[256,512]{1,0:T(8,128)(2,1)}, bf16[256,512]{1,0:T(8,128)(2,1)S(1)}, u32[]{:S(2)}, u32[]{:S(2)}) collective-permute-start(bf16[256,512]{1,0:T(8,128)(2,1)} %slice.30), channel_id=1, source_target_pairs={{0,8},{8,0},{16,24},{24,16},{1,9},{9,1},{17,25},{25,17},{2,10},{10... | collective-permute-start | bytes 786440 | tf_op jit(solution)/shard_map/ppermute | solution.py:165
  95.9 7.4 %collective-permute-start.17 = (bf16[256,512]{1,0:T(8,128)(2,1)}, bf16[256,512]{1,0:T(8,128)(2,1)S(1)}, u32[]{:S(2)}, u32[]{:S(2)}) collective-permute-start(bf16[256,512]{1,0:T(8,128)(2,1)} %slice.31), channel_id=1, source_target_pairs={{0,16},{8,24},{16,0},{24,8},{1,17},{9,25},{17,1},{25,9},{2,18},{10... | collective-permute-start | bytes 786440 | tf_op jit(solution)/shard_map/ppermute | solution.py:165
  97.3 18.4 %collective-permute-start.18 = (bf16[512,256]{1,0:T(8,128)(2,1)}, bf16[512,256]{1,0:T(8,128)(2,1)}, u32[]{:S(2)}, u32[]{:S(2)}) collective-permute-start(bf16[512,256]{1,0:T(8,128)(2,1)} %get-tuple-element.115), channel_id=1, source_target_pairs={{0,2},{1,3},{2,0},{3,1},{4,6},{5,7},{6,4},{7,5},{8,10},{9,11},{10,... | collective-permute-start | bytes 786440 | tf_op jit(solution)/shard_map/ppermute | solution.py:221
  97.4 18.8 %collective-permute-start.19 = (bf16[512,256]{1,0:T(8,128)(2,1)}, bf16[512,256]{1,0:T(8,128)(2,1)}, u32[]{:S(2)}, u32[]{:S(2)}) collective-permute-start(bf16[512,256]{1,0:T(8,128)(2,1)} %get-tuple-element.116), channel_id=1, source_target_pairs={{0,4},{1,5},{2,6},{3,7},{4,0},{5,1},{6,2},{7,3},{8,12},{9,13},{10,... | collective-permute-start | bytes 786440 | tf_op jit(solution)/shard_map/ppermute | solution.py:221
  116.2 13.3 %collective-permute-start.22 = (bf16[256,2048]{1,0:T(8,128)(2,1)}, bf16[256,2048]{1,0:T(8,128)(2,1)}, u32[]{:S(2)}, u32[]{:S(2)}) collective-permute-start(bf16[256,2048]{1,0:T(8,128)(2,1)} %get-tuple-element.126), channel_id=1, source_target_pairs={{0,1},{1,0},{2,3},{3,2},{4,5},{5,4},{6,7},{7,6},{8,9},{9,8},{10,11... | collective-permute-start | bytes 3145736 | tf_op jit(solution)/shard_map/ppermute | solution.py:165
  125.4 12.2 %collective-permute-start.21 = (bf16[128,2048]{1,0:T(8,128)(2,1)}, bf16[128,2048]{1,0:T(8,128)(2,1)S(1)}, u32[]{:S(2)}, u32[]{:S(2)}) collective-permute-start(bf16[128,2048]{1,0:T(8,128)(2,1)} %get-tuple-element.123), channel_id=1, source_target_pairs={{0,1},{1,0},{2,3},{3,2},{4,5},{5,4},{6,7},{7,6},{8,9},{9,8},{10,11... | collective-permute-start | bytes 1572872 | tf_op jit(solution)/shard_map/ppermute | solution.py:165
  (24 other events, 286.3 us)

commit v4 on v3

--- a/solution.py
+++ b/solution.py
@@ -31,53 +31,36 @@
     )
 
 
-def filter_kernel(taps_ref, high_ref, low_ref, out_ref):
+def filter_waves(taps_ref, high, low):
     blocks, rows, length = taps_ref.shape
-    values = taps_ref[...].reshape(blocks * rows, length)
-    waves = spectrum(values, high_ref[...], low_ref[...]) * (1.0 / length)
+    waves = spectrum(taps_ref[...].reshape(blocks * rows, length), high, low) * (1.0 / length)
     lane = lax.broadcasted_iota(jnp.int32, (rows, length), 1)
     sign = jnp.where(lane % 2 == 0, 1.0, -1.0)
+    out = []
     for m in range(blocks):
         real = waves[m * rows : (m + 1) * rows, :length]
         imag = waves[m * rows : (m + 1) * rows, length:]
         if m:
             real = real - sign * waves[(m - 1) * rows : m * rows, length:]
             imag = imag + sign * waves[(m - 1) * rows : m * rows, :length]
-        out_ref[m, :, :length] = real
-        out_ref[m, :, length:] = imag
-
-
-def filter_waves(moved_filter, high, low):
-    blocks, rows, length = moved_filter.shape
-    step = min(rows, 64)
-    return pl.pallas_call(
-        filter_kernel,
-        grid=(rows // step,),
-        in_specs=[
-            pl.BlockSpec((blocks, step, length), lambda g: (0, g, 0)),
-            pl.BlockSpec((length, 2 * length), lambda g: (0, 0)),
-            pl.BlockSpec((length, 2 * length), lambda g: (0, 0)),
-        ],
-        out_specs=pl.BlockSpec((blocks, step, 2 * length), lambda g: (0, g, 0)),
-        out_shape=jax.ShapeDtypeStruct((blocks, rows, 2 * length), F32),
-        compiler_params=pltpu.CompilerParams(vmem_limit_bytes=VMEM_LIMIT),
-        name="filter_waves",
-    )(moved_filter, high, low)
-
-
-def feature(own, other, taps):
+        out.append((real, imag))
+    return out
+
+
+def feature(own, other, params, stream):
     mixed = (own + other.astype(F32)).astype(BF16).astype(F32)
     lane = lax.broadcasted_iota(jnp.int32, mixed.shape, 1)
     one = jnp.where(lane >= 1, pltpu.roll(mixed, 1, 1), 0.0)
     two = jnp.where(lane >= 2, pltpu.roll(mixed, 2, 1), 0.0)
-    return taps[:, 0:1] * mixed + taps[:, 1:2] * one + taps[:, 2:3] * two
-
-
-def conv_kernel(own_ref, other_ref, taps_ref, skip_ref, waves_ref, high_ref, low_ref, out_ref):
-    blocks, rows, double = waves_ref.shape
-    length = double // 2
+    taps = [params[:, 3 * stream + n : 3 * stream + n + 1] for n in range(3)]
+    return taps[0] * mixed + taps[1] * one + taps[2] * two
+
+
+def conv_kernel(own_ref, other_ref, params_ref, filter_ref, high_ref, low_ref, out_ref):
+    blocks, rows, length = filter_ref.shape
+    params = params_ref[...]
     product = (
-        feature(own_ref[0], other_ref[0], taps_ref[1]) * feature(own_ref[1], other_ref[1], taps_ref[2])
+        feature(own_ref[0], other_ref[0], params, 1) * feature(own_ref[1], other_ref[1], params, 2)
     ).astype(BF16)
     values = jnp.concatenate(
         [product[:, p * length : (p + 1) * length] for p in range(blocks)], axis=0
@@ -85,6 +68,7 @@
     high = high_ref[...]
     low = low_ref[...]
     waves = spectrum(values, high, low)
+    taps = filter_waves(filter_ref, high, low)
     pieces = []
     for p in range(blocks):
         real = jnp.zeros((rows, length), F32)
@@ -92,8 +76,7 @@
         for q in range(p + 1):
             in_real = waves[q * rows : (q + 1) * rows, :length]
             in_imag = waves[q * rows : (q + 1) * rows, length:]
-            tap_real = waves_ref[p - q, :, :length]
-            tap_imag = waves_ref[p - q, :, length:]
+            tap_real, tap_imag = taps[p - q]
             real = real + (in_real * tap_real - in_imag * tap_imag)
             imag = imag + (in_real * tap_imag + in_imag * tap_real)
         pieces.append(jnp.concatenate([real, imag], axis=1))
@@ -106,15 +89,15 @@
         + lax.dot_general(total_low, high, dims, preferred_element_type=F32)
         + lax.dot_general(total_high, low, dims, preferred_element_type=F32)
     )
-    skip = skip_ref[...]
+    skip = params[:, 9:10]
     for p in range(blocks):
         span = slice(p * length, (p + 1) * length)
         out_ref[:, span] = back[p * rows : (p + 1) * rows] + skip * product[:, span].astype(F32)
 
 
-def convolve(own, other, taps, skip, waves, high, low):
+def convolve(own, other, params, moved_filter, high, low):
     streams, rows, span = own.shape
-    blocks, _, double = waves.shape
+    blocks, _, length = moved_filter.shape
     step = min(rows, 64)
     return pl.pallas_call(
         conv_kernel,
@@ -122,27 +105,26 @@
         in_specs=[
             pl.BlockSpec((streams, step, span), lambda g: (0, g, 0)),
             pl.BlockSpec((streams, step, span), lambda g: (0, g, 0)),
-            pl.BlockSpec((3, step, 3), lambda g: (0, g, 0)),
-            pl.BlockSpec((step, 1), lambda g: (g, 0)),
-            pl.BlockSpec((blocks, step, double), lambda g: (0, g, 0)),
-            pl.BlockSpec((double // 2, double), lambda g: (0, 0)),
-            pl.BlockSpec((double // 2, double), lambda g: (0, 0)),
+            pl.BlockSpec((step, 10), lambda g: (g, 0)),
+            pl.BlockSpec((blocks, step, length), lambda g: (0, g, 0)),
+            pl.BlockSpec((length, 2 * length), lambda g: (0, 0)),
+            pl.BlockSpec((length, 2 * length), lambda g: (0, 0)),
         ],
         out_specs=pl.BlockSpec((step, span), lambda g: (g, 0)),
         out_shape=jax.ShapeDtypeStruct((rows, span), F32),
         compiler_params=pltpu.CompilerParams(vmem_limit_bytes=PROJECT_LIMIT),
         name="convolve",
-    )(own, other, taps, skip, waves, high, low)
-
-
-def gate_kernel(own_ref, other_ref, taps_ref, answer_ref, out_ref):
+    )(own, other, params, moved_filter, high, low)
+
+
+def gate_kernel(own_ref, other_ref, params_ref, answer_ref, out_ref):
     blocks, _, length = out_ref.shape
-    gated = (feature(own_ref[...], other_ref[...], taps_ref[0]) * answer_ref[...]).astype(BF16)
+    gated = (feature(own_ref[...], other_ref[...], params_ref[...], 0) * answer_ref[...]).astype(BF16)
     for p in range(blocks):
         out_ref[p] = gated[:, p * length : (p + 1) * length]
 
 
-def gate(own, other, taps, answer, blocks):
+def gate(own, other, params, answer, blocks):
     rows, span = own.shape
     step = min(rows, 64)
     return pl.pallas_call(
@@ -151,14 +133,14 @@
         in_specs=[
             pl.BlockSpec((step, span), lambda g: (g, 0)),
             pl.BlockSpec((step, span), lambda g: (g, 0)),
-            pl.BlockSpec((3, step, 3), lambda g: (0, g, 0)),
+            pl.BlockSpec((step, 10), lambda g: (g, 0)),
             pl.BlockSpec((step, span), lambda g: (g, 0)),
         ],
         out_specs=pl.BlockSpec((blocks, step, span // blocks), lambda g: (0, g, 0)),
         out_shape=jax.ShapeDtypeStruct((blocks, rows, span // blocks), BF16),
         compiler_params=pltpu.CompilerParams(vmem_limit_bytes=VMEM_LIMIT),
         name="gate",
-    )(own, other, taps, answer)
+    )(own, other, params, answer)
 
 
 def swap(x, axis, bit):
@@ -363,17 +345,11 @@
     return total[:rows], total[rows:]
 
 
-def project(slots, weights, first, last, sums=(), send=BF16):
+def project(at, slots, weights, first, last, sums=(), send=F32):
     blocks, near, far = slots
     length, depth = blocks[0].shape
     half = length // 2
     rows = weights[0].shape[1] // 2
-    me = lax.axis_index("ctx")
-    place = lax.axis_index("chan") // 2
-    swapped = jnp.where((place == 1) | (place == 2), 1, 0)
-    at = jnp.stack(
-        [me ^ q for q in range(4)] + [0 * me, 0 * me + 1, 2 + swapped, 3 - swapped][first:last]
-    )
     arrays, plan = [], []
 
     def place_of(x):
@@ -417,7 +393,7 @@
         ],
         compiler_params=pltpu.CompilerParams(vmem_limit_bytes=PROJECT_LIMIT),
         name="project",
-    )(at.astype(jnp.int32), *weights, *arrays, *sums)
+    )(at, *weights, *arrays, *sums)
 
 
 def body(tokens, in_proj, short_taps, long_filter, skip_gain):
@@ -435,24 +411,26 @@
     fits = cycle == 4 and chips == 4 and length % 512 == 0 and depth % 128 == 0
     own_taps = lax.dynamic_slice_in_dim(short_taps, me * few, few, axis=1)
     own_skip = lax.dynamic_slice_in_dim(skip_gain, me * few, few)[:, None]
-    slots, pairs, singles, long_filter, (own_taps, own_skip) = (gather if fits else gather_plain)(
-        tokens, pairs, singles, long_filter, (own_taps, own_skip)
+    params = jnp.concatenate([own_taps[0], own_taps[1], own_taps[2], own_skip], axis=1)
+    swapped = jnp.where((place == 1) | (place == 2), 1, 0)
+    at = jnp.stack([me ^ q for q in range(4)] + [0 * me, 0 * me + 1, 2 + swapped, 3 - swapped])
+    slots, pairs, singles, long_filter, (params, at) = (gather if fits else gather_plain)(
+        tokens, pairs, singles, long_filter, (params, at.astype(jnp.int32))
     )
     moved_filter = lax.all_to_all(
         long_filter.reshape(cycle, few, length), "ctx", split_axis=0, concat_axis=0, tiled=True
     )
     if fits:
-        mine, send = project(slots, pairs, 0, 4)
+        mine, send = project(at, slots, pairs, 0, 4)
         send, singles, moved_filter = lax.optimization_barrier((send, singles, moved_filter))
     else:
         mine, send = project_plain(slots, pairs)
-    waves = filter_waves(moved_filter, high, low)
     theirs = swap(send, "chan", 1)
     answer = convolve(
-        mine.reshape(2, few, span), theirs.reshape(2, few, span), own_taps, own_skip, waves, high, low
-    )
-    mine, send = project(slots, singles, 0, 4) if fits else project_plain(slots, singles)
-    gated = gate(mine, swap(send, "chan", 1), own_taps, answer, cycle)
+        mine.reshape(2, few, span), theirs.reshape(2, few, span), params, moved_filter, high, low
+    )
+    mine, send = project(at, slots, singles, 0, 4) if fits else project_plain(slots, singles)
+    gated = gate(mine, swap(send, "chan", 1), params, answer, cycle)
     moved = lax.all_to_all(gated, "ctx", split_axis=0, concat_axis=0, tiled=True)
     return moved.reshape(cycle * few, length)
 

time: 153 us -> 152 us (level)
  local copies, waits for them, and re-layouts: 10.2 us -> 7.52 us
  waiting for transfers between devices: 55.3 us -> 57.9 us
    ppermute x12, waiting for transfers between devices: 21.1 us -> 23.2 us  [swap(): lax.ppermute(x, axis, [(i, i ^ bit) for i in range(lax.axis_size(axis))])]
    pallas_call x1 -> x0, Pallas kernels: 1.66 us -> none  [filter_waves(): pl.pallas_call(filter_kernel, grid=(rows // step,), in_specs=[pl.BlockSpe...]
  transfers between devices with their start and end apart: 24 -> 24, of which waited for: 10 -> 10; matrix products, arithmetic and copies ran while one was open for 3% -> 2% of each run, Pallas kernels for 24% -> 24%
where the time goes in v4:
time: 152 us; the launch traced here: 151 us
  waiting for transfers between devices  57.9 us (38%)
  Pallas kernels  37.4 us (25%)
  starting transfers between devices  33.9 us (22%)
  blocking collectives  11.4 us (8%)
  local copies, waits for them, and re-layouts  7.52 us (5%)
  other arithmetic  2.89 us (2%)
    ppermute x11, waiting for transfers between devices, move_chips(): lax.ppermute(x, 'chan', [(2 * a + k, 2 * b + k) for a, b in pairs for k i...  34.8 us
    ppermute x12, waiting for transfers between devices, swap(): lax.ppermute(x, axis, [(i, i ^ bit) for i in range(lax.axis_size(axis))])  23.2 us
    pallas_call x2, Pallas kernels, project(): pl.pallas_call(functools.partial(project_kernel, plan, range(len(weights)...  20.2 us
    ppermute x11, starting transfers between devices, move_chips(): lax.ppermute(x, 'chan', [(2 * a + k, 2 * b + k) for a, b in pairs for k i...  17.1 us
    ppermute x12, starting transfers between devices, swap(): lax.ppermute(x, axis, [(i, i ^ bit) for i in range(lax.axis_size(axis))])  13.2 us
    all_to_all x1, blocking collectives, body(): lax.all_to_all(gated, 'ctx', split_axis=0, concat_axis=0, tiled=True)  11.4 us
    pallas_call x1, Pallas kernels, convolve(): pl.pallas_call(conv_kernel, grid=(rows // step,), in_specs=[pl.BlockSpec(...  9.09 us
    pallas_call x1, Pallas kernels, pick_columns(): pl.pallas_call(pick_kernel, grid_spec=pltpu.PrefetchScalarGridSpec(num_sc...  7.24 us
  transfers between devices with their start and end apart: 24, of which 10 were waited for; matrix products, arithmetic and copies ran while one was open for 2% of the time, Pallas kernels for 24%

profile of v4, /device:TPU:0, one launch (start us, length us, event | category | flops | bytes accessed | tf_op | source)
XLA Modules:
  0.0 151.4 jit_solution(509171936491036561)
XLA Ops:
  0.0 3.0 %collective-permute-start = (bf16[512,512]{1,0:T(8,128)(2,1)}, bf16[512,512]{1,0:T(8,128)(2,1)S(1)}, u32[]{:S(2)}, u32[]{:S(2)}) collective-permute-start(bf16[512,512]{1,0:T(8,128)(2,1)} %refs_4_.3), channel_id=1, source_target_pairs={{0,2},{1,3},{2,0},{3,1},{4,6},{5,7},{6,4},{7,5},{8,10},{9,11},{10,... | collective-permute-start | bytes 1572872 | tf_op jit(solution)/shard_map/ppermute | solution.py:203
  3.7 1.6 %collective-permute-start.2 = (bf16[512,512]{1,0:T(8,128)(2,1)}, bf16[512,512]{1,0:T(8,128)(2,1)S(1)}, u32[]{:S(2)}, u32[]{:S(2)}) collective-permute-start(bf16[512,512]{1,0:T(8,128)(2,1)} %refs_4_.3), channel_id=1, source_target_pairs={{0,8},{8,0},{16,24},{24,16},{1,9},{9,1},{17,25},{25,17},{2,10},{10... | collective-permute-start | bytes 1572872 | tf_op jit(solution)/shard_map/ppermute | solution.py:147
  5.3 1.5 %collective-permute-start.3 = (bf16[512,512]{1,0:T(8,128)(2,1)}, bf16[512,512]{1,0:T(8,128)(2,1)S(1)}, u32[]{:S(2)}, u32[]{:S(2)}) collective-permute-start(bf16[512,512]{1,0:T(8,128)(2,1)} %refs_4_.3), channel_id=1, source_target_pairs={{0,16},{8,24},{16,0},{24,8},{1,17},{9,25},{17,1},{25,9},{2,18},{10... | collective-permute-start | bytes 1572872 | tf_op jit(solution)/shard_map/ppermute | solution.py:147
  7.4 7.2 %pick_columns.1 = (bf16[512,512]{1,0:T(8,128)(2,1)}, bf16[512,512]{1,0:T(8,128)(2,1)}, bf16[512,512]{1,0:T(8,128)(2,1)}, bf16[512,512]{1,0:T(8,128)(2,1)}, bf16[...) custom-call(s32[8]{0:T(128)} %stack.56.at_ref, ...), custom_call_target="tpu_custom_call" | custom-call | tf_op jit(solution)/shard_map/pick_columns/pallas_call | solution.py:181
  15.2 2.2 %collective-permute-done.2.refs_5_ = bf16[512,512]{1,0:T(8,128)(2,1)S(1)} collective-permute-done((bf16[512,512]{1,0:T(8,128)(2,1)}, bf16[512,512]{1,0:T(8,128)(2,1)S(1)}, u32[]{:S(2)}, u32[]{:S(2)}) %collective-permute-start.2) | collective-permute-done | bytes 524320 | tf_op jit(solution)/shard_map/ppermute | solution.py:147
  18.6 1.5 collective-permute-start.4
  21.9 1.5 %collective-permute-start.7 = (bf16[512,512]{1,0:T(8,128)(2,1)S(1)}, bf16[512,512]{1,0:T(8,128)(2,1)S(1)}, u32[]{:S(2)}, u32[]{:S(2)}) collective-permute-start(bf16[512,512]{1,0:T(8,128)(2,1)S(1)} %collective-permute-done.refs_9_), channel_id=1, source_target_pairs={{0,16},{8,24},{16,0},{24,8},{1,17},{9,25},{17,1},{25,9},{2,18},{10... | collective-permute-start | bytes 1572872 | tf_op jit(solution)/shard_map/ppermute | solution.py:147
  23.5 12.9 %collective-permute-done.5 = bf16[512,512]{1,0:T(8,128)(2,1)} collective-permute-done((bf16[512,512]{1,0:T(8,128)(2,1)S(1)}, bf16[512,512]{1,0:T(8,128)(2,1)}, u32[]{:S(2)}, u32[]{:S(2)}) %collective-permute-start.5) | collective-permute-done | bytes 524320 | tf_op jit(solution)/shard_map/ppermute | solution.py:203
  36.5 1.4 broadcast_select_fusion.1.refs_12_
  38.8 1.5 %collective-permute-start.10 = (bf16[1024,512]{1,0:T(8,128)(2,1)S(1)}, bf16[1024,512]{1,0:T(8,128)(2,1)S(1)}, u32[]{:S(2)}, u32[]{:S(2)}) collective-permute-start(bf16[1024,512]{1,0:T(8,128)(2,1)S(1)} %get-tuple-element.131), channel_id=1, source_target_pairs={{0,16},{8,24},{16,0},{24,8},{1,17},{9,25},{17,1},{25,9},{2,18},{10... | collective-permute-start | bytes 3145736 | tf_op jit(solution)/shard_map/ppermute | solution.py:147
  40.3 2.3 %collective-permute-start.11 = (bf16[512,512]{1,0:T(8,128)(2,1)S(1)}, bf16[512,512]{1,0:T(8,128)(2,1)S(1)}, u32[]{:S(2)}, u32[]{:S(2)}) collective-permute-start(bf16[512,512]{1,0:T(8,128)(2,1)S(1)} %copy-done.22), channel_id=1, source_target_pairs={{0,6},{1,7},{2,4},{3,5},{4,2},{5,3},{6,0},{7,1},{8,14},{9,15},{10,... | collective-permute-start | bytes 1572872 | tf_op jit(solution)/shard_map/ppermute | solution.py:203
  43.9 9.1 %collective-permute-done.11.refs_3_ = bf16[512,512]{1,0:T(8,128)(2,1)S(1)} collective-permute-done((bf16[512,512]{1,0:T(8,128)(2,1)S(1)}, bf16[512,512]{1,0:T(8,128)(2,1)S(1)}, u32[]{:S(2)}, u32[]{:S(2)}) %collective-permute-start.11) | collective-permute-done | bytes 524320 | tf_op jit(solution)/shard_map/ppermute | solution.py:203
  53.1 11.1 %collective-permute-done.8 = bf16[512,512]{1,0:T(8,128)(2,1)S(1)} collective-permute-done((bf16[512,512]{1,0:T(8,128)(2,1)}, bf16[512,512]{1,0:T(8,128)(2,1)S(1)}, u32[]{:S(2)}, u32[]{:S(2)}) %collective-permute-start.8) | collective-permute-done | bytes 524320 | tf_op jit(solution)/shard_map/ppermute | solution.py:203
  72.0 13.8 %collective-permute-done.12.refs_13_ = bf16[768,512]{1,0:T(8,128)(2,1)S(1)} collective-permute-done((bf16[768,512]{1,0:T(8,128)(2,1)}, bf16[768,512]{1,0:T(8,128)(2,1)S(1)}, u32[]{:S(2)}, u32[]{:S(2)}) %collective-permute-start.12) | collective-permute-done | bytes 786464 | tf_op jit(solution)/shard_map/ppermute | solution.py:147
  86.9 3.7 %all-to-all-start = ((bf16[4,128,512]{2,1,0:T(8,128)(2,1)}), bf16[4,128,512]{2,1,0:T(8,128)(2,1)S(1)}, u32[]{:S(2)}, u32[]{:S(2)}) async-start(bf16[4,128,512]{2,1,0:T(8,128)(2,1)} %bitcast.18), calls=%async_computation | async-start | bytes 1048576 | tf_op jit(solution)/shard_map/all_to_all | solution.py:420
  90.6 1.9 %collective-permute-start.16 = (bf16[256,512]{1,0:T(8,128)(2,1)S(1)}, bf16[256,512]{1,0:T(8,128)(2,1)S(1)}, u32[]{:S(2)}, u32[]{:S(2)}) collective-permute-start(bf16[256,512]{1,0:T(8,128)(2,1)S(1)} %slice.42), channel_id=1, source_target_pairs={{0,8},{8,0},{16,24},{24,16},{1,9},{9,1},{17,25},{25,17},{2,10},{10... | collective-permute-start | bytes 786440 | tf_op jit(solution)/shard_map/ppermute | solution.py:147
  92.5 1.5 %collective-permute-start.17 = (bf16[256,512]{1,0:T(8,128)(2,1)S(1)}, bf16[256,512]{1,0:T(8,128)(2,1)S(1)}, u32[]{:S(2)}, u32[]{:S(2)}) collective-permute-start(bf16[256,512]{1,0:T(8,128)(2,1)S(1)} %slice.43), channel_id=1, source_target_pairs={{0,16},{8,24},{16,0},{24,8},{1,17},{9,25},{17,1},{25,9},{2,18},{10... | collective-permute-start | bytes 786440 | tf_op jit(solution)/shard_map/ppermute | solution.py:147
  94.0 2.1 %collective-permute-start.20 = (bf16[512,256]{1,0:T(8,128)(2,1)}, bf16[512,256]{1,0:T(8,128)(2,1)S(1)}, u32[]{:S(2)}, u32[]{:S(2)}) collective-permute-start(bf16[512,256]{1,0:T(8,128)(2,1)} %get-tuple-element.106), channel_id=1, source_target_pairs={{0,6},{1,7},{2,4},{3,5},{4,2},{5,3},{6,0},{7,1},{8,14},{9,15},{10,... | collective-permute-start | bytes 786440 | tf_op jit(solution)/shard_map/ppermute | solution.py:203
  96.1 2.3 %collective-permute-start.19 = (bf16[512,256]{1,0:T(8,128)(2,1)S(1)}, bf16[512,256]{1,0:T(8,128)(2,1)}, u32[]{:S(2)}, u32[]{:S(2)}) collective-permute-start(bf16[512,256]{1,0:T(8,128)(2,1)S(1)} %copy-done.23), channel_id=1, source_target_pairs={{0,4},{1,5},{2,6},{3,7},{4,0},{5,1},{6,2},{7,3},{8,12},{9,13},{10,... | collective-permute-start | bytes 786440 | tf_op jit(solution)/shard_map/ppermute | solution.py:203
  98.4 4.9 %collective-permute-done.16.refs_16_ = bf16[256,512]{1,0:T(8,128)(2,1)S(1)} collective-permute-done((bf16[256,512]{1,0:T(8,128)(2,1)S(1)}, bf16[256,512]{1,0:T(8,128)(2,1)S(1)}, u32[]{:S(2)}, u32[]{:S(2)}) %collective-permute-start.16) | collective-permute-done | bytes 262176 | tf_op jit(solution)/shard_map/ppermute | solution.py:147
  104.7 11.1 %project.2 = (f32[256,2048]{1,0:T(8,128)}, f32[256,2048]{1,0:T(8,128)}) custom-call(s32[8]{0:T(128)} %stack.63.at_ref, bf16[512,512]{1,0:T(8,128)(2,1)} %get-tuple-element.109.refs_0_, bf16[512,512]{1,0:T(8,128)(2,1)} %collective-permute-done.14.refs_1_, bf16[512,512]{1,0:T(8,128)(2,1)} %copy-done.19, bf16[512,512]{1,0:T(8,128)(2,1)} %copy-done.18, ...), custom_call_target="tpu_custom_call" | custom-call | tf_op jit(solution)/shard_map/project/pallas_call | solution.py:375
  117.6 9.1 %project.3 = (f32[128,2048]{1,0:T(8,128)}, f32[128,2048]{1,0:T(8,128)}) custom-call(s32[8]{0:T(128)} %stack.63.at_ref, bf16[512,256]{1,0:T(8,128)(2,1)} %get-tuple-element.119.refs_0_, bf16[512,256]{1,0:T(8,128)(2,1)} %copy-done.21, bf16[512,256]{1,0:T(8,128)(2,1)} %collective-permute-done.19.refs_2_, bf16[512,256]{1,0:T(8,128)(2,1)} %copy-done.20, ...), custom_call_target="tpu_custom_call" | custom-call | tf_op jit(solution)/shard_map/project/pallas_call | solution.py:375
  128.1 9.1 %convolve.1.answer_ref = f32[128,2048]{1,0:T(8,128)} custom-call(f32[2,128,2048]{2,1,0:T(8,128)} %bitcast.27, f32[2,128,2048]{2,1,0:T(8,128)} %bitcast.20.other_ref, f32[128,10]{1,0:T(8,128)} %copy.11.params_ref, bf16[4,128,512]{2,1,0:T(8,128)(2,1)} %copy-done.15, bf16[512,1024]{1,0:T(8,128)(2,1)} %constant.52.clone.high_ref, ...), custom_call_target="tpu_custom_call" | custom-call | tf_op jit(solution)/shard_map/convolve/pallas_call | solution.py:102
  139.2 11.4 %all_to_all.10 = bf16[4,128,512]{2,1,0:T(8,128)(2,1)S(1)} all-to-all(bf16[4,128,512]{2,1,0:T(8,128)(2,1)S(1)} %gate.1), channel_id=1, replica_groups=mesh['ctx'=4,'chan'=8] {'ctx'}, dimensions={0} | all-to-all | bytes 1048576 | tf_op jit(solution)/shard_map/all_to_all | solution.py:434
  (97 shorter events, 23.3 us)
Async XLA Ops:
  0.0 15.2 %collective-permute-start = (bf16[512,512]{1,0:T(8,128)(2,1)}, bf16[512,512]{1,0:T(8,128)(2,1)S(1)}, u32[]{:S(2)}, u32[]{:S(2)}) collective-permute-start(bf16[512,512]{1,0:T(8,128)(2,1)} %refs_4_.3), channel_id=1, source_target_pairs={{0,2},{1,3},{2,0},{3,1},{4,6},{5,7},{6,4},{7,5},{8,10},{9,11},{10,... | collective-permute-start | bytes 1572872 | tf_op jit(solution)/shard_map/ppermute | solution.py:203
  3.0 12.1 %collective-permute-start.1 = (bf16[512,512]{1,0:T(8,128)(2,1)}, bf16[512,512]{1,0:T(8,128)(2,1)S(1)}, u32[]{:S(2)}, u32[]{:S(2)}) collective-permute-start(bf16[512,512]{1,0:T(8,128)(2,1)} %refs_4_.3), channel_id=1, source_target_pairs={{2,4},{3,5},{4,2},{5,3},{10,12},{11,13},{12,10},{13,11},{18,20},{1... | collective-permute-start | bytes 1572872 | tf_op jit(solution)/shard_map/ppermute | solution.py:203
  3.7 13.7 %collective-permute-start.2 = (bf16[512,512]{1,0:T(8,128)(2,1)}, bf16[512,512]{1,0:T(8,128)(2,1)S(1)}, u32[]{:S(2)}, u32[]{:S(2)}) collective-permute-start(bf16[512,512]{1,0:T(8,128)(2,1)} %refs_4_.3), channel_id=1, source_target_pairs={{0,8},{8,0},{16,24},{24,16},{1,9},{9,1},{17,25},{25,17},{2,10},{10... | collective-permute-start | bytes 1572872 | tf_op jit(solution)/shard_map/ppermute | solution.py:147
  5.3 13.3 %collective-permute-start.3 = (bf16[512,512]{1,0:T(8,128)(2,1)}, bf16[512,512]{1,0:T(8,128)(2,1)S(1)}, u32[]{:S(2)}, u32[]{:S(2)}) collective-permute-start(bf16[512,512]{1,0:T(8,128)(2,1)} %refs_4_.3), channel_id=1, source_target_pairs={{0,16},{8,24},{16,0},{24,8},{1,17},{9,25},{17,1},{25,9},{2,18},{10... | collective-permute-start | bytes 1572872 | tf_op jit(solution)/shard_map/ppermute | solution.py:147
  18.6 4.9 %collective-permute-start.4 = (bf16[512,512]{1,0:T(8,128)(2,1)S(1)}, bf16[512,512]{1,0:T(8,128)(2,1)}, u32[]{:S(2)}, u32[]{:S(2)}) collective-permute-start(bf16[512,512]{1,0:T(8,128)(2,1)S(1)} %collective-permute-done.refs_9_), channel_id=1, source_target_pairs={{2,4},{3,5},{4,2},{5,3},{10,12},{11,13},{12,10},{13,11},{18,20},{1... | collective-permute-start | bytes 1572872 | tf_op jit(solution)/shard_map/ppermute | solution.py:203
  20.1 16.4 %collective-permute-start.5 = (bf16[512,512]{1,0:T(8,128)(2,1)S(1)}, bf16[512,512]{1,0:T(8,128)(2,1)}, u32[]{:S(2)}, u32[]{:S(2)}) collective-permute-start(bf16[512,512]{1,0:T(8,128)(2,1)S(1)} %collective-permute-done.1), channel_id=1, source_target_pairs={{2,0},{3,1},{4,6},{5,7},{10,8},{11,9},{12,14},{13,15},{18,16},{19,... | collective-permute-start | bytes 1572872 | tf_op jit(solution)/shard_map/ppermute | solution.py:203
  21.3 15.1 %collective-permute-start.6 = (bf16[512,512]{1,0:T(8,128)(2,1)S(1)}, bf16[512,512]{1,0:T(8,128)(2,1)S(1)}, u32[]{:S(2)}, u32[]{:S(2)}) collective-permute-start(bf16[512,512]{1,0:T(8,128)(2,1)S(1)} %collective-permute-done.refs_9_), channel_id=1, source_target_pairs={{0,8},{8,0},{16,24},{24,16},{1,9},{9,1},{17,25},{25,17},{2,10},{10... | collective-permute-start | bytes 1572872 | tf_op jit(solution)/shard_map/ppermute | solution.py:147
  21.9 14.5 %collective-permute-start.7 = (bf16[512,512]{1,0:T(8,128)(2,1)S(1)}, bf16[512,512]{1,0:T(8,128)(2,1)S(1)}, u32[]{:S(2)}, u32[]{:S(2)}) collective-permute-start(bf16[512,512]{1,0:T(8,128)(2,1)S(1)} %collective-permute-done.refs_9_), channel_id=1, source_target_pairs={{0,16},{8,24},{16,0},{24,8},{1,17},{9,25},{17,1},{25,9},{2,18},{10... | collective-permute-start | bytes 1572872 | tf_op jit(solution)/shard_map/ppermute | solution.py:147
  38.1 26.1 %collective-permute-start.9 = (bf16[1024,512]{1,0:T(8,128)(2,1)S(1)}, bf16[1024,512]{1,0:T(8,128)(2,1)S(1)}, u32[]{:S(2)}, u32[]{:S(2)}) collective-permute-start(bf16[1024,512]{1,0:T(8,128)(2,1)S(1)} %get-tuple-element.132), channel_id=1, source_target_pairs={{0,8},{8,0},{16,24},{24,16},{1,9},{9,1},{17,25},{25,17},{2,10},{10... | collective-permute-start | bytes 3145736 | tf_op jit(solution)/shard_map/ppermute | solution.py:147
  38.8 25.4 %collective-permute-start.10 = (bf16[1024,512]{1,0:T(8,128)(2,1)S(1)}, bf16[1024,512]{1,0:T(8,128)(2,1)S(1)}, u32[]{:S(2)}, u32[]{:S(2)}) collective-permute-start(bf16[1024,512]{1,0:T(8,128)(2,1)S(1)} %get-tuple-element.131), channel_id=1, source_target_pairs={{0,16},{8,24},{16,0},{24,8},{1,17},{9,25},{17,1},{25,9},{2,18},{10... | collective-permute-start | bytes 3145736 | tf_op jit(solution)/shard_map/ppermute | solution.py:147
  40.3 12.7 %collective-permute-start.11 = (bf16[512,512]{1,0:T(8,128)(2,1)S(1)}, bf16[512,512]{1,0:T(8,128)(2,1)S(1)}, u32[]{:S(2)}, u32[]{:S(2)}) collective-permute-start(bf16[512,512]{1,0:T(8,128)(2,1)S(1)} %copy-done.22), channel_id=1, source_target_pairs={{0,6},{1,7},{2,4},{3,5},{4,2},{5,3},{6,0},{7,1},{8,14},{9,15},{10,... | collective-permute-start | bytes 1572872 | tf_op jit(solution)/shard_map/ppermute | solution.py:203
  42.6 21.5 %collective-permute-start.8 = (bf16[512,512]{1,0:T(8,128)(2,1)}, bf16[512,512]{1,0:T(8,128)(2,1)S(1)}, u32[]{:S(2)}, u32[]{:S(2)}) collective-permute-start(bf16[512,512]{1,0:T(8,128)(2,1)} %collective-permute-done.4), channel_id=1, source_target_pairs={{2,0},{3,1},{4,6},{5,7},{10,8},{11,9},{12,14},{13,15},{18,16},{19,... | collective-permute-start | bytes 1572872 | tf_op jit(solution)/shard_map/ppermute | solution.py:203
  66.1 19.7 %collective-permute-start.12 = (bf16[768,512]{1,0:T(8,128)(2,1)}, bf16[768,512]{1,0:T(8,128)(2,1)S(1)}, u32[]{:S(2)}, u32[]{:S(2)}) collective-permute-start(bf16[768,512]{1,0:T(8,128)(2,1)} %get-tuple-element.130), channel_id=1, source_target_pairs={{0,8},{8,0},{16,24},{24,16},{1,9},{9,1},{17,25},{25,17},{2,10},{10... | collective-permute-start | bytes 2359304 | tf_op jit(solution)/shard_map/ppermute | solution.py:147
  67.5 19.4 %collective-permute-start.13 = (bf16[768,512]{1,0:T(8,128)(2,1)}, bf16[768,512]{1,0:T(8,128)(2,1)S(1)}, u32[]{:S(2)}, u32[]{:S(2)}) collective-permute-start(bf16[768,512]{1,0:T(8,128)(2,1)} %get-tuple-element.129), channel_id=1, source_target_pairs={{0,16},{8,24},{16,0},{24,8},{1,17},{9,25},{17,1},{25,9},{2,18},{10... | collective-permute-start | bytes 2359304 | tf_op jit(solution)/shard_map/ppermute | solution.py:147
  68.0 28.1 %collective-permute-start.15 = (bf16[512,512]{1,0:T(8,128)(2,1)}, bf16[512,512]{1,0:T(8,128)(2,1)S(1)}, u32[]{:S(2)}, u32[]{:S(2)}) collective-permute-start(bf16[512,512]{1,0:T(8,128)(2,1)} %get-tuple-element.94), channel_id=1, source_target_pairs={{0,4},{1,5},{2,6},{3,7},{4,0},{5,1},{6,2},{7,3},{8,12},{9,13},{10,... | collective-permute-start | bytes 1572872 | tf_op jit(solution)/shard_map/ppermute | solution.py:203
  69.3 26.8 %collective-permute-start.14 = (bf16[512,512]{1,0:T(8,128)(2,1)}, bf16[512,512]{1,0:T(8,128)(2,1)}, u32[]{:S(2)}, u32[]{:S(2)}) collective-permute-start(bf16[512,512]{1,0:T(8,128)(2,1)} %get-tuple-element.110), channel_id=1, source_target_pairs={{0,2},{1,3},{2,0},{3,1},{4,6},{5,7},{6,4},{7,5},{8,10},{9,11},{10,... | collective-permute-start | bytes 1572872 | tf_op jit(solution)/shard_map/ppermute | solution.py:203
  86.9 30.7 %all-to-all-start = ((bf16[4,128,512]{2,1,0:T(8,128)(2,1)}), bf16[4,128,512]{2,1,0:T(8,128)(2,1)S(1)}, u32[]{:S(2)}, u32[]{:S(2)}) async-start(bf16[4,128,512]{2,1,0:T(8,128)(2,1)} %bitcast.18), calls=%async_computation | async-start | bytes 1048576 | tf_op jit(solution)/shard_map/all_to_all | solution.py:420
  90.6 12.7 %collective-permute-start.16 = (bf16[256,512]{1,0:T(8,128)(2,1)S(1)}, bf16[256,512]{1,0:T(8,128)(2,1)S(1)}, u32[]{:S(2)}, u32[]{:S(2)}) collective-permute-start(bf16[256,512]{1,0:T(8,128)(2,1)S(1)} %slice.42), channel_id=1, source_target_pairs={{0,8},{8,0},{16,24},{24,16},{1,9},{9,1},{17,25},{25,17},{2,10},{10... | collective-permute-start | bytes 786440 | tf_op jit(solution)/shard_map/ppermute | solution.py:147
  92.5 10.8 %collective-permute-start.17 = (bf16[256,512]{1,0:T(8,128)(2,1)S(1)}, bf16[256,512]{1,0:T(8,128)(2,1)S(1)}, u32[]{:S(2)}, u32[]{:S(2)}) collective-permute-start(bf16[256,512]{1,0:T(8,128)(2,1)S(1)} %slice.43), channel_id=1, source_target_pairs={{0,16},{8,24},{16,0},{24,8},{1,17},{9,25},{17,1},{25,9},{2,18},{10... | collective-permute-start | bytes 786440 | tf_op jit(solution)/shard_map/ppermute | solution.py:147
  94.0 21.8 %collective-permute-start.20 = (bf16[512,256]{1,0:T(8,128)(2,1)}, bf16[512,256]{1,0:T(8,128)(2,1)S(1)}, u32[]{:S(2)}, u32[]{:S(2)}) collective-permute-start(bf16[512,256]{1,0:T(8,128)(2,1)} %get-tuple-element.106), channel_id=1, source_target_pairs={{0,6},{1,7},{2,4},{3,5},{4,2},{5,3},{6,0},{7,1},{8,14},{9,15},{10,... | collective-permute-start | bytes 786440 | tf_op jit(solution)/shard_map/ppermute | solution.py:203
  96.1 19.7 %collective-permute-start.18 = (bf16[512,256]{1,0:T(8,128)(2,1)}, bf16[512,256]{1,0:T(8,128)(2,1)S(1)}, u32[]{:S(2)}, u32[]{:S(2)}) collective-permute-start(bf16[512,256]{1,0:T(8,128)(2,1)} %get-tuple-element.116), channel_id=1, source_target_pairs={{0,2},{1,3},{2,0},{3,1},{4,6},{5,7},{6,4},{7,5},{8,10},{9,11},{10,... | collective-permute-start | bytes 786440 | tf_op jit(solution)/shard_map/ppermute | solution.py:203
  96.1 21.5 %collective-permute-start.19 = (bf16[512,256]{1,0:T(8,128)(2,1)S(1)}, bf16[512,256]{1,0:T(8,128)(2,1)}, u32[]{:S(2)}, u32[]{:S(2)}) collective-permute-start(bf16[512,256]{1,0:T(8,128)(2,1)S(1)} %copy-done.23), channel_id=1, source_target_pairs={{0,4},{1,5},{2,6},{3,7},{4,0},{5,1},{6,2},{7,3},{8,12},{9,13},{10,... | collective-permute-start | bytes 786440 | tf_op jit(solution)/shard_map/ppermute | solution.py:203
  117.6 10.4 %collective-permute-start.22 = (f32[256,2048]{1,0:T(8,128)}, f32[256,2048]{1,0:T(8,128)}, u32[]{:S(2)}, u32[]{:S(2)}) collective-permute-start(f32[256,2048]{1,0:T(8,128)} %get-tuple-element.127), channel_id=1, source_target_pairs={{0,1},{1,0},{2,3},{3,2},{4,5},{5,4},{6,7},{7,6},{8,9},{9,8},{10,11... | collective-permute-start | bytes 6291464 | tf_op jit(solution)/shard_map/ppermute | solution.py:147
  126.8 10.4 %collective-permute-start.21 = (f32[128,2048]{1,0:T(8,128)}, f32[128,2048]{1,0:T(8,128)S(1)}, u32[]{:S(2)}, u32[]{:S(2)}) collective-permute-start(f32[128,2048]{1,0:T(8,128)} %get-tuple-element.124), channel_id=1, source_target_pairs={{0,1},{1,0},{2,3},{3,2},{4,5},{5,4},{6,7},{7,6},{8,9},{9,8},{10,11... | collective-permute-start | bytes 3145736 | tf_op jit(solution)/shard_map/ppermute | solution.py:147
  (24 other events, 308.8 us)

commit v5 on v4

--- a/solution.py
+++ b/solution.py
@@ -10,7 +10,8 @@
 from jax.sharding import PartitionSpec as P
 
 VMEM_LIMIT = 32 * 1024 * 1024
-PROJECT_LIMIT = 60 * 1024 * 1024
+PROJECT_LIMIT = 52 * 1024 * 1024
+CONVOLVE_LIMIT = 60 * 1024 * 1024
 F32 = jnp.float32
 BF16 = jnp.bfloat16
 
@@ -112,7 +113,7 @@
         ],
         out_specs=pl.BlockSpec((step, span), lambda g: (g, 0)),
         out_shape=jax.ShapeDtypeStruct((rows, span), F32),
-        compiler_params=pltpu.CompilerParams(vmem_limit_bytes=PROJECT_LIMIT),
+        compiler_params=pltpu.CompilerParams(vmem_limit_bytes=CONVOLVE_LIMIT),
         name="convolve",
     )(own, other, params, moved_filter, high, low)
 
@@ -189,7 +190,7 @@
         ),
         out_shape=[jax.ShapeDtypeStruct((depth, 4 * few), BF16)] * chips
         + [jax.ShapeDtypeStruct((depth, 2 * few), BF16)] * chips,
-        compiler_params=pltpu.CompilerParams(vmem_limit_bytes=PROJECT_LIMIT),
+        compiler_params=pltpu.CompilerParams(vmem_limit_bytes=CONVOLVE_LIMIT),
         name="pick_columns",
     )(at, in_proj)
     return outs[:chips], outs[chips:]
@@ -218,7 +219,8 @@
     half = length // 2
 
     def spread(to_near, to_far):
-        return swap(jnp.concatenate(to_near), "ctx", 1), swap(jnp.concatenate(to_far), "ctx", 2)
+        to_near, to_far = jnp.concatenate(to_near), jnp.concatenate(to_far)
+        return to_near, swap(to_near, "ctx", 1), swap(to_far, "ctx", 2)
 
     pair = move_chips(block, [(0, 1), (1, 0), (2, 3), (3, 2)])
     across = move_chips(block, middle)
@@ -238,7 +240,7 @@
 
     second = jnp.where(inner, across, second)
     third = move_chips(farther, ends)
-    near2, far2 = spread(
+    second, near2, far2 = spread(
         [far0[:half], far1[:half], second], [near0[half:], near1[half:], second]
     )
     pair_2 = turn_chips(pairs[2], 2)
@@ -247,14 +249,14 @@
     )
 
     third = jnp.where(inner, farther, third)
-    near3, far3 = spread(
+    third, near3, far3 = spread(
         [far2[length : length + half], third], [near2[length + half :], third]
     )
     pair_1 = turn_chips(pairs[1], 1)
     single_3 = turn_chips(singles[3], 3)
     near3, far3, singles, long_filter, early = order((near3, far3, singles, long_filter, early))
 
-    near4, far4 = spread([far3[half:length]], [near3[length:]])
+    _, near4, far4 = spread([far3[half:length]], [near3[length:]])
     single_1, single_2 = turn_chips(singles[1], 1), turn_chips(singles[2], 2)
     pairs = [pairs[0], pair_1, pair_2, pair_3]
     singles = [singles[0], single_1, single_2, single_3]
@@ -364,7 +366,7 @@
         corner, row = ((2, 0), (2, half), (3, 0), (4, 0))[s]
         plan.append(
             (
-                (place_of(blocks[s]), 0, length, 0),
+                (place_of(blocks[s]), skip, length, 0),
                 (place_of(near[s]), skip, length, length),
                 (place_of(far[s]), skip, length, 2 * length),
                 (place_of(near[corner]), row, half, 3 * length),
@@ -421,8 +423,9 @@
         long_filter.reshape(cycle, few, length), "ctx", split_axis=0, concat_axis=0, tiled=True
     )
     if fits:
+        slots, moved_filter = lax.optimization_barrier((slots, moved_filter))
         mine, send = project(at, slots, pairs, 0, 4)
-        send, singles, moved_filter = lax.optimization_barrier((send, singles, moved_filter))
+        send, singles = lax.optimization_barrier((send, singles))
     else:
         mine, send = project_plain(slots, pairs)
     theirs = swap(send, "chan", 1)

time: 152 us -> 152 us (level)
  waiting for transfers between devices: 57.9 us -> 61.6 us
  starting transfers between devices: 33.9 us -> 31.2 us
  Pallas kernels: 37.4 us -> 35.6 us
    ppermute x11, waiting for transfers between devices: 34.8 us -> 38.2 us  [move_chips(): lax.ppermute(x, 'chan', [(2 * a + k, 2 * b + k) for a, b in pairs for k i...]
    all_to_all x1, waiting for transfers between devices: 0.01 us -> 2.75 us  [body(): lax.all_to_all(long_filter.reshape(cycle, few, length), 'ctx', split_axis...]
    ppermute x12, waiting for transfers between devices: 23.2 us -> 20.7 us  [swap(): lax.ppermute(x, axis, [(i, i ^ bit) for i in range(lax.axis_size(axis))])]
    ppermute x12, starting transfers between devices: 13.2 us -> 11.2 us  [swap(): lax.ppermute(x, axis, [(i, i ^ bit) for i in range(lax.axis_size(axis))])]
    pallas_call x2, Pallas kernels: 20.2 us -> 18.5 us  [project(): pl.pallas_call(functools.partial(project_kernel, plan, range(len(weights)...]
    slice x2, local copies, waits for them, and re-layouts: 0.04 us -> 1.72 us  [gather(): _, near4, far4 = spread([far3[half:length]], [near3[length:]])]
    unnamed x49 -> x37, local copies, waits for them, and re-layouts: 4.66 us -> 3.32 us
  transfers between devices with their start and end apart: 24 -> 24, of which waited for: 10 -> 11; matrix products, arithmetic and copies ran while one was open for 2% -> 3% of each run, Pallas kernels for 24% -> 23%
where the time goes in v5:
time: 152 us; the launch traced here: 151 us
  waiting for transfers between devices  61.6 us (41%)
  Pallas kernels  35.6 us (23%)
  starting transfers between devices  31.2 us (21%)
  blocking collectives  12.1 us (8%)
  local copies, waits for them, and re-layouts  7.42 us (5%)
  other arithmetic  2.7 us (2%)
    ppermute x11, waiting for transfers between devices, move_chips(): lax.ppermute(x, 'chan', [(2 * a + k, 2 * b + k) for a, b in pairs for k i...  38.2 us
    ppermute x12, waiting for transfers between devices, swap(): lax.ppermute(x, axis, [(i, i ^ bit) for i in range(lax.axis_size(axis))])  20.7 us
    pallas_call x2, Pallas kernels, project(): pl.pallas_call(functools.partial(project_kernel, plan, range(len(weights)...  18.5 us
    ppermute x11, starting transfers between devices, move_chips(): lax.ppermute(x, 'chan', [(2 * a + k, 2 * b + k) for a, b in pairs for k i...  15.7 us
    all_to_all x1, blocking collectives, body(): lax.all_to_all(gated, 'ctx', split_axis=0, concat_axis=0, tiled=True)  12.1 us
    ppermute x12, starting transfers between devices, swap(): lax.ppermute(x, axis, [(i, i ^ bit) for i in range(lax.axis_size(axis))])  11.2 us
    pallas_call x1, Pallas kernels, convolve(): pl.pallas_call(conv_kernel, grid=(rows // step,), in_specs=[pl.BlockSpec(...  9.09 us
    pallas_call x1, Pallas kernels, pick_columns(): pl.pallas_call(pick_kernel, grid_spec=pltpu.PrefetchScalarGridSpec(num_sc...  7.25 us
  transfers between devices with their start and end apart: 24, of which 11 were waited for; matrix products, arithmetic and copies ran while one was open for 3% of the time, Pallas kernels for 23%

profile of v5, /device:TPU:0, one launch (start us, length us, event | category | flops | bytes accessed | tf_op | source)
XLA Modules:
  0.0 151.0 jit_solution(12899389468562889073)
XLA Ops:
  0.0 3.0 %collective-permute-start = (bf16[512,512]{1,0:T(8,128)(2,1)}, bf16[512,512]{1,0:T(8,128)(2,1)S(1)}, u32[]{:S(2)}, u32[]{:S(2)}) collective-permute-start(bf16[512,512]{1,0:T(8,128)(2,1)} %refs_4_.1), channel_id=1, source_target_pairs={{0,2},{1,3},{2,0},{3,1},{4,6},{5,7},{6,4},{7,5},{8,10},{9,11},{10,... | collective-permute-start | bytes 1572872 | tf_op jit(solution)/shard_map/ppermute | solution.py:204
  3.7 1.6 %collective-permute-start.2 = (bf16[512,512]{1,0:T(8,128)(2,1)}, bf16[512,512]{1,0:T(8,128)(2,1)S(1)}, u32[]{:S(2)}, u32[]{:S(2)}) collective-permute-start(bf16[512,512]{1,0:T(8,128)(2,1)} %refs_4_.1), channel_id=1, source_target_pairs={{0,8},{8,0},{16,24},{24,16},{1,9},{9,1},{17,25},{25,17},{2,10},{10... | collective-permute-start | bytes 1572872 | tf_op jit(solution)/shard_map/ppermute | solution.py:148
  5.3 1.5 %collective-permute-start.3 = (bf16[512,512]{1,0:T(8,128)(2,1)}, bf16[512,512]{1,0:T(8,128)(2,1)S(1)}, u32[]{:S(2)}, u32[]{:S(2)}) collective-permute-start(bf16[512,512]{1,0:T(8,128)(2,1)} %refs_4_.1), channel_id=1, source_target_pairs={{0,16},{8,24},{16,0},{24,8},{1,17},{9,25},{17,1},{25,9},{2,18},{10... | collective-permute-start | bytes 1572872 | tf_op jit(solution)/shard_map/ppermute | solution.py:148
  7.5 7.2 %pick_columns.1 = (bf16[512,512]{1,0:T(8,128)(2,1)}, bf16[512,512]{1,0:T(8,128)(2,1)}, bf16[512,512]{1,0:T(8,128)(2,1)}, bf16[512,512]{1,0:T(8,128)(2,1)}, bf16[...) custom-call(s32[8]{0:T(128)} %stack.56.at_ref, ...), custom_call_target="tpu_custom_call" | custom-call | tf_op jit(solution)/shard_map/pick_columns/pallas_call | solution.py:182
  15.2 2.2 %collective-permute-done.2.refs_5_ = bf16[512,512]{1,0:T(8,128)(2,1)S(1)} collective-permute-done((bf16[512,512]{1,0:T(8,128)(2,1)}, bf16[512,512]{1,0:T(8,128)(2,1)S(1)}, u32[]{:S(2)}, u32[]{:S(2)}) %collective-permute-start.2) | collective-permute-done | bytes 524320 | tf_op jit(solution)/shard_map/ppermute | solution.py:148
  18.6 1.5 collective-permute-start.4
  22.0 1.5 %collective-permute-start.7 = (bf16[512,512]{1,0:T(8,128)(2,1)S(1)}, bf16[512,512]{1,0:T(8,128)(2,1)S(1)}, u32[]{:S(2)}, u32[]{:S(2)}) collective-permute-start(bf16[512,512]{1,0:T(8,128)(2,1)S(1)} %collective-permute-done.refs_9_), channel_id=1, source_target_pairs={{0,16},{8,24},{16,0},{24,8},{1,17},{9,25},{17,1},{25,9},{2,18},{10... | collective-permute-start | bytes 1572872 | tf_op jit(solution)/shard_map/ppermute | solution.py:148
  23.5 12.9 %collective-permute-done.5 = bf16[512,512]{1,0:T(8,128)(2,1)} collective-permute-done((bf16[512,512]{1,0:T(8,128)(2,1)S(1)}, bf16[512,512]{1,0:T(8,128)(2,1)}, u32[]{:S(2)}, u32[]{:S(2)}) %collective-permute-start.5) | collective-permute-done | bytes 524320 | tf_op jit(solution)/shard_map/ppermute | solution.py:204
  38.8 1.5 %collective-permute-start.10 = (bf16[1024,512]{1,0:T(8,128)(2,1)S(1)}, bf16[1024,512]{1,0:T(8,128)(2,1)S(1)}, u32[]{:S(2)}, u32[]{:S(2)}) collective-permute-start(bf16[1024,512]{1,0:T(8,128)(2,1)S(1)} %get-tuple-element.159), channel_id=1, source_target_pairs={{0,16},{8,24},{16,0},{24,8},{1,17},{9,25},{17,1},{25,9},{2,18},{10... | collective-permute-start | bytes 3145736 | tf_op jit(solution)/shard_map/ppermute | solution.py:148
  40.3 2.3 %collective-permute-start.11 = (bf16[512,512]{1,0:T(8,128)(2,1)S(1)}, bf16[512,512]{1,0:T(8,128)(2,1)S(1)}, u32[]{:S(2)}, u32[]{:S(2)}) collective-permute-start(bf16[512,512]{1,0:T(8,128)(2,1)S(1)} %copy-done.17), channel_id=1, source_target_pairs={{0,6},{1,7},{2,4},{3,5},{4,2},{5,3},{6,0},{7,1},{8,14},{9,15},{10,... | collective-permute-start | bytes 1572872 | tf_op jit(solution)/shard_map/ppermute | solution.py:204
  43.9 9.1 %collective-permute-done.11.refs_3_ = bf16[512,512]{1,0:T(8,128)(2,1)S(1)} collective-permute-done((bf16[512,512]{1,0:T(8,128)(2,1)S(1)}, bf16[512,512]{1,0:T(8,128)(2,1)S(1)}, u32[]{:S(2)}, u32[]{:S(2)}) %collective-permute-start.11) | collective-permute-done | bytes 524320 | tf_op jit(solution)/shard_map/ppermute | solution.py:204
  53.1 11.1 %collective-permute-done.8 = bf16[512,512]{1,0:T(8,128)(2,1)S(1)} collective-permute-done((bf16[512,512]{1,0:T(8,128)(2,1)}, bf16[512,512]{1,0:T(8,128)(2,1)S(1)}, u32[]{:S(2)}, u32[]{:S(2)}) %collective-permute-start.8) | collective-permute-done | bytes 524320 | tf_op jit(solution)/shard_map/ppermute | solution.py:204
  69.9 2.2 %collective-permute-start.14 = (bf16[512,512]{1,0:T(8,128)(2,1)}, bf16[512,512]{1,0:T(8,128)(2,1)S(1)}, u32[]{:S(2)}, u32[]{:S(2)}) collective-permute-start(bf16[512,512]{1,0:T(8,128)(2,1)} %get-tuple-element.124), channel_id=1, source_target_pairs={{0,2},{1,3},{2,0},{3,1},{4,6},{5,7},{6,4},{7,5},{8,10},{9,11},{10,... | collective-permute-start | bytes 1572872 | tf_op jit(solution)/shard_map/ppermute | solution.py:204
  72.1 14.0 %collective-permute-done.12.refs_13_ = bf16[768,512]{1,0:T(8,128)(2,1)S(1)} collective-permute-done((bf16[768,512]{1,0:T(8,128)(2,1)S(1)}, bf16[768,512]{1,0:T(8,128)(2,1)S(1)}, u32[]{:S(2)}, u32[]{:S(2)}) %collective-permute-start.12) | collective-permute-done | bytes 786464 | tf_op jit(solution)/shard_map/ppermute | solution.py:148
  87.5 1.7 %slice.42 = bf16[256,512]{1,0:T(8,128)(2,1)} slice(bf16[768,512]{1,0:T(8,128)(2,1)} %collective-permute-done.13.refs_14_), slice={[256:512], [0:512]} | slice | bytes 524288 | tf_op jit(solution)/shard_map/slice | solution.py:259
  90.6 4.3 %all-to-all-start = ((bf16[4,128,512]{2,1,0:T(8,128)(2,1)}), bf16[4,128,512]{2,1,0:T(8,128)(2,1)}, u32[]{:S(2)}, u32[]{:S(2)}) async-start(bf16[4,128,512]{2,1,0:T(8,128)(2,1)} %bitcast.28), calls=%async_computation | async-start | bytes 1048576 | tf_op jit(solution)/shard_map/all_to_all | solution.py:422
  95.0 2.1 %collective-permute-start.20 = (bf16[512,256]{1,0:T(8,128)(2,1)}, bf16[512,256]{1,0:T(8,128)(2,1)S(1)}, u32[]{:S(2)}, u32[]{:S(2)}) collective-permute-start(bf16[512,256]{1,0:T(8,128)(2,1)} %get-tuple-element.120), channel_id=1, source_target_pairs={{0,6},{1,7},{2,4},{3,5},{4,2},{5,3},{6,0},{7,1},{8,14},{9,15},{10,... | collective-permute-start | bytes 786440 | tf_op jit(solution)/shard_map/ppermute | solution.py:204
  97.2 1.9 %collective-permute-done.17.refs_17_ = bf16[256,512]{1,0:T(8,128)(2,1)S(1)} collective-permute-done((bf16[256,512]{1,0:T(8,128)(2,1)S(1)}, bf16[256,512]{1,0:T(8,128)(2,1)S(1)}, u32[]{:S(2)}, u32[]{:S(2)}) %collective-permute-start.17) | collective-permute-done | bytes 262176 | tf_op jit(solution)/shard_map/ppermute | solution.py:148
  99.7 2.7 %all-to-all-done.filter_ref = bf16[4,128,512]{2,1,0:T(8,128)(2,1)} async-done(((bf16[4,128,512]{2,1,0:T(8,128)(2,1)}), bf16[4,128,512]{2,1,0:T(8,128)(2,1)}, u32[]{:S(2)}, u32[]{:S(2)}) %all-to-all-start) | async-done | bytes 524320 | tf_op jit(solution)/shard_map/all_to_all | solution.py:422
  102.5 10.6 %project.2 = (f32[256,2048]{1,0:T(8,128)}, f32[256,2048]{1,0:T(8,128)}) custom-call(s32[8]{0:T(128)S(1)} %stack.63.at_ref, bf16[512,512]{1,0:T(8,128)(2,1)S(1)} %copy-done.4, bf16[512,512]{1,0:T(8,128)(2,1)S(1)} %collective-permute-done.14.refs_1_, bf16[512,512]{1,0:T(8,128)(2,1)} %collective-permute-done.15.refs_2_, bf16[512,512]{1,0:T(8,128)(2,1)} %copy-done.16, ...), custom_call_target="tpu_custom_call" | custom-call | tf_op jit(solution)/shard_map/project/pallas_call | solution.py:377
  113.2 4.6 %collective-permute-done.19.refs_2_ = bf16[512,256]{1,0:T(8,128)(2,1)S(1)} collective-permute-done((bf16[512,256]{1,0:T(8,128)(2,1)}, bf16[512,256]{1,0:T(8,128)(2,1)S(1)}, u32[]{:S(2)}, u32[]{:S(2)}) %collective-permute-start.19) | collective-permute-done | bytes 262176 | tf_op jit(solution)/shard_map/ppermute | solution.py:204
  117.8 7.8 %project.3 = (f32[128,2048]{1,0:T(8,128)}, f32[128,2048]{1,0:T(8,128)}) custom-call(s32[8]{0:T(128)S(1)} %stack.63.at_ref, bf16[512,256]{1,0:T(8,128)(2,1)S(1)} %copy-done.5, bf16[512,256]{1,0:T(8,128)(2,1)S(1)} %collective-permute-done.18.refs_1_, bf16[512,256]{1,0:T(8,128)(2,1)S(1)} %collective-permute-done.19.refs_2_, ...), custom_call_target="tpu_custom_call" | custom-call | tf_op jit(solution)/shard_map/project/pallas_call | solution.py:377
  126.9 9.1 %convolve.1.answer_ref = f32[128,2048]{1,0:T(8,128)} custom-call(f32[2,128,2048]{2,1,0:T(8,128)} %bitcast.27, f32[2,128,2048]{2,1,0:T(8,128)} %bitcast.20.other_ref, f32[128,10]{1,0:T(8,128)} %copy.11.params_ref, bf16[4,128,512]{2,1,0:T(8,128)(2,1)} %all-to-all-done.filter_ref, bf16[512,1024]{1,0:T(8,128)(2,1)} %constant.52.clone.high_ref, ...), custom_call_target="tpu_custom_call" | custom-call | tf_op jit(solution)/shard_map/convolve/pallas_call | solution.py:103
  138.1 12.1 %all_to_all.10 = bf16[4,128,512]{2,1,0:T(8,128)(2,1)S(1)} all-to-all(bf16[4,128,512]{2,1,0:T(8,128)(2,1)S(1)} %gate.1), channel_id=1, replica_groups=mesh['ctx'=4,'chan'=8] {'ctx'}, dimensions={0} | all-to-all | bytes 1048576 | tf_op jit(solution)/shard_map/all_to_all | solution.py:437
  (85 shorter events, 22.0 us)
Async XLA Ops:
  0.0 15.2 %collective-permute-start = (bf16[512,512]{1,0:T(8,128)(2,1)}, bf16[512,512]{1,0:T(8,128)(2,1)S(1)}, u32[]{:S(2)}, u32[]{:S(2)}) collective-permute-start(bf16[512,512]{1,0:T(8,128)(2,1)} %refs_4_.1), channel_id=1, source_target_pairs={{0,2},{1,3},{2,0},{3,1},{4,6},{5,7},{6,4},{7,5},{8,10},{9,11},{10,... | collective-permute-start | bytes 1572872 | tf_op jit(solution)/shard_map/ppermute | solution.py:204
  3.0 12.1 %collective-permute-start.1 = (bf16[512,512]{1,0:T(8,128)(2,1)}, bf16[512,512]{1,0:T(8,128)(2,1)S(1)}, u32[]{:S(2)}, u32[]{:S(2)}) collective-permute-start(bf16[512,512]{1,0:T(8,128)(2,1)} %refs_4_.1), channel_id=1, source_target_pairs={{2,4},{3,5},{4,2},{5,3},{10,12},{11,13},{12,10},{13,11},{18,20},{1... | collective-permute-start | bytes 1572872 | tf_op jit(solution)/shard_map/ppermute | solution.py:204
  3.7 13.7 %collective-permute-start.2 = (bf16[512,512]{1,0:T(8,128)(2,1)}, bf16[512,512]{1,0:T(8,128)(2,1)S(1)}, u32[]{:S(2)}, u32[]{:S(2)}) collective-permute-start(bf16[512,512]{1,0:T(8,128)(2,1)} %refs_4_.1), channel_id=1, source_target_pairs={{0,8},{8,0},{16,24},{24,16},{1,9},{9,1},{17,25},{25,17},{2,10},{10... | collective-permute-start | bytes 1572872 | tf_op jit(solution)/shard_map/ppermute | solution.py:148
  5.3 13.3 %collective-permute-start.3 = (bf16[512,512]{1,0:T(8,128)(2,1)}, bf16[512,512]{1,0:T(8,128)(2,1)S(1)}, u32[]{:S(2)}, u32[]{:S(2)}) collective-permute-start(bf16[512,512]{1,0:T(8,128)(2,1)} %refs_4_.1), channel_id=1, source_target_pairs={{0,16},{8,24},{16,0},{24,8},{1,17},{9,25},{17,1},{25,9},{2,18},{10... | collective-permute-start | bytes 1572872 | tf_op jit(solution)/shard_map/ppermute | solution.py:148
  18.6 4.9 %collective-permute-start.4 = (bf16[512,512]{1,0:T(8,128)(2,1)S(1)}, bf16[512,512]{1,0:T(8,128)(2,1)}, u32[]{:S(2)}, u32[]{:S(2)}) collective-permute-start(bf16[512,512]{1,0:T(8,128)(2,1)S(1)} %collective-permute-done.refs_9_), channel_id=1, source_target_pairs={{2,4},{3,5},{4,2},{5,3},{10,12},{11,13},{12,10},{13,11},{18,20},{1... | collective-permute-start | bytes 1572872 | tf_op jit(solution)/shard_map/ppermute | solution.py:204
  20.1 16.3 %collective-permute-start.5 = (bf16[512,512]{1,0:T(8,128)(2,1)S(1)}, bf16[512,512]{1,0:T(8,128)(2,1)}, u32[]{:S(2)}, u32[]{:S(2)}) collective-permute-start(bf16[512,512]{1,0:T(8,128)(2,1)S(1)} %collective-permute-done.1), channel_id=1, source_target_pairs={{2,0},{3,1},{4,6},{5,7},{10,8},{11,9},{12,14},{13,15},{18,16},{19,... | collective-permute-start | bytes 1572872 | tf_op jit(solution)/shard_map/ppermute | solution.py:204
  21.4 15.1 %collective-permute-start.6 = (bf16[512,512]{1,0:T(8,128)(2,1)S(1)}, bf16[512,512]{1,0:T(8,128)(2,1)S(1)}, u32[]{:S(2)}, u32[]{:S(2)}) collective-permute-start(bf16[512,512]{1,0:T(8,128)(2,1)S(1)} %collective-permute-done.refs_9_), channel_id=1, source_target_pairs={{0,8},{8,0},{16,24},{24,16},{1,9},{9,1},{17,25},{25,17},{2,10},{10... | collective-permute-start | bytes 1572872 | tf_op jit(solution)/shard_map/ppermute | solution.py:148
  22.0 14.5 %collective-permute-start.7 = (bf16[512,512]{1,0:T(8,128)(2,1)S(1)}, bf16[512,512]{1,0:T(8,128)(2,1)S(1)}, u32[]{:S(2)}, u32[]{:S(2)}) collective-permute-start(bf16[512,512]{1,0:T(8,128)(2,1)S(1)} %collective-permute-done.refs_9_), channel_id=1, source_target_pairs={{0,16},{8,24},{16,0},{24,8},{1,17},{9,25},{17,1},{25,9},{2,18},{10... | collective-permute-start | bytes 1572872 | tf_op jit(solution)/shard_map/ppermute | solution.py:148
  38.1 26.1 %collective-permute-start.9 = (bf16[1024,512]{1,0:T(8,128)(2,1)S(1)}, bf16[1024,512]{1,0:T(8,128)(2,1)S(1)}, u32[]{:S(2)}, u32[]{:S(2)}) collective-permute-start(bf16[1024,512]{1,0:T(8,128)(2,1)S(1)} %get-tuple-element.137.refs_12_), channel_id=1, source_target_pairs={{0,8},{8,0},{16,24},{24,16},{1,9},{9,1},{17,25},{25,17},{2,10},{10... | collective-permute-start | bytes 3145736 | tf_op jit(solution)/shard_map/ppermute | solution.py:148
  38.8 25.4 %collective-permute-start.10 = (bf16[1024,512]{1,0:T(8,128)(2,1)S(1)}, bf16[1024,512]{1,0:T(8,128)(2,1)S(1)}, u32[]{:S(2)}, u32[]{:S(2)}) collective-permute-start(bf16[1024,512]{1,0:T(8,128)(2,1)S(1)} %get-tuple-element.159), channel_id=1, source_target_pairs={{0,16},{8,24},{16,0},{24,8},{1,17},{9,25},{17,1},{25,9},{2,18},{10... | collective-permute-start | bytes 3145736 | tf_op jit(solution)/shard_map/ppermute | solution.py:148
  40.3 12.7 %collective-permute-start.11 = (bf16[512,512]{1,0:T(8,128)(2,1)S(1)}, bf16[512,512]{1,0:T(8,128)(2,1)S(1)}, u32[]{:S(2)}, u32[]{:S(2)}) collective-permute-start(bf16[512,512]{1,0:T(8,128)(2,1)S(1)} %copy-done.17), channel_id=1, source_target_pairs={{0,6},{1,7},{2,4},{3,5},{4,2},{5,3},{6,0},{7,1},{8,14},{9,15},{10,... | collective-permute-start | bytes 1572872 | tf_op jit(solution)/shard_map/ppermute | solution.py:204
  42.7 21.5 %collective-permute-start.8 = (bf16[512,512]{1,0:T(8,128)(2,1)}, bf16[512,512]{1,0:T(8,128)(2,1)S(1)}, u32[]{:S(2)}, u32[]{:S(2)}) collective-permute-start(bf16[512,512]{1,0:T(8,128)(2,1)} %collective-permute-done.4), channel_id=1, source_target_pairs={{2,0},{3,1},{4,6},{5,7},{10,8},{11,9},{12,14},{13,15},{18,16},{19,... | collective-permute-start | bytes 1572872 | tf_op jit(solution)/shard_map/ppermute | solution.py:204
  66.6 19.5 %collective-permute-start.12 = (bf16[768,512]{1,0:T(8,128)(2,1)S(1)}, bf16[768,512]{1,0:T(8,128)(2,1)S(1)}, u32[]{:S(2)}, u32[]{:S(2)}) collective-permute-start(bf16[768,512]{1,0:T(8,128)(2,1)S(1)} %get-tuple-element.140.refs_15_), channel_id=1, source_target_pairs={{0,8},{8,0},{16,24},{24,16},{1,9},{9,1},{17,25},{25,17},{2,10},{10... | collective-permute-start | bytes 2359304 | tf_op jit(solution)/shard_map/ppermute | solution.py:148
  68.0 19.5 %collective-permute-start.13 = (bf16[768,512]{1,0:T(8,128)(2,1)}, bf16[768,512]{1,0:T(8,128)(2,1)}, u32[]{:S(2)}, u32[]{:S(2)}) collective-permute-start(bf16[768,512]{1,0:T(8,128)(2,1)} %get-tuple-element.157), channel_id=1, source_target_pairs={{0,16},{8,24},{16,0},{24,8},{1,17},{9,25},{17,1},{25,9},{2,18},{10... | collective-permute-start | bytes 2359304 | tf_op jit(solution)/shard_map/ppermute | solution.py:148
  69.3 33.2 %collective-permute-start.15 = (bf16[512,512]{1,0:T(8,128)(2,1)}, bf16[512,512]{1,0:T(8,128)(2,1)}, u32[]{:S(2)}, u32[]{:S(2)}) collective-permute-start(bf16[512,512]{1,0:T(8,128)(2,1)} %get-tuple-element.108), channel_id=1, source_target_pairs={{0,4},{1,5},{2,6},{3,7},{4,0},{5,1},{6,2},{7,3},{8,12},{9,13},{10,... | collective-permute-start | bytes 1572872 | tf_op jit(solution)/shard_map/ppermute | solution.py:204
  69.9 32.6 %collective-permute-start.14 = (bf16[512,512]{1,0:T(8,128)(2,1)}, bf16[512,512]{1,0:T(8,128)(2,1)S(1)}, u32[]{:S(2)}, u32[]{:S(2)}) collective-permute-start(bf16[512,512]{1,0:T(8,128)(2,1)} %get-tuple-element.124), channel_id=1, source_target_pairs={{0,2},{1,3},{2,0},{3,1},{4,6},{5,7},{6,4},{7,5},{8,10},{9,11},{10,... | collective-permute-start | bytes 1572872 | tf_op jit(solution)/shard_map/ppermute | solution.py:204
  89.2 7.9 %collective-permute-start.16 = (bf16[256,512]{1,0:T(8,128)(2,1)}, bf16[256,512]{1,0:T(8,128)(2,1)S(1)}, u32[]{:S(2)}, u32[]{:S(2)}) collective-permute-start(bf16[256,512]{1,0:T(8,128)(2,1)} %slice.42), channel_id=1, source_target_pairs={{0,8},{8,0},{16,24},{24,16},{1,9},{9,1},{17,25},{25,17},{2,10},{10... | collective-permute-start | bytes 786440 | tf_op jit(solution)/shard_map/ppermute | solution.py:148
  89.9 9.2 %collective-permute-start.17 = (bf16[256,512]{1,0:T(8,128)(2,1)S(1)}, bf16[256,512]{1,0:T(8,128)(2,1)S(1)}, u32[]{:S(2)}, u32[]{:S(2)}) collective-permute-start(bf16[256,512]{1,0:T(8,128)(2,1)S(1)} %slice.43), channel_id=1, source_target_pairs={{0,16},{8,24},{16,0},{24,8},{1,17},{9,25},{17,1},{25,9},{2,18},{10... | collective-permute-start | bytes 786440 | tf_op jit(solution)/shard_map/ppermute | solution.py:148
  90.6 11.9 %all-to-all-start = ((bf16[4,128,512]{2,1,0:T(8,128)(2,1)}), bf16[4,128,512]{2,1,0:T(8,128)(2,1)}, u32[]{:S(2)}, u32[]{:S(2)}) async-start(bf16[4,128,512]{2,1,0:T(8,128)(2,1)} %bitcast.28), calls=%async_computation | async-start | bytes 1048576 | tf_op jit(solution)/shard_map/all_to_all | solution.py:422
  95.0 18.2 %collective-permute-start.20 = (bf16[512,256]{1,0:T(8,128)(2,1)}, bf16[512,256]{1,0:T(8,128)(2,1)S(1)}, u32[]{:S(2)}, u32[]{:S(2)}) collective-permute-start(bf16[512,256]{1,0:T(8,128)(2,1)} %get-tuple-element.120), channel_id=1, source_target_pairs={{0,6},{1,7},{2,4},{3,5},{4,2},{5,3},{6,0},{7,1},{8,14},{9,15},{10,... | collective-permute-start | bytes 786440 | tf_op jit(solution)/shard_map/ppermute | solution.py:204
  97.1 16.1 %collective-permute-start.18 = (bf16[512,256]{1,0:T(8,128)(2,1)}, bf16[512,256]{1,0:T(8,128)(2,1)S(1)}, u32[]{:S(2)}, u32[]{:S(2)}) collective-permute-start(bf16[512,256]{1,0:T(8,128)(2,1)} %get-tuple-element.145), channel_id=1, source_target_pairs={{0,2},{1,3},{2,0},{3,1},{4,6},{5,7},{6,4},{7,5},{8,10},{9,11},{10,... | collective-permute-start | bytes 786440 | tf_op jit(solution)/shard_map/ppermute | solution.py:204
  99.0 18.7 %collective-permute-start.19 = (bf16[512,256]{1,0:T(8,128)(2,1)}, bf16[512,256]{1,0:T(8,128)(2,1)S(1)}, u32[]{:S(2)}, u32[]{:S(2)}) collective-permute-start(bf16[512,256]{1,0:T(8,128)(2,1)} %get-tuple-element.146), channel_id=1, source_target_pairs={{0,4},{1,5},{2,6},{3,7},{4,0},{5,1},{6,2},{7,3},{8,12},{9,13},{10,... | collective-permute-start | bytes 786440 | tf_op jit(solution)/shard_map/ppermute | solution.py:204
  117.8 9.2 %collective-permute-start.22 = (f32[256,2048]{1,0:T(8,128)}, f32[256,2048]{1,0:T(8,128)}, u32[]{:S(2)}, u32[]{:S(2)}) collective-permute-start(f32[256,2048]{1,0:T(8,128)} %get-tuple-element.155), channel_id=1, source_target_pairs={{0,1},{1,0},{2,3},{3,2},{4,5},{5,4},{6,7},{7,6},{8,9},{9,8},{10,11... | collective-permute-start | bytes 6291464 | tf_op jit(solution)/shard_map/ppermute | solution.py:148
  125.6 10.4 %collective-permute-start.21 = (f32[128,2048]{1,0:T(8,128)}, f32[128,2048]{1,0:T(8,128)S(1)}, u32[]{:S(2)}, u32[]{:S(2)}) collective-permute-start(f32[128,2048]{1,0:T(8,128)} %get-tuple-element.152), channel_id=1, source_target_pairs={{0,1},{1,0},{2,3},{3,2},{4,5},{5,4},{6,7},{7,6},{8,9},{9,8},{10,11... | collective-permute-start | bytes 3145736 | tf_op jit(solution)/shard_map/ppermute | solution.py:148
  (18 other events, 301.5 us)

commit v6 on v5

--- a/solution.py
+++ b/solution.py
@@ -306,7 +306,7 @@
 
     @pl.when(step == 0)
     def _():
-        for copy in weight_copies + copies[0] + copies[1]:
+        for copy in weight_copies + copies[0] + copies[1] + copies[2] + copies[3]:
             copy.start()
         for copy in weight_copies:
             copy.wait()
@@ -319,9 +319,6 @@
         def _():
             for copy in copies[q]:
                 copy.wait()
-            if 0 < q < 3:
-                for copy in copies[q + 1]:
-                    copy.start()
             total = None
             for s in range(slots):
                 part = lax.dot_general(

time: 152 us -> 150 us (0.987)
  no operation moved by 1% of the time
where the time goes in v6:
time: 150 us
  waiting for transfers between devices  60.9 us (41%)
  Pallas kernels  34.9 us (23%)
  starting transfers between devices  31.2 us (21%)
  blocking collectives  12.1 us (8%)
  local copies, waits for them, and re-layouts  7.42 us (5%)
  other arithmetic  2.7 us (2%)
    ppermute x11, waiting for transfers between devices, move_chips(): lax.ppermute(x, 'chan', [(2 * a + k, 2 * b + k) for a, b in pairs for k i...  37.5 us
    ppermute x12, waiting for transfers between devices, swap(): lax.ppermute(x, axis, [(i, i ^ bit) for i in range(lax.axis_size(axis))])  20.7 us
    pallas_call x2, Pallas kernels, project(): pl.pallas_call(functools.partial(project_kernel, plan, range(len(weights)...  17.7 us
    ppermute x11, starting transfers between devices, move_chips(): lax.ppermute(x, 'chan', [(2 * a + k, 2 * b + k) for a, b in pairs for k i...  15.7 us
    all_to_all x1, blocking collectives, body(): lax.all_to_all(gated, 'ctx', split_axis=0, concat_axis=0, tiled=True)  12.1 us
    ppermute x12, starting transfers between devices, swap(): lax.ppermute(x, axis, [(i, i ^ bit) for i in range(lax.axis_size(axis))])  11.2 us
    pallas_call x1, Pallas kernels, convolve(): pl.pallas_call(conv_kernel, grid=(rows // step,), in_specs=[pl.BlockSpec(...  9.1 us
    pallas_call x1, Pallas kernels, pick_columns(): pl.pallas_call(pick_kernel, grid_spec=pltpu.PrefetchScalarGridSpec(num_sc...  7.25 us
  transfers between devices with their start and end apart: 24, of which 11 were waited for; matrix products, arithmetic and copies ran while one was open for 3% of the time, Pallas kernels for 23%

profile of v6, /device:TPU:0, one launch (start us, length us, event | category | flops | bytes accessed | tf_op | source)
XLA Modules:
  0.0 149.5 jit_solution(8473476555105769234)
XLA Ops:
  0.0 3.0 %collective-permute-start = (bf16[512,512]{1,0:T(8,128)(2,1)}, bf16[512,512]{1,0:T(8,128)(2,1)S(1)}, u32[]{:S(2)}, u32[]{:S(2)}) collective-permute-start(bf16[512,512]{1,0:T(8,128)(2,1)} %refs_4_.1), channel_id=1, source_target_pairs={{0,2},{1,3},{2,0},{3,1},{4,6},{5,7},{6,4},{7,5},{8,10},{9,11},{10,... | collective-permute-start | bytes 1572872 | tf_op jit(solution)/shard_map/ppermute | solution.py:204
  3.7 1.6 %collective-permute-start.2 = (bf16[512,512]{1,0:T(8,128)(2,1)}, bf16[512,512]{1,0:T(8,128)(2,1)S(1)}, u32[]{:S(2)}, u32[]{:S(2)}) collective-permute-start(bf16[512,512]{1,0:T(8,128)(2,1)} %refs_4_.1), channel_id=1, source_target_pairs={{0,8},{8,0},{16,24},{24,16},{1,9},{9,1},{17,25},{25,17},{2,10},{10... | collective-permute-start | bytes 1572872 | tf_op jit(solution)/shard_map/ppermute | solution.py:148
  5.3 1.5 %collective-permute-start.3 = (bf16[512,512]{1,0:T(8,128)(2,1)}, bf16[512,512]{1,0:T(8,128)(2,1)S(1)}, u32[]{:S(2)}, u32[]{:S(2)}) collective-permute-start(bf16[512,512]{1,0:T(8,128)(2,1)} %refs_4_.1), channel_id=1, source_target_pairs={{0,16},{8,24},{16,0},{24,8},{1,17},{9,25},{17,1},{25,9},{2,18},{10... | collective-permute-start | bytes 1572872 | tf_op jit(solution)/shard_map/ppermute | solution.py:148
  7.5 7.2 %pick_columns.1 = (bf16[512,512]{1,0:T(8,128)(2,1)}, bf16[512,512]{1,0:T(8,128)(2,1)}, bf16[512,512]{1,0:T(8,128)(2,1)}, bf16[512,512]{1,0:T(8,128)(2,1)}, bf16[...) custom-call(s32[8]{0:T(128)} %stack.56.at_ref, ...), custom_call_target="tpu_custom_call" | custom-call | tf_op jit(solution)/shard_map/pick_columns/pallas_call | solution.py:182
  15.2 2.2 %collective-permute-done.2.refs_5_ = bf16[512,512]{1,0:T(8,128)(2,1)S(1)} collective-permute-done((bf16[512,512]{1,0:T(8,128)(2,1)}, bf16[512,512]{1,0:T(8,128)(2,1)S(1)}, u32[]{:S(2)}, u32[]{:S(2)}) %collective-permute-start.2) | collective-permute-done | bytes 524320 | tf_op jit(solution)/shard_map/ppermute | solution.py:148
  18.6 1.5 collective-permute-start.4
  22.0 1.5 %collective-permute-start.7 = (bf16[512,512]{1,0:T(8,128)(2,1)S(1)}, bf16[512,512]{1,0:T(8,128)(2,1)S(1)}, u32[]{:S(2)}, u32[]{:S(2)}) collective-permute-start(bf16[512,512]{1,0:T(8,128)(2,1)S(1)} %collective-permute-done.refs_9_), channel_id=1, source_target_pairs={{0,16},{8,24},{16,0},{24,8},{1,17},{9,25},{17,1},{25,9},{2,18},{10... | collective-permute-start | bytes 1572872 | tf_op jit(solution)/shard_map/ppermute | solution.py:148
  23.5 12.9 %collective-permute-done.5 = bf16[512,512]{1,0:T(8,128)(2,1)} collective-permute-done((bf16[512,512]{1,0:T(8,128)(2,1)S(1)}, bf16[512,512]{1,0:T(8,128)(2,1)}, u32[]{:S(2)}, u32[]{:S(2)}) %collective-permute-start.5) | collective-permute-done | bytes 524320 | tf_op jit(solution)/shard_map/ppermute | solution.py:204
  38.8 1.5 %collective-permute-start.10 = (bf16[1024,512]{1,0:T(8,128)(2,1)S(1)}, bf16[1024,512]{1,0:T(8,128)(2,1)S(1)}, u32[]{:S(2)}, u32[]{:S(2)}) collective-permute-start(bf16[1024,512]{1,0:T(8,128)(2,1)S(1)} %get-tuple-element.159), channel_id=1, source_target_pairs={{0,16},{8,24},{16,0},{24,8},{1,17},{9,25},{17,1},{25,9},{2,18},{10... | collective-permute-start | bytes 3145736 | tf_op jit(solution)/shard_map/ppermute | solution.py:148
  40.3 2.3 %collective-permute-start.11 = (bf16[512,512]{1,0:T(8,128)(2,1)S(1)}, bf16[512,512]{1,0:T(8,128)(2,1)S(1)}, u32[]{:S(2)}, u32[]{:S(2)}) collective-permute-start(bf16[512,512]{1,0:T(8,128)(2,1)S(1)} %copy-done.17), channel_id=1, source_target_pairs={{0,6},{1,7},{2,4},{3,5},{4,2},{5,3},{6,0},{7,1},{8,14},{9,15},{10,... | collective-permute-start | bytes 1572872 | tf_op jit(solution)/shard_map/ppermute | solution.py:204
  43.9 9.1 %collective-permute-done.11.refs_3_ = bf16[512,512]{1,0:T(8,128)(2,1)S(1)} collective-permute-done((bf16[512,512]{1,0:T(8,128)(2,1)S(1)}, bf16[512,512]{1,0:T(8,128)(2,1)S(1)}, u32[]{:S(2)}, u32[]{:S(2)}) %collective-permute-start.11) | collective-permute-done | bytes 524320 | tf_op jit(solution)/shard_map/ppermute | solution.py:204
  53.1 11.1 %collective-permute-done.8 = bf16[512,512]{1,0:T(8,128)(2,1)S(1)} collective-permute-done((bf16[512,512]{1,0:T(8,128)(2,1)}, bf16[512,512]{1,0:T(8,128)(2,1)S(1)}, u32[]{:S(2)}, u32[]{:S(2)}) %collective-permute-start.8) | collective-permute-done | bytes 524320 | tf_op jit(solution)/shard_map/ppermute | solution.py:204
  69.9 2.2 %collective-permute-start.14 = (bf16[512,512]{1,0:T(8,128)(2,1)}, bf16[512,512]{1,0:T(8,128)(2,1)S(1)}, u32[]{:S(2)}, u32[]{:S(2)}) collective-permute-start(bf16[512,512]{1,0:T(8,128)(2,1)} %get-tuple-element.124), channel_id=1, source_target_pairs={{0,2},{1,3},{2,0},{3,1},{4,6},{5,7},{6,4},{7,5},{8,10},{9,11},{10,... | collective-permute-start | bytes 1572872 | tf_op jit(solution)/shard_map/ppermute | solution.py:204
  72.1 14.0 %collective-permute-done.12.refs_13_ = bf16[768,512]{1,0:T(8,128)(2,1)S(1)} collective-permute-done((bf16[768,512]{1,0:T(8,128)(2,1)S(1)}, bf16[768,512]{1,0:T(8,128)(2,1)S(1)}, u32[]{:S(2)}, u32[]{:S(2)}) %collective-permute-start.12) | collective-permute-done | bytes 786464 | tf_op jit(solution)/shard_map/ppermute | solution.py:148
  87.5 1.7 %slice.42 = bf16[256,512]{1,0:T(8,128)(2,1)} slice(bf16[768,512]{1,0:T(8,128)(2,1)} %collective-permute-done.13.refs_14_), slice={[256:512], [0:512]} | slice | bytes 524288 | tf_op jit(solution)/shard_map/slice | solution.py:259
  90.6 4.3 %all-to-all-start = ((bf16[4,128,512]{2,1,0:T(8,128)(2,1)}), bf16[4,128,512]{2,1,0:T(8,128)(2,1)}, u32[]{:S(2)}, u32[]{:S(2)}) async-start(bf16[4,128,512]{2,1,0:T(8,128)(2,1)} %bitcast.28), calls=%async_computation | async-start | bytes 1048576 | tf_op jit(solution)/shard_map/all_to_all | solution.py:419
  95.0 2.1 %collective-permute-start.20 = (bf16[512,256]{1,0:T(8,128)(2,1)}, bf16[512,256]{1,0:T(8,128)(2,1)S(1)}, u32[]{:S(2)}, u32[]{:S(2)}) collective-permute-start(bf16[512,256]{1,0:T(8,128)(2,1)} %get-tuple-element.120), channel_id=1, source_target_pairs={{0,6},{1,7},{2,4},{3,5},{4,2},{5,3},{6,0},{7,1},{8,14},{9,15},{10,... | collective-permute-start | bytes 786440 | tf_op jit(solution)/shard_map/ppermute | solution.py:204
  97.2 1.9 %collective-permute-done.17.refs_17_ = bf16[256,512]{1,0:T(8,128)(2,1)S(1)} collective-permute-done((bf16[256,512]{1,0:T(8,128)(2,1)S(1)}, bf16[256,512]{1,0:T(8,128)(2,1)S(1)}, u32[]{:S(2)}, u32[]{:S(2)}) %collective-permute-start.17) | collective-permute-done | bytes 262176 | tf_op jit(solution)/shard_map/ppermute | solution.py:148
  99.7 2.7 %all-to-all-done.filter_ref = bf16[4,128,512]{2,1,0:T(8,128)(2,1)} async-done(((bf16[4,128,512]{2,1,0:T(8,128)(2,1)}), bf16[4,128,512]{2,1,0:T(8,128)(2,1)}, u32[]{:S(2)}, u32[]{:S(2)}) %all-to-all-start) | async-done | bytes 524320 | tf_op jit(solution)/shard_map/all_to_all | solution.py:419
  102.5 11.3 %project.2 = (f32[256,2048]{1,0:T(8,128)}, f32[256,2048]{1,0:T(8,128)}) custom-call(s32[8]{0:T(128)S(1)} %stack.63.at_ref, bf16[512,512]{1,0:T(8,128)(2,1)S(1)} %copy-done.4, bf16[512,512]{1,0:T(8,128)(2,1)S(1)} %collective-permute-done.14.refs_1_, bf16[512,512]{1,0:T(8,128)(2,1)} %collective-permute-done.15.refs_2_, bf16[512,512]{1,0:T(8,128)(2,1)} %copy-done.16, ...), custom_call_target="tpu_custom_call" | custom-call | tf_op jit(solution)/shard_map/project/pallas_call | solution.py:374
  113.9 3.9 %collective-permute-done.19.refs_2_ = bf16[512,256]{1,0:T(8,128)(2,1)S(1)} collective-permute-done((bf16[512,256]{1,0:T(8,128)(2,1)}, bf16[512,256]{1,0:T(8,128)(2,1)S(1)}, u32[]{:S(2)}, u32[]{:S(2)}) %collective-permute-start.19) | collective-permute-done | bytes 262176 | tf_op jit(solution)/shard_map/ppermute | solution.py:204
  117.8 6.4 %project.3 = (f32[128,2048]{1,0:T(8,128)}, f32[128,2048]{1,0:T(8,128)}) custom-call(s32[8]{0:T(128)S(1)} %stack.63.at_ref, bf16[512,256]{1,0:T(8,128)(2,1)S(1)} %copy-done.5, bf16[512,256]{1,0:T(8,128)(2,1)S(1)} %collective-permute-done.18.refs_1_, bf16[512,256]{1,0:T(8,128)(2,1)S(1)} %collective-permute-done.19.refs_2_, ...), custom_call_target="tpu_custom_call" | custom-call | tf_op jit(solution)/shard_map/project/pallas_call | solution.py:374
  125.5 9.1 %convolve.1.answer_ref = f32[128,2048]{1,0:T(8,128)} custom-call(f32[2,128,2048]{2,1,0:T(8,128)} %bitcast.27, f32[2,128,2048]{2,1,0:T(8,128)} %bitcast.20.other_ref, f32[128,10]{1,0:T(8,128)} %copy.11.params_ref, bf16[4,128,512]{2,1,0:T(8,128)(2,1)} %all-to-all-done.filter_ref, bf16[512,1024]{1,0:T(8,128)(2,1)} %constant.52.clone.high_ref, ...), custom_call_target="tpu_custom_call" | custom-call | tf_op jit(solution)/shard_map/convolve/pallas_call | solution.py:103
  136.6 12.1 %all_to_all.10 = bf16[4,128,512]{2,1,0:T(8,128)(2,1)S(1)} all-to-all(bf16[4,128,512]{2,1,0:T(8,128)(2,1)S(1)} %gate.1), channel_id=1, replica_groups=mesh['ctx'=4,'chan'=8] {'ctx'}, dimensions={0} | all-to-all | bytes 1048576 | tf_op jit(solution)/shard_map/all_to_all | solution.py:434
  (85 shorter events, 22.0 us)
Async XLA Ops:
  0.0 15.2 %collective-permute-start = (bf16[512,512]{1,0:T(8,128)(2,1)}, bf16[512,512]{1,0:T(8,128)(2,1)S(1)}, u32[]{:S(2)}, u32[]{:S(2)}) collective-permute-start(bf16[512,512]{1,0:T(8,128)(2,1)} %refs_4_.1), channel_id=1, source_target_pairs={{0,2},{1,3},{2,0},{3,1},{4,6},{5,7},{6,4},{7,5},{8,10},{9,11},{10,... | collective-permute-start | bytes 1572872 | tf_op jit(solution)/shard_map/ppermute | solution.py:204
  3.0 12.1 %collective-permute-start.1 = (bf16[512,512]{1,0:T(8,128)(2,1)}, bf16[512,512]{1,0:T(8,128)(2,1)S(1)}, u32[]{:S(2)}, u32[]{:S(2)}) collective-permute-start(bf16[512,512]{1,0:T(8,128)(2,1)} %refs_4_.1), channel_id=1, source_target_pairs={{2,4},{3,5},{4,2},{5,3},{10,12},{11,13},{12,10},{13,11},{18,20},{1... | collective-permute-start | bytes 1572872 | tf_op jit(solution)/shard_map/ppermute | solution.py:204
  3.7 13.7 %collective-permute-start.2 = (bf16[512,512]{1,0:T(8,128)(2,1)}, bf16[512,512]{1,0:T(8,128)(2,1)S(1)}, u32[]{:S(2)}, u32[]{:S(2)}) collective-permute-start(bf16[512,512]{1,0:T(8,128)(2,1)} %refs_4_.1), channel_id=1, source_target_pairs={{0,8},{8,0},{16,24},{24,16},{1,9},{9,1},{17,25},{25,17},{2,10},{10... | collective-permute-start | bytes 1572872 | tf_op jit(solution)/shard_map/ppermute | solution.py:148
  5.3 13.3 %collective-permute-start.3 = (bf16[512,512]{1,0:T(8,128)(2,1)}, bf16[512,512]{1,0:T(8,128)(2,1)S(1)}, u32[]{:S(2)}, u32[]{:S(2)}) collective-permute-start(bf16[512,512]{1,0:T(8,128)(2,1)} %refs_4_.1), channel_id=1, source_target_pairs={{0,16},{8,24},{16,0},{24,8},{1,17},{9,25},{17,1},{25,9},{2,18},{10... | collective-permute-start | bytes 1572872 | tf_op jit(solution)/shard_map/ppermute | solution.py:148
  18.6 4.9 %collective-permute-start.4 = (bf16[512,512]{1,0:T(8,128)(2,1)S(1)}, bf16[512,512]{1,0:T(8,128)(2,1)}, u32[]{:S(2)}, u32[]{:S(2)}) collective-permute-start(bf16[512,512]{1,0:T(8,128)(2,1)S(1)} %collective-permute-done.refs_9_), channel_id=1, source_target_pairs={{2,4},{3,5},{4,2},{5,3},{10,12},{11,13},{12,10},{13,11},{18,20},{1... | collective-permute-start | bytes 1572872 | tf_op jit(solution)/shard_map/ppermute | solution.py:204
  20.1 16.3 %collective-permute-start.5 = (bf16[512,512]{1,0:T(8,128)(2,1)S(1)}, bf16[512,512]{1,0:T(8,128)(2,1)}, u32[]{:S(2)}, u32[]{:S(2)}) collective-permute-start(bf16[512,512]{1,0:T(8,128)(2,1)S(1)} %collective-permute-done.1), channel_id=1, source_target_pairs={{2,0},{3,1},{4,6},{5,7},{10,8},{11,9},{12,14},{13,15},{18,16},{19,... | collective-permute-start | bytes 1572872 | tf_op jit(solution)/shard_map/ppermute | solution.py:204
  21.4 15.1 %collective-permute-start.6 = (bf16[512,512]{1,0:T(8,128)(2,1)S(1)}, bf16[512,512]{1,0:T(8,128)(2,1)S(1)}, u32[]{:S(2)}, u32[]{:S(2)}) collective-permute-start(bf16[512,512]{1,0:T(8,128)(2,1)S(1)} %collective-permute-done.refs_9_), channel_id=1, source_target_pairs={{0,8},{8,0},{16,24},{24,16},{1,9},{9,1},{17,25},{25,17},{2,10},{10... | collective-permute-start | bytes 1572872 | tf_op jit(solution)/shard_map/ppermute | solution.py:148
  22.0 14.5 %collective-permute-start.7 = (bf16[512,512]{1,0:T(8,128)(2,1)S(1)}, bf16[512,512]{1,0:T(8,128)(2,1)S(1)}, u32[]{:S(2)}, u32[]{:S(2)}) collective-permute-start(bf16[512,512]{1,0:T(8,128)(2,1)S(1)} %collective-permute-done.refs_9_), channel_id=1, source_target_pairs={{0,16},{8,24},{16,0},{24,8},{1,17},{9,25},{17,1},{25,9},{2,18},{10... | collective-permute-start | bytes 1572872 | tf_op jit(solution)/shard_map/ppermute | solution.py:148
  38.1 26.1 %collective-permute-start.9 = (bf16[1024,512]{1,0:T(8,128)(2,1)S(1)}, bf16[1024,512]{1,0:T(8,128)(2,1)S(1)}, u32[]{:S(2)}, u32[]{:S(2)}) collective-permute-start(bf16[1024,512]{1,0:T(8,128)(2,1)S(1)} %get-tuple-element.137.refs_12_), channel_id=1, source_target_pairs={{0,8},{8,0},{16,24},{24,16},{1,9},{9,1},{17,25},{25,17},{2,10},{10... | collective-permute-start | bytes 3145736 | tf_op jit(solution)/shard_map/ppermute | solution.py:148
  38.8 25.4 %collective-permute-start.10 = (bf16[1024,512]{1,0:T(8,128)(2,1)S(1)}, bf16[1024,512]{1,0:T(8,128)(2,1)S(1)}, u32[]{:S(2)}, u32[]{:S(2)}) collective-permute-start(bf16[1024,512]{1,0:T(8,128)(2,1)S(1)} %get-tuple-element.159), channel_id=1, source_target_pairs={{0,16},{8,24},{16,0},{24,8},{1,17},{9,25},{17,1},{25,9},{2,18},{10... | collective-permute-start | bytes 3145736 | tf_op jit(solution)/shard_map/ppermute | solution.py:148
  40.3 12.7 %collective-permute-start.11 = (bf16[512,512]{1,0:T(8,128)(2,1)S(1)}, bf16[512,512]{1,0:T(8,128)(2,1)S(1)}, u32[]{:S(2)}, u32[]{:S(2)}) collective-permute-start(bf16[512,512]{1,0:T(8,128)(2,1)S(1)} %copy-done.17), channel_id=1, source_target_pairs={{0,6},{1,7},{2,4},{3,5},{4,2},{5,3},{6,0},{7,1},{8,14},{9,15},{10,... | collective-permute-start | bytes 1572872 | tf_op jit(solution)/shard_map/ppermute | solution.py:204
  42.7 21.5 %collective-permute-start.8 = (bf16[512,512]{1,0:T(8,128)(2,1)}, bf16[512,512]{1,0:T(8,128)(2,1)S(1)}, u32[]{:S(2)}, u32[]{:S(2)}) collective-permute-start(bf16[512,512]{1,0:T(8,128)(2,1)} %collective-permute-done.4), channel_id=1, source_target_pairs={{2,0},{3,1},{4,6},{5,7},{10,8},{11,9},{12,14},{13,15},{18,16},{19,... | collective-permute-start | bytes 1572872 | tf_op jit(solution)/shard_map/ppermute | solution.py:204
  66.6 19.5 %collective-permute-start.12 = (bf16[768,512]{1,0:T(8,128)(2,1)S(1)}, bf16[768,512]{1,0:T(8,128)(2,1)S(1)}, u32[]{:S(2)}, u32[]{:S(2)}) collective-permute-start(bf16[768,512]{1,0:T(8,128)(2,1)S(1)} %get-tuple-element.140.refs_15_), channel_id=1, source_target_pairs={{0,8},{8,0},{16,24},{24,16},{1,9},{9,1},{17,25},{25,17},{2,10},{10... | collective-permute-start | bytes 2359304 | tf_op jit(solution)/shard_map/ppermute | solution.py:148
  68.0 19.5 %collective-permute-start.13 = (bf16[768,512]{1,0:T(8,128)(2,1)}, bf16[768,512]{1,0:T(8,128)(2,1)}, u32[]{:S(2)}, u32[]{:S(2)}) collective-permute-start(bf16[768,512]{1,0:T(8,128)(2,1)} %get-tuple-element.157), channel_id=1, source_target_pairs={{0,16},{8,24},{16,0},{24,8},{1,17},{9,25},{17,1},{25,9},{2,18},{10... | collective-permute-start | bytes 2359304 | tf_op jit(solution)/shard_map/ppermute | solution.py:148
  69.3 33.2 %collective-permute-start.15 = (bf16[512,512]{1,0:T(8,128)(2,1)}, bf16[512,512]{1,0:T(8,128)(2,1)}, u32[]{:S(2)}, u32[]{:S(2)}) collective-permute-start(bf16[512,512]{1,0:T(8,128)(2,1)} %get-tuple-element.108), channel_id=1, source_target_pairs={{0,4},{1,5},{2,6},{3,7},{4,0},{5,1},{6,2},{7,3},{8,12},{9,13},{10,... | collective-permute-start | bytes 1572872 | tf_op jit(solution)/shard_map/ppermute | solution.py:204
  69.9 32.6 %collective-permute-start.14 = (bf16[512,512]{1,0:T(8,128)(2,1)}, bf16[512,512]{1,0:T(8,128)(2,1)S(1)}, u32[]{:S(2)}, u32[]{:S(2)}) collective-permute-start(bf16[512,512]{1,0:T(8,128)(2,1)} %get-tuple-element.124), channel_id=1, source_target_pairs={{0,2},{1,3},{2,0},{3,1},{4,6},{5,7},{6,4},{7,5},{8,10},{9,11},{10,... | collective-permute-start | bytes 1572872 | tf_op jit(solution)/shard_map/ppermute | solution.py:204
  89.2 7.9 %collective-permute-start.16 = (bf16[256,512]{1,0:T(8,128)(2,1)}, bf16[256,512]{1,0:T(8,128)(2,1)S(1)}, u32[]{:S(2)}, u32[]{:S(2)}) collective-permute-start(bf16[256,512]{1,0:T(8,128)(2,1)} %slice.42), channel_id=1, source_target_pairs={{0,8},{8,0},{16,24},{24,16},{1,9},{9,1},{17,25},{25,17},{2,10},{10... | collective-permute-start | bytes 786440 | tf_op jit(solution)/shard_map/ppermute | solution.py:148
  89.9 9.2 %collective-permute-start.17 = (bf16[256,512]{1,0:T(8,128)(2,1)S(1)}, bf16[256,512]{1,0:T(8,128)(2,1)S(1)}, u32[]{:S(2)}, u32[]{:S(2)}) collective-permute-start(bf16[256,512]{1,0:T(8,128)(2,1)S(1)} %slice.43), channel_id=1, source_target_pairs={{0,16},{8,24},{16,0},{24,8},{1,17},{9,25},{17,1},{25,9},{2,18},{10... | collective-permute-start | bytes 786440 | tf_op jit(solution)/shard_map/ppermute | solution.py:148
  90.6 11.9 %all-to-all-start = ((bf16[4,128,512]{2,1,0:T(8,128)(2,1)}), bf16[4,128,512]{2,1,0:T(8,128)(2,1)}, u32[]{:S(2)}, u32[]{:S(2)}) async-start(bf16[4,128,512]{2,1,0:T(8,128)(2,1)} %bitcast.28), calls=%async_computation | async-start | bytes 1048576 | tf_op jit(solution)/shard_map/all_to_all | solution.py:419
  95.0 18.9 %collective-permute-start.20 = (bf16[512,256]{1,0:T(8,128)(2,1)}, bf16[512,256]{1,0:T(8,128)(2,1)S(1)}, u32[]{:S(2)}, u32[]{:S(2)}) collective-permute-start(bf16[512,256]{1,0:T(8,128)(2,1)} %get-tuple-element.120), channel_id=1, source_target_pairs={{0,6},{1,7},{2,4},{3,5},{4,2},{5,3},{6,0},{7,1},{8,14},{9,15},{10,... | collective-permute-start | bytes 786440 | tf_op jit(solution)/shard_map/ppermute | solution.py:204
  97.1 16.7 %collective-permute-start.18 = (bf16[512,256]{1,0:T(8,128)(2,1)}, bf16[512,256]{1,0:T(8,128)(2,1)S(1)}, u32[]{:S(2)}, u32[]{:S(2)}) collective-permute-start(bf16[512,256]{1,0:T(8,128)(2,1)} %get-tuple-element.145), channel_id=1, source_target_pairs={{0,2},{1,3},{2,0},{3,1},{4,6},{5,7},{6,4},{7,5},{8,10},{9,11},{10,... | collective-permute-start | bytes 786440 | tf_op jit(solution)/shard_map/ppermute | solution.py:204
  99.0 18.7 %collective-permute-start.19 = (bf16[512,256]{1,0:T(8,128)(2,1)}, bf16[512,256]{1,0:T(8,128)(2,1)S(1)}, u32[]{:S(2)}, u32[]{:S(2)}) collective-permute-start(bf16[512,256]{1,0:T(8,128)(2,1)} %get-tuple-element.146), channel_id=1, source_target_pairs={{0,4},{1,5},{2,6},{3,7},{4,0},{5,1},{6,2},{7,3},{8,12},{9,13},{10,... | collective-permute-start | bytes 786440 | tf_op jit(solution)/shard_map/ppermute | solution.py:204
  117.8 7.7 %collective-permute-start.22 = (f32[256,2048]{1,0:T(8,128)}, f32[256,2048]{1,0:T(8,128)}, u32[]{:S(2)}, u32[]{:S(2)}) collective-permute-start(f32[256,2048]{1,0:T(8,128)} %get-tuple-element.155), channel_id=1, source_target_pairs={{0,1},{1,0},{2,3},{3,2},{4,5},{5,4},{6,7},{7,6},{8,9},{9,8},{10,11... | collective-permute-start | bytes 6291464 | tf_op jit(solution)/shard_map/ppermute | solution.py:148
  124.2 10.4 %collective-permute-start.21 = (f32[128,2048]{1,0:T(8,128)}, f32[128,2048]{1,0:T(8,128)S(1)}, u32[]{:S(2)}, u32[]{:S(2)}) collective-permute-start(f32[128,2048]{1,0:T(8,128)} %get-tuple-element.152), channel_id=1, source_target_pairs={{0,1},{1,0},{2,3},{3,2},{4,5},{5,4},{6,7},{7,6},{8,9},{9,8},{10,11... | collective-permute-start | bytes 3145736 | tf_op jit(solution)/shard_map/ppermute | solution.py:148
  (18 other events, 301.5 us)
